TPU v7x, 1024 devices: a whole 8x8x8 slice. The times are simulated.
1024 devices in a mesh: mem: 64 (over y, x_hi, core), dom: 16 (over z, x_lo).
Axes of the slice: x: 8 (x_hi: 4, x_lo: 2; x = x_hi * 2 + x_lo), y: 8, z: 8, core: 2. Of those that a mesh axis runs over, the one named last changes fastest.
Arguments:
- prior_sample: bfloat16 [512, 8, 256, 256], P('mem', None, 'dom'), may hold values from -4 to 4
- prior_velocity: float32 [2, 8, 256], replicated, may hold values from -0.8 to 0.8
- obs_cells: int32 [16, 64, 128], P('dom', 'mem'), may hold values from 0 to 511
- obs_bins: int32 [16, 64, 128], P('dom', 'mem'), may hold values from 0 to 7
- obs_values: float32 [16, 64, 128], P('dom', 'mem'), may hold values from -6 to 6
- tile_owner: int32 [16, 64], P('dom'), may hold values from 0 to 63, each once within a row
Outputs:
- analysis: bfloat16 [512, 8, 256, 256], P('mem', None, 'dom')
Inputs may be any that keep to these rules, and one draw needn't show every extreme that they name: `obs_cells`: index 256 * (row within the tile) + column. `tile_owner`: each row names every slot once.
All inputs are finite; a program needn't handle non-finite values. Where the computation divides by a largest or mean magnitude, that divisor is 1e-20 or more.
Results may differ from a plain program's by a relative error of at most 0.0082.
Values may be sent and summed in bfloat16 or wider, within the bound.
No kernel may reach another device: no remote copies, remote signals or barrier semaphores. Data moves between devices by JAX's collectives and lax.ppermute only.
A program may use at most 32 MiB of HBM per device.

v0:
```python
import jax
import jax.numpy as jnp
from jax import lax
from jax.sharding import Mesh
from jax.sharding import PartitionSpec as P

WINDOW_HEIGHT = 2
STEPS = 5
MEM = ("mem_0", "mem_1", "mem_2")


advect_coef = 0.15
diffuse_coef = 0.15
loc_step = 0.35
inflation = 1.1


def with_halo(block, sides, width):
    for axis, dim in sides:
        count = lax.axis_size(axis)
        forward = [(i, i + 1) for i in range(count - 1)]
        forward.append((count - 1, 0))
        backward = [(target, source) for source, target in forward]
        low = lax.ppermute(
            lax.slice_in_dim(block, block.shape[dim] - width, None, axis=dim), axis, forward
        )
        high = lax.ppermute(lax.slice_in_dim(block, 0, width, axis=dim), axis, backward)
        block = jnp.concatenate([low, block, high], axis=dim)
    return block


def cut_along(x, dim, devices):
    shape = x.shape
    blocks = x.reshape(*shape[:dim], devices, shape[dim] // devices, *shape[dim + 1 :])
    return jnp.moveaxis(blocks, dim, 0)


def in_order(blocks, dim):
    blocks = jnp.moveaxis(blocks, 0, dim)
    shape = blocks.shape
    return blocks.reshape(*shape[:dim], shape[dim] * shape[dim + 1], *shape[dim + 2 :])


def moved_by_axis(blocks, axes, order):
    shape = [lax.axis_size(a) for a in axes]
    blocks = blocks.reshape(*shape, *blocks.shape[1:])
    for k in order:
        blocks = lax.all_to_all(blocks, axes[k], split_axis=k, concat_axis=k, tiled=True)
    return blocks.reshape(-1, *blocks.shape[len(axes) :])


def exchange_by_chip(x, groups, order, split_dim, concat_dim):
    devices = lax.axis_size(groups[0]) * lax.axis_size(groups[1])
    blocks = cut_along(x, split_dim, devices)
    return in_order(moved_by_axis(blocks, groups, order), concat_dim)


def propagate_prior(haloed_field, prior_velocity):
    centre = haloed_field[..., 1:-1, :]
    along_x = prior_velocity[0][:, None, :]
    along_y = prior_velocity[1][:, None, :]
    flux_x = (along_x + 0.5 * centre) * centre
    flux_y = (along_y + 0.5 * haloed_field) * haloed_field
    east = jnp.roll(flux_x, -1, axis=-1)
    west = jnp.roll(flux_x, 1, axis=-1)
    neighbours = (
        jnp.roll(centre, -1, axis=-1)
        + jnp.roll(centre, 1, axis=-1)
        + haloed_field[..., 2:, :]
        + haloed_field[..., :-2, :]
    )
    return (
        centre
        - advect_coef * (east - west + flux_y[..., 2:, :] - flux_y[..., :-2, :])
        + diffuse_coef * (neighbours - 4.0 * centre)
    )


def analyse(ensemble, obs_at, radius_bins, observed):
    members = ensemble.shape[0]
    values_wide = ensemble.astype(jnp.float32)
    average = jnp.mean(values_wide, axis=0)
    spread = (values_wide - average).astype(jnp.bfloat16)
    picked = jnp.take(spread, obs_at, axis=1)
    innovation = observed - jnp.take(average, obs_at)
    weights = jnp.exp(-0.5 * (loc_step * radius_bins.astype(jnp.float32)) ** 2)
    scaled = (picked.astype(jnp.float32) * weights).astype(jnp.bfloat16)
    eye_wide = jnp.eye(members, dtype=jnp.float32)
    matrix = lax.dot_general(
        picked, scaled, (((1,), (1,)), ((), ())), preferred_element_type=jnp.float32
    )
    matrix = matrix + (members - 1) / inflation * eye_wide
    norm_total = jnp.max(jnp.sum(jnp.abs(matrix), axis=1))
    current_y = (matrix / norm_total).astype(jnp.bfloat16)
    factor = (1.5 * eye_wide - 0.5 * current_y.astype(jnp.float32)).astype(jnp.bfloat16)
    current_y = jnp.dot(current_y, factor, preferred_element_type=jnp.float32).astype(jnp.bfloat16)
    current_z = factor
    for sweep_number in range(1, STEPS):
        product = jnp.dot(current_z, current_y, preferred_element_type=jnp.float32)
        factor = (1.5 * eye_wide - 0.5 * product).astype(jnp.bfloat16)
        if sweep_number + 1 < STEPS:
            current_y = jnp.dot(current_y, factor, preferred_element_type=jnp.float32).astype(
                jnp.bfloat16
            )
        current_z = jnp.dot(factor, current_z, preferred_element_type=jnp.float32).astype(
            jnp.bfloat16
        )
    inverse_root = current_z.astype(jnp.float32)
    forcing = jnp.dot(
        picked.astype(jnp.float32), weights * innovation, precision=lax.Precision.HIGHEST
    )
    inner = jnp.dot(inverse_root, forcing, precision=lax.Precision.HIGHEST)
    shift = jnp.dot(inverse_root, inner, precision=lax.Precision.HIGHEST) / norm_total
    transform = (jnp.sqrt((members - 1) / norm_total) * inverse_root + shift[:, None]).astype(
        jnp.bfloat16
    )
    update = lax.dot_general(
        transform, spread, (((0,), (0,)), ((), ())), preferred_element_type=jnp.float32
    )
    return (average + update).astype(jnp.bfloat16)


def body(prior_sample, prior_velocity, obs_cells, obs_bins, obs_values, tile_owner):
    realisations_on_chip, levels, row_count, lattice_width = prior_sample.shape
    haloed_field = with_halo(prior_sample, (("dom", 2),), 2)
    leading = propagate_prior(haloed_field.astype(jnp.float32), prior_velocity)
    prior_field = propagate_prior(leading, prior_velocity)
    prior_field = prior_field.astype(jnp.bfloat16)
    window_pieces = prior_field.reshape(realisations_on_chip, -1, WINDOW_HEIGHT * lattice_width)
    slot_count = window_pieces.shape[1]
    owners = tile_owner[0]
    positions = jnp.arange(slot_count, dtype=jnp.int32)
    matches = owners[None, :] == positions[:, None]
    inverse = jnp.sum(jnp.where(matches, positions[None, :], 0), axis=1)
    outgoing = jnp.take(window_pieces, inverse, axis=1)
    received = lax.all_to_all(outgoing, MEM, split_axis=1, concat_axis=0, tiled=True)
    obs_at = obs_cells[0]
    radius_bins = obs_bins[0]
    observed = obs_values[0]
    results = jnp.stack([analyse(received[:, 0], obs_at[0], radius_bins[0], observed[0])], axis=1)
    returned = exchange_by_chip(results, (("mem_0", "mem_1"), "mem_2"), (1, 0), 0, 1)
    restored = jnp.take(returned, owners, axis=1)
    return restored.reshape(realisations_on_chip, levels, row_count, lattice_width)


def solution(mesh):
    split = Mesh(
        mesh.devices.reshape(8, 4, 2, mesh.shape["dom"]), ("mem_0", "mem_1", "mem_2", "dom")
    )
    in_specs = (
        P(MEM, None, "dom", None),
        P(),
        P("dom", MEM, None),
        P("dom", MEM, None),
        P("dom", MEM, None),
        P("dom", None),
    )
    out_specs = P(MEM, None, "dom", None)
    return jax.shard_map(body, mesh=split, in_specs=in_specs, out_specs=out_specs, check_vma=False)
```

profile of v0, /device:TPU:8, one launch (start us, length us, event | category | flops | bytes accessed | tf_op | source)
XLA Modules:
  0.0 110.4 jit_solution(11380606068187853573)
XLA Ops:
  0.0 1.1 %fusion.61 = (bf16[8,8,2,256]{3,2,1,0:T(2,128)(2,1)S(1)}, bf16[8,8,2,256]{3,2,1,0:T(2,128)(2,1)S(1)}) fusion(bf16[8,8,16,256]{3,2,1,0:T(8,128)(2,1)} %param.8), kind=kLoop, calls=%fused_computation.125 | loop fusion | bytes 262144 | tf_op jit(solution)/shard_map/slice | solution.py:25
  1.1 2.5 %collective-permute-start = (bf16[8,8,2,256]{3,2,1,0:T(2,128)(2,1)S(1)}, bf16[8,8,2,256]{3,2,1,0:T(2,128)(2,1)S(1)}, u32[]{:S(2)}, u32[]{:S(2)}) collective-permute-start(bf16[8,8,2,256]{3,2,1,0:T(2,128)(2,1)S(1)} %get-tuple-element.24), channel_id=1, source_target_pairs={{0,1},{1,2},{2,3},{3,4},{4,5},{5,6},{6,7},{7,8},{8,9},{9,10},{10,1... | collective-permute-start | bytes 196616 | tf_op jit(solution)/shard_map/ppermute | solution.py:24
  3.6 16.8 %collective-permute-start.1 = (bf16[8,8,2,256]{3,2,1,0:T(2,128)(2,1)S(1)}, bf16[8,8,2,256]{3,2,1,0:T(2,128)(2,1)S(1)}, u32[]{:S(2)}, u32[]{:S(2)}) collective-permute-start(bf16[8,8,2,256]{3,2,1,0:T(2,128)(2,1)S(1)} %get-tuple-element.25), channel_id=1, source_target_pairs={{1,0},{2,1},{3,2},{4,3},{5,4},{6,5},{7,6},{8,7},{9,8},{10,9},{11,1... | collective-permute-start | bytes 196616 | tf_op jit(solution)/shard_map/ppermute | solution.py:27
  20.4 0.8 select_reduce_fusion
  21.2 0.7 slice_bitcast_fusion.1
  22.3 1.4 %maximum_convert_fusion = f32[8,8,20,256]{3,2,1,0:T(8,128)S(1)} fusion(bf16[8,8,2,256]{3,2,1,0:T(2,128)(2,1)S(1)} %collective-permute-done.1, bf16[8,8,16,256]{3,2,1,0:T(8,128)(2,1)} %param.8, bf16[8,8,2,256]{3,2,1,0:T(2,128)(2,1)S(1)} %collective-permute-done), kind=kLoop, calls=%fused_computation.66 | loop fusion | flops 1966080 | bytes 1966080 | tf_op jit(solution)/shard_map/convert_element_type | solution.py:126
  24.0 1.1 %fusion.55 = (f32[8,8,18,255]{3,2,1,0:T(8,128)S(1)}, f32[8,8,18,255]{3,2,1,0:T(8,128)S(1)}, f32[8,8,18,255]{3,2,1,0:T(8,128)S(1)}, f32[8,8,18,255]{3,2,1,0:T(8,128)S(1)}) fusion(f32[8,8,18,256]{3,2,1,0:T(8,128)S(1)} %add_multiply_fusion.2, f32[8,8,20,256]{3,2,1,0:T(8,128)S(1)} %maximum_convert_fusion), kind=kLoop, calls=%fused_computation.119 | loop fusion | bytes 9400320 | tf_op jit(solution)/shard_map/jit(_roll_static)/slice | solution.py:64
  25.2 0.5 fusion.56
  25.7 0.5 copy-done
  26.2 0.5 add_multiply_fusion.1
  26.7 2.2 %add_multiply_fusion = (f32[8,8,18,256]{3,2,1,0:T(8,128)S(1)}, f32[8,8,18,256]{3,2,1,0:T(8,128)S(1)}) fusion(f32[8,256]{1,0:T(8,128)S(1)} %get-tuple-element.27, f32[8,8,20,256]{3,2,1,0:T(8,128)S(1)} %maximum_convert_fusion, f32[8,8,18,255]{3,2,1,0:T(8,128)S(1)} %get-tuple-element.30, f32[8,8,18,1]{3,2,1,0:T(8,128)S(1)} %get-tuple-element.32, ...), kind=kLoop, calls=%fused_computation.20 | loop fusion | flops 5603328 | bytes 12984320 | tf_op jit(solution)/shard_map/mul | solution.py:63
  30.4 1.2 %fusion.16 = bf16[8,8,16,256]{3,2,1,0:T(8,128)(2,1)S(1)} fusion(f32[8,8,18,256]{3,2,1,0:T(8,128)S(1)} %get-tuple-element.7, f32[8,8,18,256]{3,2,1,0:T(8,128)S(1)} %get-tuple-element.6, f32[8,8,16,1]{3,2,1,0:T(8,128)S(1)} %get-tuple-element.21, f32[8,8,16,255]{3,2,1,0:T(8,128)S(1)} %get-tuple-element.23, f32[8,8,16,255]{3,2,1,0:T(8,128)S(1)} %get-tuple-element.22, ...), kind=kLoop, calls=%fused_computation.53 | loop fusion | flops 4456448 | bytes 9961472 | tf_op jit(solution)/shard_map/convert_element_type | solution.py:128
  32.1 0.6 gather_fusion.2
  32.7 0.9 select_bitcast_fusion.1
  33.6 13.5 %all-to-all-start = ((bf16[8,64,512]{2,0,1:T(8,128)(2,1)}), bf16[8,64,512]{2,0,1:T(8,128)(2,1)S(1)}, u32[]{:S(2)}, u32[]{:S(2)}) async-start(bf16[8,64,512]{2,0,1:T(8,128)(2,1)} %select_bitcast_fusion.1), calls=%async_computation | async-start | bytes 1048576 | tf_op jit(solution)/shard_map/all_to_all | solution.py:136
  47.2 17.4 %all-to-all-done = bf16[8,64,512]{2,0,1:T(8,128)(2,1)S(1)} async-done(((bf16[8,64,512]{2,0,1:T(8,128)(2,1)}), bf16[8,64,512]{2,0,1:T(8,128)(2,1)S(1)}, u32[]{:S(2)}, u32[]{:S(2)}) %all-to-all-start) | async-done | bytes 524320 | tf_op jit(solution)/shard_map/all_to_all | solution.py:136
  65.0 1.3 %gather_fusion.1 = f32[128]{0:T(128)S(1)} fusion(f32[512]{0:T(512)S(1)} %broadcast_multiply_fusion, s32[1024]{0:T(1024)S(1)} %pad_clamp_fusion.1), kind=kCustom, calls=%fused_computation.3 | custom fusion | bytes 1536 | tf_op jit(solution)/shard_map/jit(_take)/gather | solution.py:85
  66.3 0.8 gather_fusion
  67.6 0.6 reduce_max.9
  68.2 0.8 divide_convert_fusion
  69.5 0.5 fusion.5
  74.1 0.9 convolution_convert_fusion
  75.0 0.5 convolution_bitcast_fusion.1
  75.5 0.5 fusion.62
  76.0 0.7 broadcast_divide_fusion
  77.4 0.6 fusion.9
  78.1 4.2 %all_to_all.19 = bf16[32,2,8,1,512]{4,2,0,3,1:T(8,128)(2,1)S(1)} all-to-all(bf16[32,2,8,1,512]{4,2,0,3,1:T(8,128)(2,1)S(1)} %copy.37), channel_id=1, replica_groups=mesh['mem_0'=8,'mem_1'=4,'mem_2'=2,'dom'=16] {'mem_2'}, dimensions={1} | all-to-all | bytes 1048576 | tf_op jit(solution)/shard_map/all_to_all | solution.py:48
  82.2 0.9 copy.38
  83.1 7.9 %all-to-all-start.2 = ((bf16[32,2,8,1,512]{4,2,1,3,0:T(8,128)(2,1)}), bf16[32,2,8,1,512]{4,2,1,3,0:T(8,128)(2,1)S(1)}, u32[]{:S(2)}, u32[]{:S(2)}) async-start(bf16[32,2,8,1,512]{4,2,1,3,0:T(8,128)(2,1)} %copy.38), calls=%async_computation.2 | async-start | bytes 1048576 | tf_op jit(solution)/shard_map/all_to_all | solution.py:48
  91.0 17.5 %all-to-all-done.2 = bf16[32,2,8,1,512]{4,2,1,3,0:T(8,128)(2,1)S(1)} async-done(((bf16[32,2,8,1,512]{4,2,1,3,0:T(8,128)(2,1)}), bf16[32,2,8,1,512]{4,2,1,3,0:T(8,128)(2,1)S(1)}, u32[]{:S(2)}, u32[]{:S(2)}) %all-to-all-start.2) | async-done | bytes 524320 | tf_op jit(solution)/shard_map/all_to_all | solution.py:48
  108.5 0.6 gather_fusion.3
  109.5 1.0 reshape.81
  (47 shorter events, 8.4 us)
Async XLA Ops:
  1.1 20.8 %collective-permute-start = (bf16[8,8,2,256]{3,2,1,0:T(2,128)(2,1)S(1)}, bf16[8,8,2,256]{3,2,1,0:T(2,128)(2,1)S(1)}, u32[]{:S(2)}, u32[]{:S(2)}) collective-permute-start(bf16[8,8,2,256]{3,2,1,0:T(2,128)(2,1)S(1)} %get-tuple-element.24), channel_id=1, source_target_pairs={{0,1},{1,2},{2,3},{3,4},{4,5},{5,6},{6,7},{7,8},{8,9},{9,10},{10,1... | collective-permute-start | bytes 196616 | tf_op jit(solution)/shard_map/ppermute | solution.py:24
  3.6 18.7 %collective-permute-start.1 = (bf16[8,8,2,256]{3,2,1,0:T(2,128)(2,1)S(1)}, bf16[8,8,2,256]{3,2,1,0:T(2,128)(2,1)S(1)}, u32[]{:S(2)}, u32[]{:S(2)}) collective-permute-start(bf16[8,8,2,256]{3,2,1,0:T(2,128)(2,1)S(1)} %get-tuple-element.25), channel_id=1, source_target_pairs={{1,0},{2,1},{3,2},{4,3},{5,4},{6,5},{7,6},{8,7},{9,8},{10,9},{11,1... | collective-permute-start | bytes 196616 | tf_op jit(solution)/shard_map/ppermute | solution.py:27
  25.2 1.0 copy-start
  32.0 15.1 %copy-start.1 = (s32[1,1,128]{2,1,0:T(1,128)S(1)}, s32[1,1,128]{2,1,0:T(1,128)}, u32[]{:S(2)}) copy-start(s32[1,1,128]{2,1,0:T(1,128)} %param.10) | copy-start | bytes 1540
  32.1 15.1 %copy-start.2 = (s32[1,1,128]{2,1,0:T(1,128)S(1)}, s32[1,1,128]{2,1,0:T(1,128)}, u32[]{:S(2)}) copy-start(s32[1,1,128]{2,1,0:T(1,128)} %param.11) | copy-start | bytes 1540
  33.6 31.0 %all-to-all-start = ((bf16[8,64,512]{2,0,1:T(8,128)(2,1)}), bf16[8,64,512]{2,0,1:T(8,128)(2,1)S(1)}, u32[]{:S(2)}, u32[]{:S(2)}) async-start(bf16[8,64,512]{2,0,1:T(8,128)(2,1)} %select_bitcast_fusion.1), calls=%async_computation | async-start | bytes 1048576 | tf_op jit(solution)/shard_map/all_to_all | solution.py:136
  72.9 1.0 copy-start.3
  78.0 12.9 %copy-start.4 = (s32[1,64]{1,0:T(1,128)S(1)}, s32[1,64]{1,0:T(1,128)}, u32[]{:S(2)}) copy-start(s32[1,64]{1,0:T(1,128)} %param.13) | copy-start | bytes 772
  83.1 25.5 %all-to-all-start.2 = ((bf16[32,2,8,1,512]{4,2,1,3,0:T(8,128)(2,1)}), bf16[32,2,8,1,512]{4,2,1,3,0:T(8,128)(2,1)S(1)}, u32[]{:S(2)}, u32[]{:S(2)}) async-start(bf16[32,2,8,1,512]{4,2,1,3,0:T(8,128)(2,1)} %copy.38), calls=%async_computation.2 | async-start | bytes 1048576 | tf_op jit(solution)/shard_map/all_to_all | solution.py:48
where the time goes:
time: 111 us; the launch traced here: 110 us
  starting transfers between devices  40.6 us (37%)
  waiting for transfers between devices  35.3 us (32%)
  local copies, waits for them, and re-layouts  11.3 us (10%)
  other arithmetic  9.91 us (9%)
  matrix products  7.94 us (7%)
  blocking collectives  4.15 us (4%)
  between operations  1.16 us (1%)
    all_to_all x1, waiting for transfers between devices, moved_by_axis(): lax.all_to_all(blocks, axes[k], split_axis=k, concat_axis=k, tiled=True)  17.5 us
    all_to_all x1, waiting for transfers between devices, body(): lax.all_to_all(outgoing, MEM, split_axis=1, concat_axis=0, tiled=True)  17.4 us
    ppermute x1, starting transfers between devices, with_halo(): lax.ppermute(lax.slice_in_dim(block, 0, width, axis=dim), axis, backward)  16.8 us
    all_to_all x1, starting transfers between devices, body(): lax.all_to_all(outgoing, MEM, split_axis=1, concat_axis=0, tiled=True)  13.5 us
    all_to_all x1, starting transfers between devices, moved_by_axis(): lax.all_to_all(blocks, axes[k], split_axis=k, concat_axis=k, tiled=True)  7.89 us
    all_to_all x1, blocking collectives, moved_by_axis(): lax.all_to_all(blocks, axes[k], split_axis=k, concat_axis=k, tiled=True)  4.15 us
    mul x2, other arithmetic, propagate_prior(): flux_y = (along_y + 0.5 * haloed_field) * haloed_field  2.71 us
    ppermute x1, starting transfers between devices, with_halo(): lax.ppermute(lax.slice_in_dim(block, block.shape[dim] - width, None, axis...  2.5 us
  transfers between devices with their start and end apart: 4, of which 3 were waited for; matrix products, arithmetic and copies ran while one was open for 1% of the time, Pallas kernels for 0%

commit v1 on v0

v1 whole, which is shorter than its diff:
```python
import functools

import jax
import jax.numpy as jnp
from jax import lax
from jax.experimental import pallas as pl
from jax.experimental.pallas import tpu as pltpu
from jax.sharding import Mesh
from jax.sharding import PartitionSpec as P

STEPS = 5
MEM = ("mem_0", "mem_1", "mem_2")

advect_coef = 0.15
diffuse_coef = 0.15
loc_step = 0.35
inflation = 1.1

F32 = jnp.float32
BF16 = jnp.bfloat16
VMEM = pl.BlockSpec(memory_space=pltpu.VMEM)
SMEM = pl.BlockSpec(memory_space=pltpu.SMEM)
PARAMS = pltpu.CompilerParams(vmem_limit_bytes=48 * 1024 * 1024)


def rows_first(block):
    return jnp.swapaxes(block.astype(F32), 0, 1)


def step(rows, along_x, along_y):
    width = rows[0].shape[-1]
    below, above, inner = [], [], []
    last = len(rows) - 1
    for r, v in enumerate(rows):
        half = 0.5 * v
        flux_y = (along_y + half) * v
        below.append(v - flux_y if r >= 2 else None)
        above.append(v + flux_y if r <= last - 2 else None)
        if 1 <= r <= last - 1:
            flux_x = (along_x + half) * v
            east = pltpu.roll(v - flux_x, width - 1, axis=1)
            west = pltpu.roll(v + flux_x, 1, axis=1)
            inner.append((east + west) - 4.0 * v)
        else:
            inner.append(None)
    return [
        rows[r] + advect_coef * (inner[r] + (below[r + 1] + above[r - 1]))
        for r in range(1, last)
    ]


def edges_kernel(x_ref, low_ref, high_ref):
    levels, rows = x_ref.shape[1], x_ref.shape[2]
    for level in range(levels):
        block = x_ref[:, level]
        low_ref[level] = rows_first(block[:, 0:2]).astype(BF16)
        high_ref[level] = rows_first(block[:, rows - 2 : rows]).astype(BF16)


def put(out_ref, slot, rows, width):
    out_ref[slot, :, 0:width] = rows[0].astype(BF16)
    out_ref[slot, :, width : 2 * width] = rows[1].astype(BF16)


def interior_kernel(owner_ref, velocity_ref, x_ref, out_ref):
    members, levels, rows, width = x_ref.shape
    pairs = rows // 2

    def one(level, carry):
        along_x = velocity_ref[0, pl.ds(level, 1), :]
        along_y = velocity_ref[1, pl.ds(level, 1), :]
        field = rows_first(x_ref[:, level])
        done = [field[r] for r in range(rows)]
        for _ in range(2):
            done = step(done, along_x, along_y)
        for p in range(1, pairs - 1):
            put(out_ref, owner_ref[0, level * pairs + p], done[2 * p - 2 : 2 * p], width)
        return carry

    lax.fori_loop(0, levels, one, 0)


def outer_kernel(owner_ref, velocity_ref, x_ref, before_ref, after_ref, partial_ref, out_ref):
    members, levels, rows, width = x_ref.shape
    pairs = rows // 2
    out_ref[...] = partial_ref[...]

    def one(level, carry):
        along_x = velocity_ref[0, pl.ds(level, 1), :]
        along_y = velocity_ref[1, pl.ds(level, 1), :]
        field = rows_first(x_ref[:, level])
        before = before_ref[level].astype(F32)
        after = after_ref[level].astype(F32)
        top = [before[0], before[1]] + [field[r] for r in range(4)]
        bottom = [field[r] for r in range(rows - 4, rows)] + [after[0], after[1]]
        for p, done in ((0, top), (pairs - 1, bottom)):
            for _ in range(2):
                done = step(done, along_x, along_y)
            put(out_ref, owner_ref[0, level * pairs + p], done, width)
        return carry

    lax.fori_loop(0, levels, one, 0)


def dot(a, b):
    return jnp.dot(a, b, preferred_element_type=F32)


def dot_t(a, b):
    return lax.dot_general(a, b, (((1,), (1,)), ((), ())), preferred_element_type=F32)


def thirds(row):
    first = row.astype(BF16)
    rest = row - first.astype(F32)
    second = rest.astype(BF16)
    third = (rest - second.astype(F32)).astype(BF16)
    which = lax.broadcasted_iota(jnp.int32, (16, row.shape[1]), 0)
    parts = jnp.where(
        which == 0,
        first.astype(F32),
        jnp.where(which == 1, second.astype(F32), jnp.where(which == 2, third.astype(F32), 0.0)),
    )
    return parts.astype(BF16)


def whole(parts):
    return (parts[2:3] + parts[1:2]) + parts[0:1]


def analysis_kernel(cells_ref, bins_ref, values_ref, x_ref, out_ref, y_ref, z_ref, f_ref):
    members, tile = x_ref.shape
    obs = cells_ref.shape[1]
    ensemble = x_ref[...].astype(F32)
    average = jnp.sum(ensemble, axis=0, keepdims=True) * (1.0 / members)
    spread = (ensemble - average).astype(BF16)
    cells = cells_ref[...]
    chosen = lax.broadcasted_iota(jnp.int32, (tile, obs), 0) == cells
    chosen = jnp.where(chosen, 1.0, 0.0).astype(BF16)
    picked = dot(spread, chosen).astype(BF16)
    innovation = values_ref[...] - whole(dot(thirds(average), chosen))
    weights = jnp.exp(-0.5 * (loc_step * bins_ref[...].astype(F32)) ** 2)
    scaled = (picked.astype(F32) * weights).astype(BF16)
    diagonal = lax.broadcasted_iota(jnp.int32, (members, members), 0) == lax.broadcasted_iota(
        jnp.int32, (members, members), 1
    )
    matrix = dot_t(scaled, picked) + jnp.where(diagonal, (members - 1) / inflation, 0.0)
    sums = jnp.sum(jnp.abs(matrix), axis=0, keepdims=True)
    norm_total = jnp.max(sums, axis=1, keepdims=True)
    current = (matrix / norm_total).astype(BF16)
    eye = jnp.where(diagonal, 1.5, 0.0)
    y_ref[...] = current
    first = (eye - 0.5 * current.astype(F32)).astype(BF16)
    z_ref[...] = first
    y_ref[...] = dot(first, current).astype(BF16)

    def factor():
        product = dot(y_ref[...], z_ref[...])
        on = lax.broadcasted_iota(jnp.int32, (members, members), 0) == lax.broadcasted_iota(
            jnp.int32, (members, members), 1
        )
        f_ref[...] = (jnp.where(on, 1.5, 0.0) - 0.5 * product).astype(BF16)

    def sweep(_, carry):
        factor()
        y_ref[...] = dot(f_ref[...], y_ref[...]).astype(BF16)
        z_ref[...] = dot(z_ref[...], f_ref[...]).astype(BF16)
        return carry

    lax.fori_loop(0, STEPS - 2, sweep, 0)
    factor()
    root = dot(z_ref[...], f_ref[...]).astype(BF16)
    forcing = whole(dot_t(thirds(weights * innovation), picked))
    inner = whole(dot(thirds(forcing), root))
    shift = whole(dot(thirds(inner), root)) / norm_total
    transform = (jnp.sqrt((members - 1) / norm_total) * root.astype(F32) + shift).astype(BF16)
    out_ref[...] = (average + dot(transform, spread)).astype(BF16)


def restore_kernel(owner_ref, x_ref, out_ref):
    members, levels, rows, width = out_ref.shape
    pairs = rows // 2

    def one(level, carry):
        tiles = [x_ref[owner_ref[0, level * pairs + p]].astype(F32) for p in range(pairs)]
        field = jnp.stack([t[:, k * width : (k + 1) * width] for t in tiles for k in range(2)])
        out_ref[:, level] = jnp.swapaxes(field, 0, 1).astype(BF16)
        return carry

    lax.fori_loop(0, levels, one, 0)


def call(kernel, out, in_specs, flops, moved, **more):
    return pl.pallas_call(
        kernel,
        out_shape=out,
        in_specs=in_specs,
        out_specs=jax.tree.map(lambda _: VMEM, out),
        compiler_params=PARAMS,
        cost_estimate=pl.CostEstimate(flops=flops, bytes_accessed=moved, transcendentals=0),
        **more,
    )


def body(prior_sample, prior_velocity, obs_cells, obs_bins, obs_values, tile_owner):
    members, levels, rows, width = prior_sample.shape
    slots = tile_owner.shape[1]
    edge = jax.ShapeDtypeStruct((levels, 2, members, width), BF16)
    low, high = call(edges_kernel, (edge, edge), [VMEM], 10**5, 10**6)(prior_sample)
    count = lax.axis_size("dom")
    up = [(i, (i + 1) % count) for i in range(count)]
    before = lax.ppermute(high, "dom", up)
    after = lax.ppermute(low, "dom", [(t, s) for s, t in up])
    pieces = jax.ShapeDtypeStruct((slots, members, 2 * width), BF16)
    partial = call(interior_kernel, pieces, [SMEM, VMEM, VMEM], 10**7, 2 * 10**6)(
        tile_owner, prior_velocity, prior_sample
    )
    outgoing = call(
        outer_kernel,
        pieces,
        [SMEM, VMEM, VMEM, VMEM, VMEM, VMEM],
        10**7,
        10**6,
    )(tile_owner, prior_velocity, prior_sample, before, after, partial)
    received = lax.all_to_all(outgoing, MEM, split_axis=0, concat_axis=0, tiled=True)
    total = slots * members
    square = pltpu.VMEM((total, total), BF16)
    updated = call(
        analysis_kernel,
        jax.ShapeDtypeStruct((total, 2 * width), BF16),
        [VMEM] * 4,
        4 * 10**9,
        2 * 10**6,
        scratch_shapes=[square] * 3,
    )(obs_cells[0], obs_bins[0], obs_values[0], received.reshape(total, 2 * width))
    results = updated.reshape(slots, members, 2 * width)
    returned = lax.all_to_all(results, MEM, split_axis=0, concat_axis=0, tiled=True)
    return call(
        restore_kernel,
        jax.ShapeDtypeStruct(prior_sample.shape, BF16),
        [SMEM, VMEM],
        10**6,
        10**6,
    )(tile_owner, returned)


def solution(mesh):
    split = Mesh(
        mesh.devices.reshape(8, 4, 2, mesh.shape["dom"]), ("mem_0", "mem_1", "mem_2", "dom")
    )
    in_specs = (
        P(MEM, None, "dom", None),
        P(),
        P("dom", MEM, None),
        P("dom", MEM, None),
        P("dom", MEM, None),
        P("dom", None),
    )
    out_specs = P(MEM, None, "dom", None)
    return jax.shard_map(body, mesh=split, in_specs=in_specs, out_specs=out_specs, check_vma=False)
```

time: 111 us -> 91.2 us (0.82)
  the two profiles are of different devices: /device:TPU:8 before, /device:TPU:1 now
where the time goes in v1:
time: 91.2 us; the launch traced here: 90.9 us
  blocking collectives  56.3 us (62%)
  starting transfers between devices  20.7 us (23%)
  Pallas kernels  12.1 us (13%)
  local copies, waits for them, and re-layouts  1.74 us (2%)
    all_to_all x1, blocking collectives, body(): lax.all_to_all(outgoing, MEM, split_axis=0, concat_axis=0, tiled=True)  30.7 us
    all_to_all x1, blocking collectives, body(): lax.all_to_all(results, MEM, split_axis=0, concat_axis=0, tiled=True)  25.6 us
    ppermute x1, starting transfers between devices, body(): after = lax.ppermute(low, 'dom', [(t, s) for s, t in up])  16.8 us
    pallas_call x1, Pallas kernels, body(): call(analysis_kernel, jax.ShapeDtypeStruct((total, 2 * width), BF16), [VM...  5.89 us
    ppermute x1, starting transfers between devices, body(): before = lax.ppermute(high, 'dom', up)  3.95 us
    pallas_call x1, Pallas kernels, body(): call(interior_kernel, pieces, [SMEM, VMEM, VMEM], 10 ** 7, 2 * 10 ** 6)  2.35 us
    pallas_call x1, Pallas kernels, body(): call(outer_kernel, pieces, [SMEM, VMEM, VMEM, VMEM, VMEM, VMEM], 10 ** 7,...  2.06 us
  transfers between devices with their start and end apart: 2, of which 0 were waited for; matrix products, arithmetic and copies ran while one was open for 0% of the time, Pallas kernels for 3%

profile of v1, /device:TPU:1, one launch (start us, length us, event | category | flops | bytes accessed | tf_op | source)
XLA Modules:
  0.0 90.9 jit_solution(10920669366723781939)
XLA Ops:
  0.0 0.0 copy-start
  0.0 1.0 %copy-done = bf16[8,8,16,256]{3,2,1,0:T(8,128)(2,1)S(1)} copy-done((bf16[8,8,16,256]{3,2,1,0:T(8,128)(2,1)S(1)}, bf16[8,8,16,256]{3,2,1,0:T(8,128)(2,1)}, u32[]{:S(2)}) %copy-start) | copy-done | bytes 524312
  1.0 0.0 copy-start.1
  1.0 0.1 shard_map.64
  1.2 0.0 copy-start.2
  1.2 3.9 %collective-permute-start = (bf16[8,2,8,256]{3,2,1,0:T(8,128)(2,1)S(1)}, bf16[8,2,8,256]{3,2,1,0:T(8,128)(2,1)S(1)}, u32[]{:S(2)}, u32[]{:S(2)}) collective-permute-start(bf16[8,2,8,256]{3,2,1,0:T(8,128)(2,1)S(1)} %get-tuple-element.7), channel_id=1, source_target_pairs={{0,1},{1,2},{2,3},{3,4},{4,5},{5,6},{6,7},{7,8},{8,9},{9,10},{10,1... | collective-permute-start | bytes 196616 | tf_op jit(solution)/shard_map/ppermute | solution.py:212
  5.1 16.8 %collective-permute-start.1 = (bf16[8,2,8,256]{3,2,1,0:T(8,128)(2,1)S(1)}, bf16[8,2,8,256]{3,2,1,0:T(8,128)(2,1)S(1)}, u32[]{:S(2)}, u32[]{:S(2)}) collective-permute-start(bf16[8,2,8,256]{3,2,1,0:T(8,128)(2,1)S(1)} %get-tuple-element.8), channel_id=1, source_target_pairs={{1,0},{2,1},{3,2},{4,3},{5,4},{6,5},{7,6},{8,7},{9,8},{10,9},{11,1... | collective-permute-start | bytes 196616 | tf_op jit(solution)/shard_map/ppermute | solution.py:213
  21.9 0.0 copy-done.1
  21.9 0.0 copy-done.2
  21.9 2.3 %shard_map.65.partial_ref = bf16[64,8,512]{2,1,0:T(8,128)(2,1)S(1)} custom-call(s32[1,64]{1,0:T(1,128)S(1)} %copy-done.2, f32[2,8,256]{2,1,0:T(8,128)S(1)} %copy-done.1, bf16[8,8,16,256]{3,2,1,0:T(8,128)(2,1)S(1)} %copy-done), custom_call_target="tpu_custom_call" | custom-call | flops 10000000 | bytes 2000000 | tf_op jit(solution)/shard_map/pallas_call | solution.py:215
  24.3 0.0 collective-permute-done.before_ref
  24.3 0.0 collective-permute-done.1.after_ref
  24.3 2.1 %shard_map.66 = bf16[64,8,512]{2,1,0:T(8,128)(2,1)S(1)} custom-call(s32[1,64]{1,0:T(1,128)S(1)} %copy-done.2, f32[2,8,256]{2,1,0:T(8,128)S(1)} %copy-done.1, bf16[8,8,16,256]{3,2,1,0:T(8,128)(2,1)S(1)} %copy-done, bf16[8,2,8,256]{3,2,1,0:T(8,128)(2,1)S(1)} %collective-permute-done.before_ref, bf16[8,2,8,256]{3,2,1,0:T(8,128)(2,1)S(1)} %collective-permute-done.1.after_ref, ...), custom_call_target="tpu_custom_call" | custom-call | flops 10000000 | bytes 1000000 | tf_op jit(solution)/shard_map/pallas_call | solution.py:218
  26.4 30.7 %all_to_all.10 = bf16[64,8,512]{2,1,0:T(8,128)(2,1)S(1)} all-to-all(bf16[64,8,512]{2,1,0:T(8,128)(2,1)S(1)} %shard_map.66), channel_id=1, replica_groups=mesh['mem_0'=8,'mem_1'=4,'mem_2'=2,'dom'=16] {'mem_0','mem_1','mem_2'}, dimensions={0} | all-to-all | bytes 1048576 | tf_op jit(solution)/shard_map/all_to_all | solution.py:225
  57.1 0.0 copy-start.3
  57.1 0.0 copy-start.4
  57.1 0.0 copy-start.5
  57.1 0.6 copy-done.3
  57.7 0.0 copy-done.4
  57.8 0.0 copy-done.5
  57.8 5.9 %shard_map.67 = bf16[512,512]{1,0:T(8,128)(2,1)S(1)} custom-call(s32[1,128]{1,0:T(1,128)S(1)} %bitcast.7, s32[1,128]{1,0:T(1,128)S(1)} %bitcast.8, f32[1,128]{1,0:T(1,128)S(1)} %bitcast.9, bf16[512,512]{1,0:T(8,128)(2,1)S(1)} %bitcast.5), custom_call_target="tpu_custom_call" | custom-call | flops 4000000000 | bytes 2000000 | tf_op jit(solution)/shard_map/pallas_call | solution.py:228
  63.7 25.6 %all_to_all.11.x_ref = bf16[64,8,512]{2,1,0:T(8,128)(2,1)S(1)} all-to-all(bf16[64,8,512]{2,1,0:T(8,128)(2,1)S(1)} %bitcast.6), channel_id=1, replica_groups=mesh['mem_0'=8,'mem_1'=4,'mem_2'=2,'dom'=16] {'mem_0','mem_1','mem_2'}, dimensions={0} | all-to-all | bytes 1048576 | tf_op jit(solution)/shard_map/all_to_all | solution.py:237
  89.2 1.6 %shard_map.68 = bf16[8,8,16,256]{3,2,1,0:T(8,128)(2,1)} custom-call(s32[1,64]{1,0:T(1,128)S(1)} %copy-done.2, bf16[64,8,512]{2,1,0:T(8,128)(2,1)S(1)} %all_to_all.11.x_ref), custom_call_target="tpu_custom_call" | custom-call | flops 1000000 | bytes 1000000 | tf_op jit(solution)/shard_map/pallas_call | solution.py:238
Async XLA Ops:
  0.0 1.0 %copy-start = (bf16[8,8,16,256]{3,2,1,0:T(8,128)(2,1)S(1)}, bf16[8,8,16,256]{3,2,1,0:T(8,128)(2,1)}, u32[]{:S(2)}) copy-start(bf16[8,8,16,256]{3,2,1,0:T(8,128)(2,1)} %x_ref.5) | copy-start | bytes 1572868
  1.0 20.9 %copy-start.1 = (f32[2,8,256]{2,1,0:T(8,128)S(1)}, f32[2,8,256]{2,1,0:T(8,128)}, u32[]{:S(2)}) copy-start(f32[2,8,256]{2,1,0:T(8,128)} %velocity_ref.3) | copy-start | bytes 49156
  1.2 20.8 %copy-start.2 = (s32[1,64]{1,0:T(1,128)S(1)}, s32[1,64]{1,0:T(1,128)}, u32[]{:S(2)}) copy-start(s32[1,64]{1,0:T(1,128)} %owner_ref.5) | copy-start | bytes 772
  1.2 23.1 %collective-permute-start = (bf16[8,2,8,256]{3,2,1,0:T(8,128)(2,1)S(1)}, bf16[8,2,8,256]{3,2,1,0:T(8,128)(2,1)S(1)}, u32[]{:S(2)}, u32[]{:S(2)}) collective-permute-start(bf16[8,2,8,256]{3,2,1,0:T(8,128)(2,1)S(1)} %get-tuple-element.7), channel_id=1, source_target_pairs={{0,1},{1,2},{2,3},{3,4},{4,5},{5,6},{6,7},{7,8},{8,9},{9,10},{10,1... | collective-permute-start | bytes 196616 | tf_op jit(solution)/shard_map/ppermute | solution.py:212
  5.1 19.2 %collective-permute-start.1 = (bf16[8,2,8,256]{3,2,1,0:T(8,128)(2,1)S(1)}, bf16[8,2,8,256]{3,2,1,0:T(8,128)(2,1)S(1)}, u32[]{:S(2)}, u32[]{:S(2)}) collective-permute-start(bf16[8,2,8,256]{3,2,1,0:T(8,128)(2,1)S(1)} %get-tuple-element.8), channel_id=1, source_target_pairs={{1,0},{2,1},{3,2},{4,3},{5,4},{6,5},{7,6},{8,7},{9,8},{10,9},{11,1... | collective-permute-start | bytes 196616 | tf_op jit(solution)/shard_map/ppermute | solution.py:213
  57.1 0.7 copy-start.3
  57.1 0.7 copy-start.4
  57.1 0.7 copy-start.5

commit v2 on v1

v2 whole, which is shorter than its diff:
```python
import jax
import jax.numpy as jnp
from jax import lax
from jax.experimental import pallas as pl
from jax.experimental.pallas import tpu as pltpu
from jax.sharding import Mesh
from jax.sharding import PartitionSpec as P

STEPS = 5
MEM = ("mem_0", "mem_1", "mem_2")

advect_coef = 0.15
diffuse_coef = 0.15
loc_step = 0.35
inflation = 1.1

F32 = jnp.float32
BF16 = jnp.bfloat16
VMEM = pl.BlockSpec(memory_space=pltpu.VMEM)
SMEM = pl.BlockSpec(memory_space=pltpu.SMEM)
PARAMS = pltpu.CompilerParams(vmem_limit_bytes=48 * 1024 * 1024)


def rows_first(block):
    return jnp.swapaxes(block.astype(F32), 0, 1)


def step(rows, along_x, along_y):
    width = rows[0].shape[-1]
    below, above, inner = [], [], []
    last = len(rows) - 1
    for r, v in enumerate(rows):
        half = 0.5 * v
        flux_y = (along_y + half) * v
        below.append(v - flux_y if r >= 2 else None)
        above.append(v + flux_y if r <= last - 2 else None)
        if 1 <= r <= last - 1:
            flux_x = (along_x + half) * v
            east = pltpu.roll(v - flux_x, width - 1, axis=1)
            west = pltpu.roll(v + flux_x, 1, axis=1)
            inner.append((east + west) - 4.0 * v)
        else:
            inner.append(None)
    return [
        rows[r] + advect_coef * (inner[r] + (below[r + 1] + above[r - 1]))
        for r in range(1, last)
    ]


def edges_kernel(x_ref, in_pair_ref, across_ref):
    levels, rows = x_ref.shape[1], x_ref.shape[2]
    even = lax.rem(lax.axis_index("dom"), 2) == 0

    def send(low_ref, high_ref):
        for level in range(levels):
            block = x_ref[:, level]
            low_ref[level] = rows_first(block[:, 0:2]).astype(BF16)
            high_ref[level] = rows_first(block[:, rows - 2 : rows]).astype(BF16)

    @pl.when(even)
    def _():
        send(across_ref, in_pair_ref)

    @pl.when(jnp.logical_not(even))
    def _():
        send(in_pair_ref, across_ref)


def put(out_ref, slot, rows, width):
    out_ref[slot, :, 0:width] = rows[0].astype(BF16)
    out_ref[slot, :, width : 2 * width] = rows[1].astype(BF16)


def interior(owner_ref, velocity_ref, x_ref, out_ref, first_ref):
    members, levels, rows, width = x_ref.shape
    pairs = rows // 2

    def one(level, carry):
        along_x = velocity_ref[0, pl.ds(level, 1), :]
        along_y = velocity_ref[1, pl.ds(level, 1), :]
        field = rows_first(x_ref[:, level])
        first = step([field[r] for r in range(rows)], along_x, along_y)
        for k, r in enumerate((0, 1, rows - 4, rows - 3)):
            first_ref[level, k] = first[r]
        done = step(first, along_x, along_y)
        for p in range(1, pairs - 1):
            put(out_ref, owner_ref[0, level * pairs + p], done[2 * p - 2 : 2 * p], width)
        return carry

    lax.fori_loop(0, levels, one, 0)


def interior_kernel(
    owner_ref, velocity_ref, x_ref, cells_ref, bins_ref, values_ref,
    out_ref, first_ref, chosen_ref, weights_ref, observed_ref,
):
    tile, obs = chosen_ref.shape
    rows = lax.broadcasted_iota(jnp.int32, (tile, obs), 0)
    chosen_ref[...] = jnp.where(rows == cells_ref[...], 1.0, 0.0).astype(BF16)
    weights_ref[...] = jnp.exp(-0.5 * (loc_step * bins_ref[...].astype(F32)) ** 2)
    observed_ref[...] = values_ref[...]

    @pl.when(lax.axis_index("dom") != lax.axis_size("dom") - 1)
    def _():
        interior(owner_ref, velocity_ref, x_ref, out_ref, first_ref)


def outer_kernel(
    owner_ref, velocity_ref, x_ref, in_pair_ref, across_ref, got_across_ref, got_pair_ref, got_last_ref,
    partial_ref, kept_ref, out_ref, first_ref,
):
    members, levels, rows, width = x_ref.shape
    pairs = rows // 2
    me, count = lax.axis_index("dom"), lax.axis_size("dom")
    late = me == count - 1

    @pl.when(late)
    def _():
        interior(owner_ref, velocity_ref, x_ref, out_ref, first_ref)

    @pl.when(jnp.logical_not(late))
    def _():
        out_ref[...] = partial_ref[...]
        first_ref[...] = kept_ref[...]

    def finish(before_ref, low_ref, high_ref, after_ref):
        def one(level, carry):
            along_x = velocity_ref[0, pl.ds(level, 1), :]
            along_y = velocity_ref[1, pl.ds(level, 1), :]

            def pair_of(ref):
                both = ref[level].astype(F32)
                return [both[0], both[1]]

            top = step(pair_of(before_ref) + pair_of(low_ref), along_x, along_y)
            top = step(top + [first_ref[level, 0], first_ref[level, 1]], along_x, along_y)
            put(out_ref, owner_ref[0, level * pairs], top, width)
            end = step(pair_of(high_ref) + pair_of(after_ref), along_x, along_y)
            end = step([first_ref[level, 2], first_ref[level, 3]] + end, along_x, along_y)
            put(out_ref, owner_ref[0, level * pairs + pairs - 1], end, width)
            return carry

        lax.fori_loop(0, levels, one, 0)

    even = lax.rem(me, 2) == 0
    ending = me >= count - 2
    for is_even in (True, False):
        for is_ending in (True, False):
            got_ref = got_last_ref if is_ending else got_pair_ref

            @pl.when(jnp.logical_and(even == is_even, ending == is_ending))
            def _():
                if is_even:
                    finish(got_across_ref, across_ref, in_pair_ref, got_ref)
                else:
                    finish(got_ref, in_pair_ref, across_ref, got_across_ref)


def dot(a, b):
    return jnp.dot(a, b, preferred_element_type=F32)


def dot_t(a, b):
    return lax.dot_general(a, b, (((1,), (1,)), ((), ())), preferred_element_type=F32)


def split(x):
    high = x.astype(BF16)
    return high, (x - high.astype(F32)).astype(BF16)


def dot3(a, b):
    a_high, a_low = split(a)
    b_high, b_low = split(b)
    return dot(a_high, b_high) + (dot(a_high, b_low) + dot(a_low, b_high))


def thirds(row):
    first = row.astype(BF16).astype(F32)
    second = (row - first).astype(BF16).astype(F32)
    third = (row - first) - second
    which = lax.broadcasted_iota(jnp.int32, (16, row.shape[1]), 0)
    parts = jnp.where(which == 0, first, jnp.where(which == 1, second, jnp.where(which == 2, third, 0.0)))
    return parts.astype(BF16)


def whole(parts):
    return (parts[2:3] + parts[1:2]) + parts[0:1]


def analysis_kernel(chosen_ref, weights_ref, values_ref, x_ref, out_ref):
    members, tile = x_ref.shape
    obs = chosen_ref.shape[1]
    ensemble = x_ref[...].astype(F32)
    average = jnp.sum(ensemble, axis=0, keepdims=True) * (1.0 / members)
    spread = (ensemble - average).astype(BF16)
    chosen = chosen_ref[...]
    weights = weights_ref[...]
    exact = dot(spread, chosen)
    picked = exact.astype(BF16)
    scaled = (exact * weights).astype(BF16)
    across = exact.T.astype(BF16)
    matrix = dot_t(scaled, picked)
    diagonal = lax.broadcasted_iota(jnp.int32, (members, members), 0) == lax.broadcasted_iota(
        jnp.int32, (members, members), 1
    )
    ridge = (members - 1) / inflation
    matrix = jnp.abs(matrix + jnp.where(diagonal, ridge, 0.0))
    norm_total = jnp.max(jnp.sum(matrix, axis=0, keepdims=True), axis=1, keepdims=True)
    over = 1.0 / norm_total
    gram = dot(across, spread)
    innovation = values_ref[...] - whole(dot(thirds(average), chosen))

    eye = jnp.where(
        lax.broadcasted_iota(jnp.int32, (obs, obs), 0) == lax.broadcasted_iota(jnp.int32, (obs, obs), 1), 1.0, 0.0
    )
    y_a = ridge * over
    y_c = eye
    y_small = y_a * eye + dot(across, scaled) * over
    z_a = 1.5 - 0.5 * y_a
    z_c = -0.5 * y_c
    z_small = 1.5 * eye - 0.5 * y_small
    f_a, f_c, f_small = z_a, z_c, z_small
    both = dot3(y_small, jnp.concatenate([f_small, f_c], axis=1))
    y_c = both[:, obs:] + f_a * y_c
    y_small = both[:, :obs]
    y_a = y_a * f_a
    for sweep in range(1, STEPS):
        both = dot3(z_small, jnp.concatenate([y_small, y_c], axis=1))
        f_small = 1.5 * eye - 0.5 * both[:, :obs]
        f_c = -0.5 * (both[:, obs:] + y_a * z_c)
        f_a = 1.5 - 0.5 * (z_a * y_a)
        right = jnp.concatenate([f_small, f_c], axis=1)
        if sweep + 1 < STEPS:
            both = dot3(jnp.concatenate([z_small, y_small], axis=0), right)
            y_c = both[obs:, obs:] + f_a * y_c
            y_small = both[obs:, :obs]
            y_a = y_a * f_a
        else:
            both = dot3(z_small, right)
        z_c = both[:obs, obs:] + f_a * z_c
        z_small = both[:obs, :obs]
        z_a = z_a * f_a

    scale = jnp.sqrt((members - 1) * over)
    line = jnp.broadcast_to(weights * innovation, (16, obs))
    line = dot3(dot3(line, z_small), z_small) * over
    mixed = dot3(jnp.concatenate([z_c * (scale * over), line], axis=0), gram)
    high, low = split(mixed[:obs])
    rest = dot(scaled, high) + dot(scaled, low)
    base = average + mixed[obs : obs + 1]
    out_ref[...] = (base + ((scale * z_a) * spread.astype(F32) + rest)).astype(BF16)


def restore_kernel(owner_ref, x_ref, out_ref, held_ref, sent):
    members, levels, rows, width = held_ref.shape
    pairs = rows // 2

    def copy(level):
        return pltpu.make_async_copy(held_ref.at[:, level], out_ref.at[:, level], sent.at[level])

    for level in range(levels):
        tiles = [x_ref[owner_ref[0, level * pairs + p]].astype(F32) for p in range(pairs)]
        field = jnp.stack([t[:, k * width : (k + 1) * width] for t in tiles for k in range(2)])
        held_ref[:, level] = jnp.swapaxes(field, 0, 1).astype(BF16)
        copy(level).start()
    for level in range(levels):
        copy(level).wait()


def call(kernel, out, in_specs, flops, moved, out_specs=None, **more):
    return pl.pallas_call(
        kernel,
        out_shape=out,
        in_specs=in_specs,
        out_specs=jax.tree.map(lambda _: VMEM, out) if out_specs is None else out_specs,
        compiler_params=PARAMS,
        cost_estimate=pl.CostEstimate(flops=flops, bytes_accessed=moved, transcendentals=0),
        **more,
    )


def advected(prior_sample, prior_velocity, obs_cells, obs_bins, obs_values, tile_owner):
    members, levels, rows, width = prior_sample.shape
    slots, obs = tile_owner.shape[1], obs_cells.shape[2]
    tile = 2 * width
    shape = jax.ShapeDtypeStruct
    edge = shape((levels, 2, members, width), BF16)
    in_pair, across = call(edges_kernel, (edge, edge), [VMEM], 10**5, 10**6)(prior_sample)
    count = lax.axis_size("dom")
    swaps = [(i, i ^ 1) for i in range(count)]
    got_pair = lax.ppermute(in_pair, "dom", swaps[:-2])
    pieces = shape((slots, members, tile), BF16)
    first = shape((levels, 4, members, width), F32)
    partial, kept, chosen, weights, values = call(
        interior_kernel,
        (pieces, first, shape((tile, obs), BF16), shape((1, obs), F32), shape((1, obs), F32)),
        [SMEM] + [VMEM] * 5,
        10**7,
        2 * 10**6,
    )(tile_owner, prior_velocity, prior_sample, obs_cells[0], obs_bins[0], obs_values[0])
    ready, in_pair, partial = lax.optimization_barrier((across, in_pair, partial))
    got_across = lax.ppermute(
        ready, "dom", [(i, (i + 1 if i % 2 else i - 1) % count) for i in range(count)]
    )
    got_last = lax.ppermute(in_pair, "dom", swaps[-2:])
    outgoing = call(
        outer_kernel,
        pieces,
        [SMEM] + [VMEM] * 9,
        10**7,
        10**6,
        scratch_shapes=[pltpu.VMEM(first.shape, F32)],
    )(
        tile_owner, prior_velocity, prior_sample, in_pair, across, got_across, got_pair, got_last,
        partial, kept,
    )
    return outgoing, chosen, weights, values


def body(prior_sample, prior_velocity, obs_cells, obs_bins, obs_values, tile_owner):
    outgoing, chosen, weights, values = advected(
        prior_sample, prior_velocity, obs_cells, obs_bins, obs_values, tile_owner
    )
    slots, members, tile = outgoing.shape
    total = slots * members
    received = lax.all_to_all(outgoing, MEM, split_axis=0, concat_axis=0, tiled=True)
    updated = analyse(chosen, weights, values, received.reshape(total, tile))
    results = updated.reshape(slots, members, tile)
    returned = lax.all_to_all(results, MEM, split_axis=0, concat_axis=0, tiled=True)
    return restored(tile_owner, returned, prior_sample.shape)


def analyse(chosen, weights, values, ensemble):
    out = jax.ShapeDtypeStruct(ensemble.shape, BF16)
    return call(analysis_kernel, out, [VMEM] * 4, 10**9, 2 * 10**6)(chosen, weights, values, ensemble)


def restored(tile_owner, returned, shape):
    return call(
        restore_kernel,
        jax.ShapeDtypeStruct(shape, BF16),
        [SMEM, VMEM],
        10**6,
        10**6,
        out_specs=pl.BlockSpec(memory_space=pl.ANY),
        scratch_shapes=[pltpu.VMEM(shape, BF16), pltpu.SemaphoreType.DMA((shape[1],))],
    )(tile_owner, returned)


def solution(mesh):
    split = Mesh(
        mesh.devices.reshape(8, 4, 2, mesh.shape["dom"]), ("mem_0", "mem_1", "mem_2", "dom")
    )
    in_specs = (
        P(MEM, None, "dom", None),
        P(),
        P("dom", MEM, None),
        P("dom", MEM, None),
        P("dom", MEM, None),
        P("dom", None),
    )
    out_specs = P(MEM, None, "dom", None)
    return jax.shard_map(body, mesh=split, in_specs=in_specs, out_specs=out_specs, check_vma=False)
```

time: 91.2 us -> 90.1 us (0.988)
  starting transfers between devices: 20.7 us -> 18.5 us
  Pallas kernels: 12.1 us -> 10.1 us
  blocking collectives: 56.3 us -> 57.7 us
  waiting for transfers between devices: 0.01 us -> 0.96 us
    ppermute x2 -> x3, starting transfers between devices: 20.7 us -> 18.5 us  [the longest x1 13.7 us: advected(): lax.ppermute(ready, 'dom', [(i, (i + 1 if i % 2 else i - 1) % count) for...]
    pallas_call x5, Pallas kernels: 12.1 us -> 10.1 us  [the longest x1 4.16 us: analyse(): call(analysis_kernel, out, [VMEM] * 4, 10 ** 9, 2 * 10 ** 6)]
    ppermute x2 -> x3, waiting for transfers between devices: 0.01 us -> 0.96 us  [the longest x1 0.96 us: advected(): lax.ppermute(ready, 'dom', [(i, (i + 1 if i % 2 else i - 1) % count) for...]
    unnamed x12 -> x16, local copies, waits for them, and re-layouts: 1.74 us -> 2.42 us
  transfers between devices with their start and end apart: 2 -> 3, of which waited for: 0 -> 1; matrix products, arithmetic and copies ran while one was open for 0% -> 0% of each run, Pallas kernels for 3% -> 3%
where the time goes in v2:
time: 90.1 us; the launch traced here: 89.8 us
  blocking collectives  57.7 us (64%)
  starting transfers between devices  18.5 us (21%)
  Pallas kernels  10.1 us (11%)
  local copies, waits for them, and re-layouts  2.42 us (3%)
  waiting for transfers between devices  0.96 us (1%)
    all_to_all x1, blocking collectives, body(): lax.all_to_all(outgoing, MEM, split_axis=0, concat_axis=0, tiled=True)  31.6 us
    all_to_all x1, blocking collectives, body(): lax.all_to_all(results, MEM, split_axis=0, concat_axis=0, tiled=True)  26.1 us
    ppermute x1, starting transfers between devices, advected(): lax.ppermute(ready, 'dom', [(i, (i + 1 if i % 2 else i - 1) % count) for...  13.7 us
    pallas_call x1, Pallas kernels, analyse(): call(analysis_kernel, out, [VMEM] * 4, 10 ** 9, 2 * 10 ** 6)  4.16 us
    ppermute x1, starting transfers between devices, advected(): got_pair = lax.ppermute(in_pair, 'dom', swaps[:-2])  4.08 us
    unnamed x16, local copies, waits for them, and re-layouts  2.42 us
    pallas_call x1, Pallas kernels, advected(): call(interior_kernel, (pieces, first, shape((tile, obs), BF16), shape((1,...  2.38 us
    pallas_call x1, Pallas kernels, advected(): call(outer_kernel, pieces, [SMEM] + [VMEM] * 9, 10 ** 7, 10 ** 6, scratch...  1.95 us
  transfers between devices with their start and end apart: 3, of which 1 were waited for; matrix products, arithmetic and copies ran while one was open for 0% of the time, Pallas kernels for 3%

profile of v2, /device:TPU:1, one launch (start us, length us, event | category | flops | bytes accessed | tf_op | source)
XLA Modules:
  0.0 89.8 jit_solution(651343157574939269)
XLA Ops:
  0.0 0.0 copy-start
  0.0 1.0 %copy-done = bf16[8,8,16,256]{3,2,1,0:T(8,128)(2,1)S(1)} copy-done((bf16[8,8,16,256]{3,2,1,0:T(8,128)(2,1)S(1)}, bf16[8,8,16,256]{3,2,1,0:T(8,128)(2,1)}, u32[]{:S(2)}) %copy-start) | copy-done | bytes 524312
  1.0 0.0 copy-start.1
  1.0 0.1 shard_map.65
  1.2 0.0 copy-start.7
  1.2 4.1 %collective-permute-start.1 = (bf16[8,2,8,256]{3,2,1,0:T(8,128)(2,1)S(1)}, bf16[8,2,8,256]{3,2,1,0:T(8,128)(2,1)S(1)}, u32[]{:S(2)}, u32[]{:S(2)}) collective-permute-start(bf16[8,2,8,256]{3,2,1,0:T(8,128)(2,1)S(1)} %get-tuple-element.21.in_pair_ref), channel_id=1, source_target_pairs={{0,1},{1,0},{2,3},{3,2},{4,5},{5,4},{6,7},{7,6},{8,9},{9,8},{10,11... | collective-permute-start | bytes 196616 | tf_op jit(solution)/shard_map/ppermute | solution.py:292
  5.3 0.0 copy-start.4
  5.3 0.0 copy-start.5
  5.3 0.0 copy-start.6
  5.3 0.0 copy-done.1
  5.3 0.0 copy-done.7
  5.3 0.6 copy-done.4
  5.9 0.0 copy-done.5
  5.9 0.0 copy-done.6
  6.0 0.0 copy-start.2
  6.0 0.7 copy-done.2
  6.7 0.0 copy-start.3
  6.7 2.4 %shard_map.64 = (bf16[64,8,512]{2,1,0:T(8,128)(2,1)S(1)}, f32[8,4,8,256]{3,2,1,0:T(8,128)S(1)}, bf16[512,128]{1,0:T(8,128)(2,1)S(1)}, f32[1,128]{1,0:T(1,128)S(1)}, f32[1,128]{1,0:T(1,128)S(1)}) custom-call(s32[1,64]{1,0:T(1,128)S(1)} %copy-done.4, f32[2,8,256]{2,1,0:T(8,128)S(1)} %copy-done.2, bf16[8,8,16,256]{3,2,1,0:T(8,128)(2,1)S(1)} %copy-done.1, ...), custom_call_target="tpu_custom_call" | custom-call | flops 10000000 | bytes 2000000 | tf_op jit(solution)/shard_map/pallas_call | solution.py:295
  9.1 13.7 %collective-permute-start = (bf16[8,2,8,256]{3,2,1,0:T(8,128)(2,1)S(1)}, bf16[8,2,8,256]{3,2,1,0:T(8,128)(2,1)S(1)}, u32[]{:S(2)}, u32[]{:S(2)}) collective-permute-start(bf16[8,2,8,256]{3,2,1,0:T(8,128)(2,1)S(1)} %get-tuple-element.22.across_ref), channel_id=1, source_target_pairs={{0,15},{1,2},{2,1},{3,4},{4,3},{5,6},{6,5},{7,8},{8,7},{9,10},{10,... | collective-permute-start | bytes 196616 | tf_op jit(solution)/shard_map/ppermute | solution.py:303
  22.8 0.7 collective-permute-start.2
  23.5 0.0 collective-permute-done.1.got_pair_ref
  23.5 1.0 %collective-permute-done.got_across_ref = bf16[8,2,8,256]{3,2,1,0:T(8,128)(2,1)S(1)} collective-permute-done((bf16[8,2,8,256]{3,2,1,0:T(8,128)(2,1)S(1)}, bf16[8,2,8,256]{3,2,1,0:T(8,128)(2,1)S(1)}, u32[]{:S(2)}, u32[]{:S(2)}) %collective-permute-start) | collective-permute-done | bytes 65568 | tf_op jit(solution)/shard_map/ppermute | solution.py:303
  24.4 0.0 collective-permute-done.2.got_last_ref
  24.4 0.0 copy-done.3
  24.4 2.0 %shard_map.66 = bf16[64,8,512]{2,1,0:T(8,128)(2,1)S(1)} custom-call(s32[1,64]{1,0:T(1,128)S(1)} %copy-done.4, f32[2,8,256]{2,1,0:T(8,128)S(1)} %copy-done.3, bf16[8,8,16,256]{3,2,1,0:T(8,128)(2,1)S(1)} %copy-done.1, bf16[8,2,8,256]{3,2,1,0:T(8,128)(2,1)S(1)} %get-tuple-element.21.in_pair_ref, bf16[8,2,8,256]{3,2,1,0:T(8,128)(2,1)S(1)} %get-tuple-element.22.across_ref, ...), custom_call_target="tpu_custom_call" | custom-call | flops 10000000 | bytes 1000000 | tf_op jit(solution)/shard_map/pallas_call | solution.py:307
  26.4 31.6 %all_to_all.10 = bf16[64,8,512]{2,1,0:T(8,128)(2,1)S(1)} all-to-all(bf16[64,8,512]{2,1,0:T(8,128)(2,1)S(1)} %shard_map.66), channel_id=1, replica_groups=mesh['mem_0'=8,'mem_1'=4,'mem_2'=2,'dom'=16] {'mem_0','mem_1','mem_2'}, dimensions={0} | all-to-all | bytes 1048576 | tf_op jit(solution)/shard_map/all_to_all | solution.py:327
  58.0 4.2 %shard_map.67 = bf16[512,512]{1,0:T(8,128)(2,1)S(1)} custom-call(bf16[512,128]{1,0:T(8,128)(2,1)S(1)} %get-tuple-element.15.chosen_ref, f32[1,128]{1,0:T(1,128)S(1)} %get-tuple-element.16.weights_ref, f32[1,128]{1,0:T(1,128)S(1)} %get-tuple-element.17.values_ref, bf16[512,512]{1,0:T(8,128)(2,1)S(1)} %bitcast.5), custom_call_target="tpu_custom_call" | custom-call | flops 1000000000 | bytes 2000000 | tf_op jit(solution)/shard_map/pallas_call | solution.py:336
  62.2 26.1 %all_to_all.11.x_ref = bf16[64,8,512]{2,1,0:T(8,128)(2,1)S(1)} all-to-all(bf16[64,8,512]{2,1,0:T(8,128)(2,1)S(1)} %bitcast.6), channel_id=1, replica_groups=mesh['mem_0'=8,'mem_1'=4,'mem_2'=2,'dom'=16] {'mem_0','mem_1','mem_2'}, dimensions={0} | all-to-all | bytes 1048576 | tf_op jit(solution)/shard_map/all_to_all | solution.py:330
  88.3 1.5 %shard_map.68 = bf16[8,8,16,256]{3,2,1,0:T(8,128)(2,1)} custom-call(s32[1,64]{1,0:T(1,128)S(1)} %copy-done.4, bf16[64,8,512]{2,1,0:T(8,128)(2,1)S(1)} %all_to_all.11.x_ref), custom_call_target="tpu_custom_call" | custom-call | flops 1000000 | bytes 1000000 | tf_op jit(solution)/shard_map/pallas_call | solution.py:340
Async XLA Ops:
  0.0 1.0 %copy-start = (bf16[8,8,16,256]{3,2,1,0:T(8,128)(2,1)S(1)}, bf16[8,8,16,256]{3,2,1,0:T(8,128)(2,1)}, u32[]{:S(2)}) copy-start(bf16[8,8,16,256]{3,2,1,0:T(8,128)(2,1)} %x_ref.5) | copy-start | bytes 1572868
  1.0 4.3 %copy-start.1 = (bf16[8,8,16,256]{3,2,1,0:T(8,128)(2,1)S(1)}, bf16[8,8,16,256]{3,2,1,0:T(8,128)(2,1)}, u32[]{:S(2)}) copy-start(bf16[8,8,16,256]{3,2,1,0:T(8,128)(2,1)} %x_ref.5) | copy-start | bytes 1572868
  1.2 4.1 %copy-start.7 = (f32[1,1,128]{2,1,0:T(1,128)S(1)}, f32[1,1,128]{2,1,0:T(1,128)}, u32[]{:S(2)}) copy-start(f32[1,1,128]{2,1,0:T(1,128)} %param.10) | copy-start | bytes 1540
  1.2 22.3 %collective-permute-start.1 = (bf16[8,2,8,256]{3,2,1,0:T(8,128)(2,1)S(1)}, bf16[8,2,8,256]{3,2,1,0:T(8,128)(2,1)S(1)}, u32[]{:S(2)}, u32[]{:S(2)}) collective-permute-start(bf16[8,2,8,256]{3,2,1,0:T(8,128)(2,1)S(1)} %get-tuple-element.21.in_pair_ref), channel_id=1, source_target_pairs={{0,1},{1,0},{2,3},{3,2},{4,5},{5,4},{6,7},{7,6},{8,9},{9,8},{10,11... | collective-permute-start | bytes 196616 | tf_op jit(solution)/shard_map/ppermute | solution.py:292
  5.3 0.7 copy-start.4
  5.3 0.7 copy-start.5
  5.3 0.7 copy-start.6
  6.0 0.7 copy-start.2
  6.7 17.8 %copy-start.3 = (f32[2,8,256]{2,1,0:T(8,128)S(1)}, f32[2,8,256]{2,1,0:T(8,128)}, u32[]{:S(2)}) copy-start(f32[2,8,256]{2,1,0:T(8,128)} %velocity_ref.3) | copy-start | bytes 49156
  9.1 15.4 %collective-permute-start = (bf16[8,2,8,256]{3,2,1,0:T(8,128)(2,1)S(1)}, bf16[8,2,8,256]{3,2,1,0:T(8,128)(2,1)S(1)}, u32[]{:S(2)}, u32[]{:S(2)}) collective-permute-start(bf16[8,2,8,256]{3,2,1,0:T(8,128)(2,1)S(1)} %get-tuple-element.22.across_ref), channel_id=1, source_target_pairs={{0,15},{1,2},{2,1},{3,4},{4,3},{5,6},{6,5},{7,8},{8,7},{9,10},{10,... | collective-permute-start | bytes 196616 | tf_op jit(solution)/shard_map/ppermute | solution.py:303
  22.8 1.6 %collective-permute-start.2 = (bf16[8,2,8,256]{3,2,1,0:T(8,128)(2,1)S(1)}, bf16[8,2,8,256]{3,2,1,0:T(8,128)(2,1)S(1)}, u32[]{:S(2)}, u32[]{:S(2)}) collective-permute-start(bf16[8,2,8,256]{3,2,1,0:T(8,128)(2,1)S(1)} %get-tuple-element.21.in_pair_ref), channel_id=1, source_target_pairs={{14,15},{15,14},{30,31},{31,30},{46,47},{47,46},{62,63},{63,62},{7... | collective-permute-start | bytes 196616 | tf_op jit(solution)/shard_map/ppermute | solution.py:306

commit v3 on v2

--- a/solution.py
+++ b/solution.py
@@ -47,7 +47,8 @@
     ]
 
 
-def edges_kernel(x_ref, in_pair_ref, across_ref):
+def edges_kernel(x_ref, out_ref, in_pair_ref, across_ref):
+    out_ref[...] = x_ref[...]
     levels, rows = x_ref.shape[1], x_ref.shape[2]
     even = lax.rem(lax.axis_index("dom"), 2) == 0
 
@@ -87,27 +88,32 @@
             put(out_ref, owner_ref[0, level * pairs + p], done[2 * p - 2 : 2 * p], width)
         return carry
 
-    lax.fori_loop(0, levels, one, 0)
-
-
-def interior_kernel(
-    owner_ref, velocity_ref, x_ref, cells_ref, bins_ref, values_ref,
-    out_ref, first_ref, chosen_ref, weights_ref, observed_ref,
-):
+    lax.fori_loop(0, levels, one, 0, unroll=2)
+
+
+def prepare(cells_ref, bins_ref, values_ref, chosen_ref, weights_ref, observed_ref):
     tile, obs = chosen_ref.shape
     rows = lax.broadcasted_iota(jnp.int32, (tile, obs), 0)
     chosen_ref[...] = jnp.where(rows == cells_ref[...], 1.0, 0.0).astype(BF16)
     weights_ref[...] = jnp.exp(-0.5 * (loc_step * bins_ref[...].astype(F32)) ** 2)
     observed_ref[...] = values_ref[...]
 
+
+def interior_kernel(
+    owner_ref, velocity_ref, x_ref, cells_ref, bins_ref, values_ref,
+    out_ref, first_ref, chosen_ref, weights_ref, observed_ref,
+):
     @pl.when(lax.axis_index("dom") != lax.axis_size("dom") - 1)
     def _():
         interior(owner_ref, velocity_ref, x_ref, out_ref, first_ref)
+        prepare(cells_ref, bins_ref, values_ref, chosen_ref, weights_ref, observed_ref)
 
 
 def outer_kernel(
-    owner_ref, velocity_ref, x_ref, in_pair_ref, across_ref, got_across_ref, got_pair_ref, got_last_ref,
-    partial_ref, kept_ref, out_ref, first_ref,
+    owner_ref, velocity_ref, x_ref, cells_ref, bins_ref, values_ref,
+    in_pair_ref, across_ref, got_across_ref, got_pair_ref, got_last_ref,
+    partial_ref, kept_ref, ready_ref, weight_ref, value_ref,
+    out_ref, chosen_ref, weights_ref, observed_ref, first_ref,
 ):
     members, levels, rows, width = x_ref.shape
     pairs = rows // 2
@@ -117,43 +123,39 @@
     @pl.when(late)
     def _():
         interior(owner_ref, velocity_ref, x_ref, out_ref, first_ref)
+        prepare(cells_ref, bins_ref, values_ref, chosen_ref, weights_ref, observed_ref)
 
     @pl.when(jnp.logical_not(late))
     def _():
         out_ref[...] = partial_ref[...]
         first_ref[...] = kept_ref[...]
-
-    def finish(before_ref, low_ref, high_ref, after_ref):
-        def one(level, carry):
-            along_x = velocity_ref[0, pl.ds(level, 1), :]
-            along_y = velocity_ref[1, pl.ds(level, 1), :]
-
-            def pair_of(ref):
-                both = ref[level].astype(F32)
-                return [both[0], both[1]]
-
-            top = step(pair_of(before_ref) + pair_of(low_ref), along_x, along_y)
-            top = step(top + [first_ref[level, 0], first_ref[level, 1]], along_x, along_y)
-            put(out_ref, owner_ref[0, level * pairs], top, width)
-            end = step(pair_of(high_ref) + pair_of(after_ref), along_x, along_y)
-            end = step([first_ref[level, 2], first_ref[level, 3]] + end, along_x, along_y)
-            put(out_ref, owner_ref[0, level * pairs + pairs - 1], end, width)
-            return carry
-
-        lax.fori_loop(0, levels, one, 0)
-
-    even = lax.rem(me, 2) == 0
-    ending = me >= count - 2
-    for is_even in (True, False):
-        for is_ending in (True, False):
-            got_ref = got_last_ref if is_ending else got_pair_ref
-
-            @pl.when(jnp.logical_and(even == is_even, ending == is_ending))
-            def _():
-                if is_even:
-                    finish(got_across_ref, across_ref, in_pair_ref, got_ref)
-                else:
-                    finish(got_ref, in_pair_ref, across_ref, got_across_ref)
+        chosen_ref[...] = ready_ref[...]
+        weights_ref[...] = weight_ref[...]
+        observed_ref[...] = value_ref[...]
+
+    shape = (members, width)
+    even = jnp.broadcast_to(lax.rem(me, 2), shape) == 0
+    ending = jnp.broadcast_to(me, shape) >= count - 2
+
+    for level in range(levels):
+        along_x = velocity_ref[0, level : level + 1, :]
+        along_y = velocity_ref[1, level : level + 1, :]
+        low, high, before, after = [], [], [], []
+        for k in range(2):
+            pair = in_pair_ref[level, k].astype(F32)
+            other = across_ref[level, k].astype(F32)
+            low.append(jnp.where(even, other, pair))
+            high.append(jnp.where(even, pair, other))
+            pair = jnp.where(ending, got_last_ref[level, k].astype(F32), got_pair_ref[level, k].astype(F32))
+            other = got_across_ref[level, k].astype(F32)
+            before.append(jnp.where(even, other, pair))
+            after.append(jnp.where(even, pair, other))
+        top = step(before + low, along_x, along_y)
+        top = step(top + [first_ref[level, 0], first_ref[level, 1]], along_x, along_y)
+        put(out_ref, owner_ref[0, level * pairs], top, width)
+        end = step(high + after, along_x, along_y)
+        end = step([first_ref[level, 2], first_ref[level, 3]] + end, along_x, along_y)
+        put(out_ref, owner_ref[0, level * pairs + pairs - 1], end, width)
 
 
 def dot(a, b):
@@ -172,7 +174,10 @@
 def dot3(a, b):
     a_high, a_low = split(a)
     b_high, b_low = split(b)
-    return dot(a_high, b_high) + (dot(a_high, b_low) + dot(a_low, b_high))
+    return dot(
+        jnp.concatenate([a_low, a_high, a_high], axis=1),
+        jnp.concatenate([b_high, b_low, b_high], axis=0),
+    )
 
 
 def thirds(row):
@@ -286,36 +291,33 @@
     tile = 2 * width
     shape = jax.ShapeDtypeStruct
     edge = shape((levels, 2, members, width), BF16)
-    in_pair, across = call(edges_kernel, (edge, edge), [VMEM], 10**5, 10**6)(prior_sample)
+    sample, in_pair, across = call(
+        edges_kernel, (shape(prior_sample.shape, BF16), edge, edge), [VMEM], 10**5, 10**6
+    )(prior_sample)
     count = lax.axis_size("dom")
     swaps = [(i, i ^ 1) for i in range(count)]
     got_pair = lax.ppermute(in_pair, "dom", swaps[:-2])
     pieces = shape((slots, members, tile), BF16)
     first = shape((levels, 4, members, width), F32)
-    partial, kept, chosen, weights, values = call(
-        interior_kernel,
-        (pieces, first, shape((tile, obs), BF16), shape((1, obs), F32), shape((1, obs), F32)),
-        [SMEM] + [VMEM] * 5,
-        10**7,
-        2 * 10**6,
-    )(tile_owner, prior_velocity, prior_sample, obs_cells[0], obs_bins[0], obs_values[0])
-    ready, in_pair, partial = lax.optimization_barrier((across, in_pair, partial))
+    prepared = (shape((tile, obs), BF16), shape((1, obs), F32), shape((1, obs), F32))
+    inputs = (tile_owner, prior_velocity, sample, obs_cells[0], obs_bins[0], obs_values[0])
+    done = call(
+        interior_kernel, (pieces, first) + prepared, [SMEM] + [VMEM] * 5, 10**7, 2 * 10**6
+    )(*inputs)
+    ready, in_pair, partial = lax.optimization_barrier((across, in_pair, done[0]))
     got_across = lax.ppermute(
         ready, "dom", [(i, (i + 1 if i % 2 else i - 1) % count) for i in range(count)]
     )
     got_last = lax.ppermute(in_pair, "dom", swaps[-2:])
-    outgoing = call(
+    outgoing, chosen, weights, observed = call(
         outer_kernel,
-        pieces,
-        [SMEM] + [VMEM] * 9,
+        (pieces,) + prepared,
+        [SMEM] + [VMEM] * 15,
         10**7,
         10**6,
         scratch_shapes=[pltpu.VMEM(first.shape, F32)],
-    )(
-        tile_owner, prior_velocity, prior_sample, in_pair, across, got_across, got_pair, got_last,
-        partial, kept,
-    )
-    return outgoing, chosen, weights, values
+    )(*inputs, in_pair, across, got_across, got_pair, got_last, partial, *done[1:])
+    return outgoing, chosen, weights, observed
 
 
 def body(prior_sample, prior_velocity, obs_cells, obs_bins, obs_values, tile_owner):

time: 90.1 us -> 88.2 us (0.979)
  Pallas kernels: 10.1 us -> 8.95 us
    unnamed x16 -> x12, local copies, waits for them, and re-layouts: 2.42 us -> 1.71 us
  transfers between devices with their start and end apart: 3 -> 3, of which waited for: 1 -> 1; matrix products, arithmetic and copies ran while one was open for 0% -> 0% of each run, Pallas kernels for 3% -> 2%
where the time goes in v3:
time: 88.2 us; the launch traced here: 87.8 us
  blocking collectives  57.5 us (65%)
  starting transfers between devices  18.6 us (21%)
  Pallas kernels  8.95 us (10%)
  local copies, waits for them, and re-layouts  1.71 us (2%)
  waiting for transfers between devices  0.96 us (1%)
    all_to_all x1, blocking collectives, body(): lax.all_to_all(outgoing, MEM, split_axis=0, concat_axis=0, tiled=True)  31.5 us
    all_to_all x1, blocking collectives, body(): lax.all_to_all(results, MEM, split_axis=0, concat_axis=0, tiled=True)  26.1 us
    ppermute x1, starting transfers between devices, advected(): lax.ppermute(ready, 'dom', [(i, (i + 1 if i % 2 else i - 1) % count) for...  14 us
    ppermute x1, starting transfers between devices, advected(): got_pair = lax.ppermute(in_pair, 'dom', swaps[:-2])  3.95 us
    pallas_call x1, Pallas kernels, analyse(): call(analysis_kernel, out, [VMEM] * 4, 10 ** 9, 2 * 10 ** 6)  3.8 us
    pallas_call x1, Pallas kernels, advected(): call(interior_kernel, (pieces, first) + prepared, [SMEM] + [VMEM] * 5, 10...  2.09 us
  transfers between devices with their start and end apart: 3, of which 1 were waited for; matrix products, arithmetic and copies ran while one was open for 0% of the time, Pallas kernels for 2%

profile of v3, /device:TPU:1, one launch (start us, length us, event | category | flops | bytes accessed | tf_op | source)
XLA Modules:
  0.0 87.8 jit_solution(7079319935069393523)
XLA Ops:
  0.0 0.0 copy-start
  0.0 1.0 %copy-done = bf16[8,8,16,256]{3,2,1,0:T(8,128)(2,1)S(1)} copy-done((bf16[8,8,16,256]{3,2,1,0:T(8,128)(2,1)S(1)}, bf16[8,8,16,256]{3,2,1,0:T(8,128)(2,1)}, u32[]{:S(2)}) %copy-start) | copy-done | bytes 524312
  1.0 0.0 copy-start.1
  1.0 0.2 shard_map.64
  1.2 3.9 %collective-permute-start.1 = (bf16[8,2,8,256]{3,2,1,0:T(8,128)(2,1)S(1)}, bf16[8,2,8,256]{3,2,1,0:T(8,128)(2,1)S(1)}, u32[]{:S(2)}, u32[]{:S(2)}) collective-permute-start(bf16[8,2,8,256]{3,2,1,0:T(8,128)(2,1)S(1)} %get-tuple-element.24.in_pair_ref), channel_id=1, source_target_pairs={{0,1},{1,0},{2,3},{3,2},{4,5},{5,4},{6,7},{7,6},{8,9},{9,8},{10,11... | collective-permute-start | bytes 196616 | tf_op jit(solution)/shard_map/ppermute | solution.py:299
  5.2 0.0 copy-start.5
  5.2 0.0 copy-start.2
  5.2 0.0 copy-start.3
  5.2 0.0 copy-start.4
  5.2 0.0 copy-done.1
  5.2 0.6 copy-done.5
  5.8 0.0 copy-done.2
  5.8 0.0 copy-done.3
  5.8 0.0 copy-done.4
  5.9 2.1 %shard_map.65 = (bf16[64,8,512]{2,1,0:T(8,128)(2,1)S(1)}, f32[8,4,8,256]{3,2,1,0:T(8,128)S(1)}, bf16[512,128]{1,0:T(8,128)(2,1)S(1)}, f32[1,128]{1,0:T(1,128)S(1)}, f32[1,128]{1,0:T(1,128)S(1)}) custom-call(s32[1,64]{1,0:T(1,128)S(1)} %copy-done.2, f32[2,8,256]{2,1,0:T(8,128)S(1)} %copy-done.1, bf16[8,8,16,256]{3,2,1,0:T(8,128)(2,1)S(1)} %get-tuple-element.20.x_ref, ...), custom_call_target="tpu_custom_call" | custom-call | flops 10000000 | bytes 2000000 | tf_op jit(solution)/shard_map/pallas_call | solution.py:304
  8.0 14.0 %collective-permute-start = (bf16[8,2,8,256]{3,2,1,0:T(8,128)(2,1)S(1)}, bf16[8,2,8,256]{3,2,1,0:T(8,128)(2,1)S(1)}, u32[]{:S(2)}, u32[]{:S(2)}) collective-permute-start(bf16[8,2,8,256]{3,2,1,0:T(8,128)(2,1)S(1)} %get-tuple-element.25.across_ref), channel_id=1, source_target_pairs={{0,15},{1,2},{2,1},{3,4},{4,3},{5,6},{6,5},{7,8},{8,7},{9,10},{10,... | collective-permute-start | bytes 196616 | tf_op jit(solution)/shard_map/ppermute | solution.py:308
  21.9 0.7 collective-permute-start.2
  22.6 0.0 collective-permute-done.1.got_pair_ref
  22.6 1.0 %collective-permute-done.got_across_ref = bf16[8,2,8,256]{3,2,1,0:T(8,128)(2,1)S(1)} collective-permute-done((bf16[8,2,8,256]{3,2,1,0:T(8,128)(2,1)S(1)}, bf16[8,2,8,256]{3,2,1,0:T(8,128)(2,1)S(1)}, u32[]{:S(2)}, u32[]{:S(2)}) %collective-permute-start) | collective-permute-done | bytes 65568 | tf_op jit(solution)/shard_map/ppermute | solution.py:308
  23.6 0.0 collective-permute-done.2.got_last_ref
  23.6 1.4 %shard_map.66 = (bf16[64,8,512]{2,1,0:T(8,128)(2,1)S(1)}, bf16[512,128]{1,0:T(8,128)(2,1)S(1)}, f32[1,128]{1,0:T(1,128)S(1)}, f32[1,128]{1,0:T(1,128)S(1)}) custom-call(s32[1,64]{1,0:T(1,128)S(1)} %copy-done.2, f32[2,8,256]{2,1,0:T(8,128)S(1)} %copy-done.1, bf16[8,8,16,256]{3,2,1,0:T(8,128)(2,1)S(1)} %get-tuple-element.20.x_ref, s32[1,128]{1,0:T(1,128)S(1)} %bitcast.8, ...), custom_call_target="tpu_custom_call" | custom-call | flops 10000000 | bytes 1000000 | tf_op jit(solution)/shard_map/pallas_call | solution.py:312
  25.0 31.5 %all_to_all.10 = bf16[64,8,512]{2,1,0:T(8,128)(2,1)S(1)} all-to-all(bf16[64,8,512]{2,1,0:T(8,128)(2,1)S(1)} %get-tuple-element.34), channel_id=1, replica_groups=mesh['mem_0'=8,'mem_1'=4,'mem_2'=2,'dom'=16] {'mem_0','mem_1','mem_2'}, dimensions={0} | all-to-all | bytes 1048576 | tf_op jit(solution)/shard_map/all_to_all | solution.py:329
  56.5 3.8 %shard_map.67 = bf16[512,512]{1,0:T(8,128)(2,1)S(1)} custom-call(bf16[512,128]{1,0:T(8,128)(2,1)S(1)} %get-tuple-element.31.chosen_ref, f32[1,128]{1,0:T(1,128)S(1)} %get-tuple-element.32.weights_ref, f32[1,128]{1,0:T(1,128)S(1)} %get-tuple-element.33.values_ref, bf16[512,512]{1,0:T(8,128)(2,1)S(1)} %bitcast.5), custom_call_target="tpu_custom_call" | custom-call | flops 1000000000 | bytes 2000000 | tf_op jit(solution)/shard_map/pallas_call | solution.py:338
  60.3 26.1 %all_to_all.11.x_ref = bf16[64,8,512]{2,1,0:T(8,128)(2,1)S(1)} all-to-all(bf16[64,8,512]{2,1,0:T(8,128)(2,1)S(1)} %bitcast.6), channel_id=1, replica_groups=mesh['mem_0'=8,'mem_1'=4,'mem_2'=2,'dom'=16] {'mem_0','mem_1','mem_2'}, dimensions={0} | all-to-all | bytes 1048576 | tf_op jit(solution)/shard_map/all_to_all | solution.py:332
  86.3 1.5 %shard_map.68 = bf16[8,8,16,256]{3,2,1,0:T(8,128)(2,1)} custom-call(s32[1,64]{1,0:T(1,128)S(1)} %copy-done.2, bf16[64,8,512]{2,1,0:T(8,128)(2,1)S(1)} %all_to_all.11.x_ref), custom_call_target="tpu_custom_call" | custom-call | flops 1000000 | bytes 1000000 | tf_op jit(solution)/shard_map/pallas_call | solution.py:342
Async XLA Ops:
  0.0 1.0 %copy-start = (bf16[8,8,16,256]{3,2,1,0:T(8,128)(2,1)S(1)}, bf16[8,8,16,256]{3,2,1,0:T(8,128)(2,1)}, u32[]{:S(2)}) copy-start(bf16[8,8,16,256]{3,2,1,0:T(8,128)(2,1)} %x_ref.1) | copy-start | bytes 1572868
  1.0 4.2 %copy-start.1 = (f32[2,8,256]{2,1,0:T(8,128)S(1)}, f32[2,8,256]{2,1,0:T(8,128)}, u32[]{:S(2)}) copy-start(f32[2,8,256]{2,1,0:T(8,128)} %velocity_ref.3) | copy-start | bytes 49156
  1.2 21.4 %collective-permute-start.1 = (bf16[8,2,8,256]{3,2,1,0:T(8,128)(2,1)S(1)}, bf16[8,2,8,256]{3,2,1,0:T(8,128)(2,1)S(1)}, u32[]{:S(2)}, u32[]{:S(2)}) collective-permute-start(bf16[8,2,8,256]{3,2,1,0:T(8,128)(2,1)S(1)} %get-tuple-element.24.in_pair_ref), channel_id=1, source_target_pairs={{0,1},{1,0},{2,3},{3,2},{4,5},{5,4},{6,7},{7,6},{8,9},{9,8},{10,11... | collective-permute-start | bytes 196616 | tf_op jit(solution)/shard_map/ppermute | solution.py:299
  5.2 0.7 copy-start.5
  5.2 0.7 copy-start.2
  5.2 0.7 copy-start.3
  5.2 0.7 copy-start.4
  8.0 15.6 %collective-permute-start = (bf16[8,2,8,256]{3,2,1,0:T(8,128)(2,1)S(1)}, bf16[8,2,8,256]{3,2,1,0:T(8,128)(2,1)S(1)}, u32[]{:S(2)}, u32[]{:S(2)}) collective-permute-start(bf16[8,2,8,256]{3,2,1,0:T(8,128)(2,1)S(1)} %get-tuple-element.25.across_ref), channel_id=1, source_target_pairs={{0,15},{1,2},{2,1},{3,4},{4,3},{5,6},{6,5},{7,8},{8,7},{9,10},{10,... | collective-permute-start | bytes 196616 | tf_op jit(solution)/shard_map/ppermute | solution.py:308
  21.9 1.6 %collective-permute-start.2 = (bf16[8,2,8,256]{3,2,1,0:T(8,128)(2,1)S(1)}, bf16[8,2,8,256]{3,2,1,0:T(8,128)(2,1)S(1)}, u32[]{:S(2)}, u32[]{:S(2)}) collective-permute-start(bf16[8,2,8,256]{3,2,1,0:T(8,128)(2,1)S(1)} %get-tuple-element.24.in_pair_ref), channel_id=1, source_target_pairs={{14,15},{15,14},{30,31},{31,30},{46,47},{47,46},{62,63},{63,62},{7... | collective-permute-start | bytes 196616 | tf_op jit(solution)/shard_map/ppermute | solution.py:311

commit v4 on v3

--- a/solution.py
+++ b/solution.py
@@ -72,7 +72,7 @@
     out_ref[slot, :, width : 2 * width] = rows[1].astype(BF16)
 
 
-def interior(owner_ref, velocity_ref, x_ref, out_ref, first_ref):
+def interior(slot_of, velocity_ref, x_ref, out_ref, first_ref):
     members, levels, rows, width = x_ref.shape
     pairs = rows // 2
 
@@ -85,77 +85,90 @@
             first_ref[level, k] = first[r]
         done = step(first, along_x, along_y)
         for p in range(1, pairs - 1):
-            put(out_ref, owner_ref[0, level * pairs + p], done[2 * p - 2 : 2 * p], width)
+            put(out_ref, slot_of(level * pairs + p), done[2 * p - 2 : 2 * p], width)
         return carry
 
     lax.fori_loop(0, levels, one, 0, unroll=2)
 
 
-def prepare(cells_ref, bins_ref, values_ref, chosen_ref, weights_ref, observed_ref):
+def is_last():
+    return lax.axis_index("dom") == lax.axis_size("dom") - 1
+
+
+def in_last_pair():
+    return lax.axis_index("dom") >= lax.axis_size("dom") - 2
+
+
+def is_even():
+    return lax.rem(lax.axis_index("dom"), 2) == 0
+
+
+def interior_kernel(velocity_ref, x_ref, out_ref, first_ref):
+    @pl.when(jnp.logical_not(is_last()))
+    def _():
+        interior(lambda tile: tile, velocity_ref, x_ref, out_ref, first_ref)
+
+
+def border(at_top, owner_ref, velocity_ref, own_ref, got_ref, first_ref, out_ref):
+    levels, _, members, width = own_ref.shape
+    pairs = owner_ref.shape[1] // levels
+    top = jnp.broadcast_to(at_top.astype(jnp.int32), (members, width)) == 1
+    kept = jnp.where(at_top, 0, 2)
+    place = jnp.where(at_top, 0, pairs - 1)
+    for level in range(levels):
+        along_x = velocity_ref[0, level : level + 1, :]
+        along_y = velocity_ref[1, level : level + 1, :]
+        own = [own_ref[level, k].astype(F32) for k in range(2)]
+        got = [got_ref[level, k].astype(F32) for k in range(2)]
+        rows = [jnp.where(top, g, o) for g, o in zip(got + own, own + got)]
+        outer = step(rows, along_x, along_y)
+        inner = [first_ref[level, kept + k] for k in range(2)]
+        rows = [jnp.where(top, o, i) for o, i in zip(outer + inner, inner + outer)]
+        put(out_ref, owner_ref[0, level * pairs + place], step(rows, along_x, along_y), width)
+
+
+def between_kernel(
+    owner_ref, velocity_ref, x_ref, cells_ref, bins_ref, values_ref, in_pair_ref, got_pair_ref, partial_ref, kept_ref,
+    out_ref, first_ref, chosen_ref, weights_ref, observed_ref,
+):
     tile, obs = chosen_ref.shape
+    levels = x_ref.shape[1]
+    pairs = owner_ref.shape[1] // levels
+
+    @pl.when(is_last())
+    def _():
+        interior(lambda t: owner_ref[0, t], velocity_ref, x_ref, out_ref, first_ref)
+
+    @pl.when(jnp.logical_not(is_last()))
+    def _():
+        for level in range(levels):
+            for p in range(1, pairs - 1):
+                out_ref[owner_ref[0, level * pairs + p]] = partial_ref[level * pairs + p]
+        first_ref[...] = kept_ref[...]
+
+    @pl.when(jnp.logical_not(in_last_pair()))
+    def _():
+        border(
+            jnp.logical_not(is_even()), owner_ref, velocity_ref, in_pair_ref, got_pair_ref, first_ref, out_ref
+        )
+
     rows = lax.broadcasted_iota(jnp.int32, (tile, obs), 0)
     chosen_ref[...] = jnp.where(rows == cells_ref[...], 1.0, 0.0).astype(BF16)
     weights_ref[...] = jnp.exp(-0.5 * (loc_step * bins_ref[...].astype(F32)) ** 2)
     observed_ref[...] = values_ref[...]
 
 
-def interior_kernel(
-    owner_ref, velocity_ref, x_ref, cells_ref, bins_ref, values_ref,
-    out_ref, first_ref, chosen_ref, weights_ref, observed_ref,
+def border_kernel(
+    owner_ref, velocity_ref, in_pair_ref, across_ref, got_across_ref, got_last_ref, first_ref, partial_ref, out_ref
 ):
-    @pl.when(lax.axis_index("dom") != lax.axis_size("dom") - 1)
-    def _():
-        interior(owner_ref, velocity_ref, x_ref, out_ref, first_ref)
-        prepare(cells_ref, bins_ref, values_ref, chosen_ref, weights_ref, observed_ref)
-
-
-def outer_kernel(
-    owner_ref, velocity_ref, x_ref, cells_ref, bins_ref, values_ref,
-    in_pair_ref, across_ref, got_across_ref, got_pair_ref, got_last_ref,
-    partial_ref, kept_ref, ready_ref, weight_ref, value_ref,
-    out_ref, chosen_ref, weights_ref, observed_ref, first_ref,
-):
-    members, levels, rows, width = x_ref.shape
-    pairs = rows // 2
-    me, count = lax.axis_index("dom"), lax.axis_size("dom")
-    late = me == count - 1
-
-    @pl.when(late)
-    def _():
-        interior(owner_ref, velocity_ref, x_ref, out_ref, first_ref)
-        prepare(cells_ref, bins_ref, values_ref, chosen_ref, weights_ref, observed_ref)
-
-    @pl.when(jnp.logical_not(late))
-    def _():
-        out_ref[...] = partial_ref[...]
-        first_ref[...] = kept_ref[...]
-        chosen_ref[...] = ready_ref[...]
-        weights_ref[...] = weight_ref[...]
-        observed_ref[...] = value_ref[...]
-
-    shape = (members, width)
-    even = jnp.broadcast_to(lax.rem(me, 2), shape) == 0
-    ending = jnp.broadcast_to(me, shape) >= count - 2
-
-    for level in range(levels):
-        along_x = velocity_ref[0, level : level + 1, :]
-        along_y = velocity_ref[1, level : level + 1, :]
-        low, high, before, after = [], [], [], []
-        for k in range(2):
-            pair = in_pair_ref[level, k].astype(F32)
-            other = across_ref[level, k].astype(F32)
-            low.append(jnp.where(even, other, pair))
-            high.append(jnp.where(even, pair, other))
-            pair = jnp.where(ending, got_last_ref[level, k].astype(F32), got_pair_ref[level, k].astype(F32))
-            other = got_across_ref[level, k].astype(F32)
-            before.append(jnp.where(even, other, pair))
-            after.append(jnp.where(even, pair, other))
-        top = step(before + low, along_x, along_y)
-        top = step(top + [first_ref[level, 0], first_ref[level, 1]], along_x, along_y)
-        put(out_ref, owner_ref[0, level * pairs], top, width)
-        end = step(high + after, along_x, along_y)
-        end = step([first_ref[level, 2], first_ref[level, 3]] + end, along_x, along_y)
-        put(out_ref, owner_ref[0, level * pairs + pairs - 1], end, width)
+    out_ref[...] = partial_ref[...]
+    border(is_even(), owner_ref, velocity_ref, across_ref, got_across_ref, first_ref, out_ref)
+
+    @pl.when(in_last_pair())
+    def _():
+        border(
+            jnp.logical_not(is_even()), owner_ref, velocity_ref, in_pair_ref, got_last_ref, first_ref, out_ref
+        )
 
 
 def dot(a, b):
@@ -205,13 +218,9 @@
     picked = exact.astype(BF16)
     scaled = (exact * weights).astype(BF16)
     across = exact.T.astype(BF16)
-    matrix = dot_t(scaled, picked)
-    diagonal = lax.broadcasted_iota(jnp.int32, (members, members), 0) == lax.broadcasted_iota(
-        jnp.int32, (members, members), 1
-    )
     ridge = (members - 1) / inflation
-    matrix = jnp.abs(matrix + jnp.where(diagonal, ridge, 0.0))
-    norm_total = jnp.max(jnp.sum(matrix, axis=0, keepdims=True), axis=1, keepdims=True)
+    sums = jnp.sum(jnp.abs(dot_t(scaled, picked)), axis=0, keepdims=True)
+    norm_total = jnp.max(sums, axis=1, keepdims=True) + ridge
     over = 1.0 / norm_total
     gram = dot(across, spread)
     innovation = values_ref[...] - whole(dot(thirds(average), chosen))
@@ -252,7 +261,7 @@
     line = dot3(dot3(line, z_small), z_small) * over
     mixed = dot3(jnp.concatenate([z_c * (scale * over), line], axis=0), gram)
     high, low = split(mixed[:obs])
-    rest = dot(scaled, high) + dot(scaled, low)
+    rest = dot(jnp.concatenate([scaled, scaled], axis=1), jnp.concatenate([low, high], axis=0))
     base = average + mixed[obs : obs + 1]
     out_ref[...] = (base + ((scale * z_a) * spread.astype(F32) + rest)).astype(BF16)
 
@@ -300,23 +309,23 @@
     pieces = shape((slots, members, tile), BF16)
     first = shape((levels, 4, members, width), F32)
     prepared = (shape((tile, obs), BF16), shape((1, obs), F32), shape((1, obs), F32))
-    inputs = (tile_owner, prior_velocity, sample, obs_cells[0], obs_bins[0], obs_values[0])
-    done = call(
-        interior_kernel, (pieces, first) + prepared, [SMEM] + [VMEM] * 5, 10**7, 2 * 10**6
-    )(*inputs)
-    ready, in_pair, partial = lax.optimization_barrier((across, in_pair, done[0]))
+    partial, kept = call(interior_kernel, (pieces, first), [VMEM] * 2, 10**7, 2 * 10**6)(
+        prior_velocity, sample
+    )
+    ready, in_pair, partial = lax.optimization_barrier((across, in_pair, partial))
     got_across = lax.ppermute(
         ready, "dom", [(i, (i + 1 if i % 2 else i - 1) % count) for i in range(count)]
     )
     got_last = lax.ppermute(in_pair, "dom", swaps[-2:])
-    outgoing, chosen, weights, observed = call(
-        outer_kernel,
-        (pieces,) + prepared,
-        [SMEM] + [VMEM] * 15,
-        10**7,
-        10**6,
-        scratch_shapes=[pltpu.VMEM(first.shape, F32)],
-    )(*inputs, in_pair, across, got_across, got_pair, got_last, partial, *done[1:])
+    partial, kept, chosen, weights, observed = call(
+        between_kernel, (pieces, first) + prepared, [SMEM] + [VMEM] * 9, 10**7, 2 * 10**6
+    )(
+        tile_owner, prior_velocity, sample, obs_cells[0], obs_bins[0], obs_values[0],
+        in_pair, got_pair, partial, kept,
+    )
+    outgoing = call(border_kernel, pieces, [SMEM] + [VMEM] * 7, 10**6, 10**6)(
+        tile_owner, prior_velocity, in_pair, across, got_across, got_last, kept, partial
+    )
     return outgoing, chosen, weights, observed
 
 

time: 88.2 us -> 86.2 us (0.977)
  waiting for transfers between devices: 0.96 us -> 0.01 us
    ppermute x1, waiting for transfers between devices: 0.96 us -> 0.01 us  [advected(): lax.ppermute(ready, 'dom', [(i, (i + 1 if i % 2 else i - 1) % count) for...]
    pallas_call x2 -> x3, Pallas kernels: 3.51 us -> 3.22 us  [the longest x1 1.52 us: advected(): call(interior_kernel, (pieces, first), [VMEM] * 2, 10 ** 7, 2 * 10 ** 6)]
  transfers between devices with their start and end apart: 3 -> 3, of which waited for: 1 -> 0; matrix products, arithmetic and copies ran while one was open for 0% -> 0% of each run, Pallas kernels for 2% -> 3%
where the time goes in v4:
time: 86.2 us; the launch traced here: 85.8 us
  blocking collectives  56.9 us (66%)
  starting transfers between devices  18.6 us (22%)
  Pallas kernels  8.53 us (10%)
  local copies, waits for them, and re-layouts  1.71 us (2%)
    all_to_all x1, blocking collectives, body(): lax.all_to_all(outgoing, MEM, split_axis=0, concat_axis=0, tiled=True)  30.8 us
    all_to_all x1, blocking collectives, body(): lax.all_to_all(results, MEM, split_axis=0, concat_axis=0, tiled=True)  26 us
    ppermute x1, starting transfers between devices, advected(): lax.ppermute(ready, 'dom', [(i, (i + 1 if i % 2 else i - 1) % count) for...  14 us
    ppermute x1, starting transfers between devices, advected(): got_pair = lax.ppermute(in_pair, 'dom', swaps[:-2])  3.95 us
    pallas_call x1, Pallas kernels, analyse(): call(analysis_kernel, out, [VMEM] * 4, 10 ** 9, 2 * 10 ** 6)  3.68 us
  transfers between devices with their start and end apart: 3, of which 0 were waited for; matrix products, arithmetic and copies ran while one was open for 0% of the time, Pallas kernels for 3%

profile of v4, /device:TPU:1, one launch (start us, length us, event | category | flops | bytes accessed | tf_op | source)
XLA Modules:
  0.0 85.8 jit_solution(7924396522387826218)
XLA Ops:
  0.0 0.0 copy-start
  0.0 1.0 %copy-done = bf16[8,8,16,256]{3,2,1,0:T(8,128)(2,1)S(1)} copy-done((bf16[8,8,16,256]{3,2,1,0:T(8,128)(2,1)S(1)}, bf16[8,8,16,256]{3,2,1,0:T(8,128)(2,1)}, u32[]{:S(2)}) %copy-start) | copy-done | bytes 524312
  1.0 0.0 copy-start.1
  1.0 0.2 shard_map.64
  1.2 3.9 %collective-permute-start = (bf16[8,2,8,256]{3,2,1,0:T(8,128)(2,1)S(1)}, bf16[8,2,8,256]{3,2,1,0:T(8,128)(2,1)S(1)}, u32[]{:S(2)}, u32[]{:S(2)}) collective-permute-start(bf16[8,2,8,256]{3,2,1,0:T(8,128)(2,1)S(1)} %get-tuple-element.22.in_pair_ref), channel_id=1, source_target_pairs={{0,1},{1,0},{2,3},{3,2},{4,5},{5,4},{6,7},{7,6},{8,9},{9,8},{10,11... | collective-permute-start | bytes 196616 | tf_op jit(solution)/shard_map/ppermute | solution.py:308
  5.2 0.0 copy-done.1
  5.2 0.0 copy-start.5
  5.2 1.5 %shard_map.65 = (bf16[64,8,512]{2,1,0:T(8,128)(2,1)S(1)}, f32[8,4,8,256]{3,2,1,0:T(8,128)S(1)}) custom-call(f32[2,8,256]{2,1,0:T(8,128)S(1)} %copy-done.1, bf16[8,8,16,256]{3,2,1,0:T(8,128)(2,1)S(1)} %get-tuple-element.18.x_ref), custom_call_target="tpu_custom_call" | custom-call | flops 10000000 | bytes 2000000 | tf_op jit(solution)/shard_map/pallas_call | solution.py:312
  6.7 14.0 %collective-permute-start.1 = (bf16[8,2,8,256]{3,2,1,0:T(8,128)(2,1)S(1)}, bf16[8,2,8,256]{3,2,1,0:T(8,128)(2,1)S(1)}, u32[]{:S(2)}, u32[]{:S(2)}) collective-permute-start(bf16[8,2,8,256]{3,2,1,0:T(8,128)(2,1)S(1)} %get-tuple-element.28.across_ref), channel_id=1, source_target_pairs={{0,15},{1,2},{2,1},{3,4},{4,3},{5,6},{6,5},{7,8},{8,7},{9,10},{10,... | collective-permute-start | bytes 196616 | tf_op jit(solution)/shard_map/ppermute | solution.py:316
  20.7 0.7 collective-permute-start.2
  21.4 0.0 collective-permute-done.got_pair_ref
  21.4 0.0 copy-start.2
  21.4 0.0 copy-start.3
  21.4 0.0 copy-start.4
  21.4 0.0 copy-done.5
  21.4 0.6 copy-done.2
  22.1 0.0 copy-done.3
  22.1 0.0 copy-done.4
  22.1 0.9 %shard_map.66 = (bf16[64,8,512]{2,1,0:T(8,128)(2,1)S(1)}, f32[8,4,8,256]{3,2,1,0:T(8,128)S(1)}, bf16[512,128]{1,0:T(8,128)(2,1)S(1)}, f32[1,128]{1,0:T(1,128)S(1)}, f32[1,128]{1,0:T(1,128)S(1)}) custom-call(s32[1,64]{1,0:T(1,128)S(1)} %copy-done.2, f32[2,8,256]{2,1,0:T(8,128)S(1)} %copy-done.1, bf16[8,8,16,256]{3,2,1,0:T(8,128)(2,1)S(1)} %get-tuple-element.18.x_ref, ...), custom_call_target="tpu_custom_call" | custom-call | flops 10000000 | bytes 2000000 | tf_op jit(solution)/shard_map/pallas_call | solution.py:320
  23.0 0.0 collective-permute-done.1.got_across_ref
  23.0 0.0 collective-permute-done.2.got_last_ref
  23.0 0.8 shard_map.67
  23.8 30.8 %all_to_all.10 = bf16[64,8,512]{2,1,0:T(8,128)(2,1)S(1)} all-to-all(bf16[64,8,512]{2,1,0:T(8,128)(2,1)S(1)} %shard_map.67), channel_id=1, replica_groups=mesh['mem_0'=8,'mem_1'=4,'mem_2'=2,'dom'=16] {'mem_0','mem_1','mem_2'}, dimensions={0} | all-to-all | bytes 1048576 | tf_op jit(solution)/shard_map/all_to_all | solution.py:338
  54.7 3.7 %shard_map.68 = bf16[512,512]{1,0:T(8,128)(2,1)S(1)} custom-call(bf16[512,128]{1,0:T(8,128)(2,1)S(1)} %get-tuple-element.25.chosen_ref, f32[1,128]{1,0:T(1,128)S(1)} %get-tuple-element.26.weights_ref, f32[1,128]{1,0:T(1,128)S(1)} %get-tuple-element.27.values_ref, bf16[512,512]{1,0:T(8,128)(2,1)S(1)} %bitcast.5), custom_call_target="tpu_custom_call" | custom-call | flops 1000000000 | bytes 2000000 | tf_op jit(solution)/shard_map/pallas_call | solution.py:347
  58.3 26.0 %all_to_all.11.x_ref = bf16[64,8,512]{2,1,0:T(8,128)(2,1)S(1)} all-to-all(bf16[64,8,512]{2,1,0:T(8,128)(2,1)S(1)} %bitcast.6), channel_id=1, replica_groups=mesh['mem_0'=8,'mem_1'=4,'mem_2'=2,'dom'=16] {'mem_0','mem_1','mem_2'}, dimensions={0} | all-to-all | bytes 1048576 | tf_op jit(solution)/shard_map/all_to_all | solution.py:341
  84.4 1.5 %shard_map.69 = bf16[8,8,16,256]{3,2,1,0:T(8,128)(2,1)} custom-call(s32[1,64]{1,0:T(1,128)S(1)} %copy-done.2, bf16[64,8,512]{2,1,0:T(8,128)(2,1)S(1)} %all_to_all.11.x_ref), custom_call_target="tpu_custom_call" | custom-call | flops 1000000 | bytes 1000000 | tf_op jit(solution)/shard_map/pallas_call | solution.py:351
Async XLA Ops:
  0.0 1.0 %copy-start = (bf16[8,8,16,256]{3,2,1,0:T(8,128)(2,1)S(1)}, bf16[8,8,16,256]{3,2,1,0:T(8,128)(2,1)}, u32[]{:S(2)}) copy-start(bf16[8,8,16,256]{3,2,1,0:T(8,128)(2,1)} %x_ref.1) | copy-start | bytes 1572868
  1.0 4.1 %copy-start.1 = (f32[2,8,256]{2,1,0:T(8,128)S(1)}, f32[2,8,256]{2,1,0:T(8,128)}, u32[]{:S(2)}) copy-start(f32[2,8,256]{2,1,0:T(8,128)} %velocity_ref.5) | copy-start | bytes 49156
  1.2 20.2 %collective-permute-start = (bf16[8,2,8,256]{3,2,1,0:T(8,128)(2,1)S(1)}, bf16[8,2,8,256]{3,2,1,0:T(8,128)(2,1)S(1)}, u32[]{:S(2)}, u32[]{:S(2)}) collective-permute-start(bf16[8,2,8,256]{3,2,1,0:T(8,128)(2,1)S(1)} %get-tuple-element.22.in_pair_ref), channel_id=1, source_target_pairs={{0,1},{1,0},{2,3},{3,2},{4,5},{5,4},{6,7},{7,6},{8,9},{9,8},{10,11... | collective-permute-start | bytes 196616 | tf_op jit(solution)/shard_map/ppermute | solution.py:308
  5.2 16.3 %copy-start.5 = (f32[1,1,128]{2,1,0:T(1,128)S(1)}, f32[1,1,128]{2,1,0:T(1,128)}, u32[]{:S(2)}) copy-start(f32[1,1,128]{2,1,0:T(1,128)} %param.10) | copy-start | bytes 1540
  6.7 16.3 %collective-permute-start.1 = (bf16[8,2,8,256]{3,2,1,0:T(8,128)(2,1)S(1)}, bf16[8,2,8,256]{3,2,1,0:T(8,128)(2,1)S(1)}, u32[]{:S(2)}, u32[]{:S(2)}) collective-permute-start(bf16[8,2,8,256]{3,2,1,0:T(8,128)(2,1)S(1)} %get-tuple-element.28.across_ref), channel_id=1, source_target_pairs={{0,15},{1,2},{2,1},{3,4},{4,3},{5,6},{6,5},{7,8},{8,7},{9,10},{10,... | collective-permute-start | bytes 196616 | tf_op jit(solution)/shard_map/ppermute | solution.py:316
  20.7 2.3 %collective-permute-start.2 = (bf16[8,2,8,256]{3,2,1,0:T(8,128)(2,1)S(1)}, bf16[8,2,8,256]{3,2,1,0:T(8,128)(2,1)S(1)}, u32[]{:S(2)}, u32[]{:S(2)}) collective-permute-start(bf16[8,2,8,256]{3,2,1,0:T(8,128)(2,1)S(1)} %get-tuple-element.22.in_pair_ref), channel_id=1, source_target_pairs={{14,15},{15,14},{30,31},{31,30},{46,47},{47,46},{62,63},{63,62},{7... | collective-permute-start | bytes 196616 | tf_op jit(solution)/shard_map/ppermute | solution.py:319
  21.4 0.7 copy-start.2
  21.4 0.7 copy-start.3
  21.4 0.7 copy-start.4

commit v5 on v4

--- a/solution.py
+++ b/solution.py
@@ -128,10 +128,8 @@
 
 
 def between_kernel(
-    owner_ref, velocity_ref, x_ref, cells_ref, bins_ref, values_ref, in_pair_ref, got_pair_ref, partial_ref, kept_ref,
-    out_ref, first_ref, chosen_ref, weights_ref, observed_ref,
+    owner_ref, velocity_ref, x_ref, in_pair_ref, got_pair_ref, partial_ref, kept_ref, out_ref, first_ref
 ):
-    tile, obs = chosen_ref.shape
     levels = x_ref.shape[1]
     pairs = owner_ref.shape[1] // levels
 
@@ -151,11 +149,6 @@
         border(
             jnp.logical_not(is_even()), owner_ref, velocity_ref, in_pair_ref, got_pair_ref, first_ref, out_ref
         )
-
-    rows = lax.broadcasted_iota(jnp.int32, (tile, obs), 0)
-    chosen_ref[...] = jnp.where(rows == cells_ref[...], 1.0, 0.0).astype(BF16)
-    weights_ref[...] = jnp.exp(-0.5 * (loc_step * bins_ref[...].astype(F32)) ** 2)
-    observed_ref[...] = values_ref[...]
 
 
 def border_kernel(
@@ -169,6 +162,16 @@
         border(
             jnp.logical_not(is_even()), owner_ref, velocity_ref, in_pair_ref, got_last_ref, first_ref, out_ref
         )
+
+
+def prepare_kernel(cells_ref, bins_ref, values_ref, chosen_ref, turned_ref, weights_ref, observed_ref):
+    tile, obs = chosen_ref.shape
+    rows = lax.broadcasted_iota(jnp.int32, (tile, obs), 0)
+    chosen = jnp.where(rows == cells_ref[...], 1.0, 0.0)
+    chosen_ref[...] = chosen.astype(BF16)
+    turned_ref[...] = chosen.T.astype(BF16)
+    weights_ref[...] = jnp.exp(-0.5 * (loc_step * bins_ref[...].astype(F32)) ** 2)
+    observed_ref[...] = values_ref[...]
 
 
 def dot(a, b):
@@ -206,7 +209,7 @@
     return (parts[2:3] + parts[1:2]) + parts[0:1]
 
 
-def analysis_kernel(chosen_ref, weights_ref, values_ref, x_ref, out_ref):
+def analysis_kernel(chosen_ref, turned_ref, weights_ref, values_ref, x_ref, out_ref):
     members, tile = x_ref.shape
     obs = chosen_ref.shape[1]
     ensemble = x_ref[...].astype(F32)
@@ -217,7 +220,7 @@
     exact = dot(spread, chosen)
     picked = exact.astype(BF16)
     scaled = (exact * weights).astype(BF16)
-    across = exact.T.astype(BF16)
+    across = dot_t(turned_ref[...], spread).astype(BF16)
     ridge = (members - 1) / inflation
     sums = jnp.sum(jnp.abs(dot_t(scaled, picked)), axis=0, keepdims=True)
     norm_total = jnp.max(sums, axis=1, keepdims=True) + ridge
@@ -257,12 +260,11 @@
         z_a = z_a * f_a
 
     scale = jnp.sqrt((members - 1) * over)
-    line = jnp.broadcast_to(weights * innovation, (16, obs))
-    line = dot3(dot3(line, z_small), z_small) * over
-    mixed = dot3(jnp.concatenate([z_c * (scale * over), line], axis=0), gram)
+    line = dot3(jnp.broadcast_to(weights * innovation, (16, obs)), z_small) * over
+    mixed = dot3(jnp.concatenate([z_c * (scale * over), z_small], axis=0), gram)
     high, low = split(mixed[:obs])
+    base = average + dot3(line, mixed[obs:])[0:1]
     rest = dot(jnp.concatenate([scaled, scaled], axis=1), jnp.concatenate([low, high], axis=0))
-    base = average + mixed[obs : obs + 1]
     out_ref[...] = (base + ((scale * z_a) * spread.astype(F32) + rest)).astype(BF16)
 
 
@@ -294,10 +296,9 @@
     )
 
 
-def advected(prior_sample, prior_velocity, obs_cells, obs_bins, obs_values, tile_owner):
+def advected(prior_sample, prior_velocity, tile_owner):
     members, levels, rows, width = prior_sample.shape
-    slots, obs = tile_owner.shape[1], obs_cells.shape[2]
-    tile = 2 * width
+    slots, tile = tile_owner.shape[1], 2 * width
     shape = jax.ShapeDtypeStruct
     edge = shape((levels, 2, members, width), BF16)
     sample, in_pair, across = call(
@@ -308,7 +309,6 @@
     got_pair = lax.ppermute(in_pair, "dom", swaps[:-2])
     pieces = shape((slots, members, tile), BF16)
     first = shape((levels, 4, members, width), F32)
-    prepared = (shape((tile, obs), BF16), shape((1, obs), F32), shape((1, obs), F32))
     partial, kept = call(interior_kernel, (pieces, first), [VMEM] * 2, 10**7, 2 * 10**6)(
         prior_velocity, sample
     )
@@ -317,34 +317,40 @@
         ready, "dom", [(i, (i + 1 if i % 2 else i - 1) % count) for i in range(count)]
     )
     got_last = lax.ppermute(in_pair, "dom", swaps[-2:])
-    partial, kept, chosen, weights, observed = call(
-        between_kernel, (pieces, first) + prepared, [SMEM] + [VMEM] * 9, 10**7, 2 * 10**6
-    )(
-        tile_owner, prior_velocity, sample, obs_cells[0], obs_bins[0], obs_values[0],
-        in_pair, got_pair, partial, kept,
-    )
-    outgoing = call(border_kernel, pieces, [SMEM] + [VMEM] * 7, 10**6, 10**6)(
+    partial, kept = call(
+        between_kernel, (pieces, first), [SMEM] + [VMEM] * 6, 10**7, 2 * 10**6
+    )(tile_owner, prior_velocity, sample, in_pair, got_pair, partial, kept)
+    return call(border_kernel, pieces, [SMEM] + [VMEM] * 7, 10**6, 10**6)(
         tile_owner, prior_velocity, in_pair, across, got_across, got_last, kept, partial
     )
-    return outgoing, chosen, weights, observed
+
+
+def prepared(cells, bins, values, tile):
+    shape = jax.ShapeDtypeStruct
+    obs = cells.shape[1]
+    row = shape((1, obs), F32)
+    out = (shape((tile, obs), BF16), shape((obs, tile), BF16), row, row)
+    return call(prepare_kernel, out, [VMEM] * 3, 10**6, 10**6)(cells, bins, values)
 
 
 def body(prior_sample, prior_velocity, obs_cells, obs_bins, obs_values, tile_owner):
-    outgoing, chosen, weights, values = advected(
-        prior_sample, prior_velocity, obs_cells, obs_bins, obs_values, tile_owner
-    )
+    outgoing = advected(prior_sample, prior_velocity, tile_owner)
     slots, members, tile = outgoing.shape
     total = slots * members
+    cells, bins, values, outgoing = lax.optimization_barrier((obs_cells, obs_bins, obs_values, outgoing))
     received = lax.all_to_all(outgoing, MEM, split_axis=0, concat_axis=0, tiled=True)
-    updated = analyse(chosen, weights, values, received.reshape(total, tile))
+    ready = prepared(cells[0], bins[0], values[0], tile)
+    updated = analyse(*ready, received.reshape(total, tile))
     results = updated.reshape(slots, members, tile)
     returned = lax.all_to_all(results, MEM, split_axis=0, concat_axis=0, tiled=True)
     return restored(tile_owner, returned, prior_sample.shape)
 
 
-def analyse(chosen, weights, values, ensemble):
+def analyse(chosen, turned, weights, values, ensemble):
     out = jax.ShapeDtypeStruct(ensemble.shape, BF16)
-    return call(analysis_kernel, out, [VMEM] * 4, 10**9, 2 * 10**6)(chosen, weights, values, ensemble)
+    return call(analysis_kernel, out, [VMEM] * 5, 10**9, 2 * 10**6)(
+        chosen, turned, weights, values, ensemble
+    )
 
 
 def restored(tile_owner, returned, shape):

time: 86.2 us -> 87.1 us (1.010)
  blocking collectives: 56.9 us -> 25.6 us
  waiting for transfers between devices: 0.01 us -> 17.7 us
  starting transfers between devices: 18.6 us -> 32.3 us
    all_to_all x1 -> x0, blocking collectives: 30.8 us -> none  [body(): lax.all_to_all(outgoing, MEM, split_axis=0, concat_axis=0, tiled=True)]
    all_to_all x0 -> x1, waiting for transfers between devices: none -> 17.6 us  [body(): lax.all_to_all(outgoing, MEM, split_axis=0, concat_axis=0, tiled=True)]
    all_to_all x0 -> x1, starting transfers between devices: none -> 13.7 us  [body(): lax.all_to_all(outgoing, MEM, split_axis=0, concat_axis=0, tiled=True)]
    pallas_call x2 -> x3, Pallas kernels: 4.56 us -> 4.51 us  [the longest x1 3.56 us: analyse(): call(analysis_kernel, out, [VMEM] * 5, 10 ** 9, 2 * 10 ** 6)]
  transfers between devices with their start and end apart: 3 -> 4, of which waited for: 0 -> 2; matrix products, arithmetic and copies ran while one was open for 0% -> 0% of each run, Pallas kernels for 3% -> 3%
where the time goes in v5:
time: 87.1 us; the launch traced here: 86.7 us
  starting transfers between devices  32.3 us (37%)
  blocking collectives  25.6 us (29%)
  waiting for transfers between devices  17.7 us (20%)
  Pallas kernels  9.27 us (11%)
  local copies, waits for them, and re-layouts  1.72 us (2%)
    all_to_all x1, blocking collectives, body(): lax.all_to_all(results, MEM, split_axis=0, concat_axis=0, tiled=True)  25.6 us
    all_to_all x1, waiting for transfers between devices, body(): lax.all_to_all(outgoing, MEM, split_axis=0, concat_axis=0, tiled=True)  17.6 us
    ppermute x1, starting transfers between devices, advected(): lax.ppermute(ready, 'dom', [(i, (i + 1 if i % 2 else i - 1) % count) for...  14 us
    all_to_all x1, starting transfers between devices, body(): lax.all_to_all(outgoing, MEM, split_axis=0, concat_axis=0, tiled=True)  13.7 us
    ppermute x1, starting transfers between devices, advected(): got_pair = lax.ppermute(in_pair, 'dom', swaps[:-2])  3.95 us
    pallas_call x1, Pallas kernels, analyse(): call(analysis_kernel, out, [VMEM] * 5, 10 ** 9, 2 * 10 ** 6)  3.56 us
  transfers between devices with their start and end apart: 4, of which 2 were waited for; matrix products, arithmetic and copies ran while one was open for 0% of the time, Pallas kernels for 3%

profile of v5, /device:TPU:1, one launch (start us, length us, event | category | flops | bytes accessed | tf_op | source)
XLA Modules:
  0.0 86.7 jit_solution(1207158172299014431)
XLA Ops:
  0.0 0.0 copy-start
  0.0 1.0 %copy-done = bf16[8,8,16,256]{3,2,1,0:T(8,128)(2,1)S(1)} copy-done((bf16[8,8,16,256]{3,2,1,0:T(8,128)(2,1)S(1)}, bf16[8,8,16,256]{3,2,1,0:T(8,128)(2,1)}, u32[]{:S(2)}) %copy-start) | copy-done | bytes 524312
  1.0 0.0 copy-start.1
  1.0 0.2 shard_map.64
  1.2 3.9 %collective-permute-start.2 = (bf16[8,2,8,256]{3,2,1,0:T(8,128)(2,1)S(1)}, bf16[8,2,8,256]{3,2,1,0:T(8,128)(2,1)S(1)}, u32[]{:S(2)}, u32[]{:S(2)}) collective-permute-start(bf16[8,2,8,256]{3,2,1,0:T(8,128)(2,1)S(1)} %get-tuple-element.27.in_pair_ref), channel_id=1, source_target_pairs={{0,1},{1,0},{2,3},{3,2},{4,5},{5,4},{6,7},{7,6},{8,9},{9,8},{10,11... | collective-permute-start | bytes 196616 | tf_op jit(solution)/shard_map/ppermute | solution.py:309
  5.2 0.0 copy-done.1
  5.2 1.5 %shard_map.65 = (bf16[64,8,512]{2,1,0:T(8,128)(2,1)S(1)}, f32[8,4,8,256]{3,2,1,0:T(8,128)S(1)}) custom-call(f32[2,8,256]{2,1,0:T(8,128)S(1)} %copy-done.1, bf16[8,8,16,256]{3,2,1,0:T(8,128)(2,1)S(1)} %get-tuple-element.25.x_ref), custom_call_target="tpu_custom_call" | custom-call | flops 10000000 | bytes 2000000 | tf_op jit(solution)/shard_map/pallas_call | solution.py:312
  6.7 0.0 copy-start.2
  6.7 14.0 %collective-permute-start = (bf16[8,2,8,256]{3,2,1,0:T(8,128)(2,1)S(1)}, bf16[8,2,8,256]{3,2,1,0:T(8,128)(2,1)S(1)}, u32[]{:S(2)}, u32[]{:S(2)}) collective-permute-start(bf16[8,2,8,256]{3,2,1,0:T(8,128)(2,1)S(1)} %get-tuple-element.28.across_ref), channel_id=1, source_target_pairs={{0,15},{1,2},{2,1},{3,4},{4,3},{5,6},{6,5},{7,8},{8,7},{9,10},{10,... | collective-permute-start | bytes 196616 | tf_op jit(solution)/shard_map/ppermute | solution.py:316
  20.7 0.7 collective-permute-start.1
  21.4 0.0 collective-permute-done.2.got_pair_ref
  21.4 0.0 copy-done.2
  21.4 0.9 shard_map.66
  22.3 0.1 collective-permute-done.got_across_ref
  22.4 0.0 collective-permute-done.1.got_last_ref
  22.4 1.6 %shard_map.67 = bf16[64,8,512]{2,1,0:T(8,128)(2,1)} custom-call(s32[1,64]{1,0:T(1,128)S(1)} %copy-done.2, f32[2,8,256]{2,1,0:T(8,128)S(1)} %copy-done.1, bf16[8,2,8,256]{3,2,1,0:T(8,128)(2,1)S(1)} %get-tuple-element.27.in_pair_ref, bf16[8,2,8,256]{3,2,1,0:T(8,128)(2,1)S(1)} %get-tuple-element.28.across_ref, ...), custom_call_target="tpu_custom_call" | custom-call | flops 1000000 | bytes 1000000 | tf_op jit(solution)/shard_map/pallas_call | solution.py:323
  24.0 13.7 %all-to-all-start = ((bf16[64,8,512]{2,1,0:T(8,128)(2,1)}), bf16[64,8,512]{2,1,0:T(8,128)(2,1)S(1)}, u32[]{:S(2)}, u32[]{:S(2)}) async-start(bf16[64,8,512]{2,1,0:T(8,128)(2,1)} %shard_map.67), calls=%async_computation | async-start | bytes 1048576 | tf_op jit(solution)/shard_map/all_to_all | solution.py:341
  37.7 0.0 copy-start.3
  37.7 0.0 copy-start.4
  37.7 0.0 copy-start.5
  37.7 0.6 copy-done.3
  38.3 0.0 copy-done.4
  38.3 0.0 copy-done.5
  38.3 0.1 shard_map.68
  38.5 17.6 %all-to-all-done = bf16[64,8,512]{2,1,0:T(8,128)(2,1)S(1)} async-done(((bf16[64,8,512]{2,1,0:T(8,128)(2,1)}), bf16[64,8,512]{2,1,0:T(8,128)(2,1)S(1)}, u32[]{:S(2)}, u32[]{:S(2)}) %all-to-all-start) | async-done | bytes 524320 | tf_op jit(solution)/shard_map/all_to_all | solution.py:341
  56.1 3.6 %shard_map.69 = bf16[512,512]{1,0:T(8,128)(2,1)S(1)} custom-call(bf16[512,128]{1,0:T(8,128)(2,1)S(1)} %get-tuple-element.36.chosen_ref, bf16[128,512]{1,0:T(8,128)(2,1)S(1)} %get-tuple-element.37.turned_ref, f32[1,128]{1,0:T(1,128)S(1)} %get-tuple-element.38.weights_ref, f32[1,128]{1,0:T(1,128)S(1)} %get-tuple-element.39.values_ref, bf16[512,512]{1,0:T(8,128)(2,1)S(1)} %bitcast.5), custom_call_target="tpu_custom_call" | custom-call | flops 1000000000 | bytes 2000000 | tf_op jit(solution)/shard_map/pallas_call | solution.py:351
  59.6 25.6 %all_to_all.10.x_ref = bf16[64,8,512]{2,1,0:T(8,128)(2,1)S(1)} all-to-all(bf16[64,8,512]{2,1,0:T(8,128)(2,1)S(1)} %bitcast.6), channel_id=1, replica_groups=mesh['mem_0'=8,'mem_1'=4,'mem_2'=2,'dom'=16] {'mem_0','mem_1','mem_2'}, dimensions={0} | all-to-all | bytes 1048576 | tf_op jit(solution)/shard_map/all_to_all | solution.py:345
  85.3 1.5 %shard_map.70 = bf16[8,8,16,256]{3,2,1,0:T(8,128)(2,1)} custom-call(s32[1,64]{1,0:T(1,128)S(1)} %copy-done.2, bf16[64,8,512]{2,1,0:T(8,128)(2,1)S(1)} %all_to_all.10.x_ref), custom_call_target="tpu_custom_call" | custom-call | flops 1000000 | bytes 1000000 | tf_op jit(solution)/shard_map/pallas_call | solution.py:357
Async XLA Ops:
  0.0 1.0 %copy-start = (bf16[8,8,16,256]{3,2,1,0:T(8,128)(2,1)S(1)}, bf16[8,8,16,256]{3,2,1,0:T(8,128)(2,1)}, u32[]{:S(2)}) copy-start(bf16[8,8,16,256]{3,2,1,0:T(8,128)(2,1)} %x_ref.1) | copy-start | bytes 1572868
  1.0 4.1 %copy-start.1 = (f32[2,8,256]{2,1,0:T(8,128)S(1)}, f32[2,8,256]{2,1,0:T(8,128)}, u32[]{:S(2)}) copy-start(f32[2,8,256]{2,1,0:T(8,128)} %velocity_ref.5) | copy-start | bytes 49156
  1.2 20.2 %collective-permute-start.2 = (bf16[8,2,8,256]{3,2,1,0:T(8,128)(2,1)S(1)}, bf16[8,2,8,256]{3,2,1,0:T(8,128)(2,1)S(1)}, u32[]{:S(2)}, u32[]{:S(2)}) collective-permute-start(bf16[8,2,8,256]{3,2,1,0:T(8,128)(2,1)S(1)} %get-tuple-element.27.in_pair_ref), channel_id=1, source_target_pairs={{0,1},{1,0},{2,3},{3,2},{4,5},{5,4},{6,7},{7,6},{8,9},{9,8},{10,11... | collective-permute-start | bytes 196616 | tf_op jit(solution)/shard_map/ppermute | solution.py:309
  6.7 14.7 %copy-start.2 = (s32[1,64]{1,0:T(1,128)S(1)}, s32[1,64]{1,0:T(1,128)}, u32[]{:S(2)}) copy-start(s32[1,64]{1,0:T(1,128)} %owner_ref.5) | copy-start | bytes 772
  6.7 15.7 %collective-permute-start = (bf16[8,2,8,256]{3,2,1,0:T(8,128)(2,1)S(1)}, bf16[8,2,8,256]{3,2,1,0:T(8,128)(2,1)S(1)}, u32[]{:S(2)}, u32[]{:S(2)}) collective-permute-start(bf16[8,2,8,256]{3,2,1,0:T(8,128)(2,1)S(1)} %get-tuple-element.28.across_ref), channel_id=1, source_target_pairs={{0,15},{1,2},{2,1},{3,4},{4,3},{5,6},{6,5},{7,8},{8,7},{9,10},{10,... | collective-permute-start | bytes 196616 | tf_op jit(solution)/shard_map/ppermute | solution.py:316
  20.7 1.6 %collective-permute-start.1 = (bf16[8,2,8,256]{3,2,1,0:T(8,128)(2,1)S(1)}, bf16[8,2,8,256]{3,2,1,0:T(8,128)(2,1)S(1)}, u32[]{:S(2)}, u32[]{:S(2)}) collective-permute-start(bf16[8,2,8,256]{3,2,1,0:T(8,128)(2,1)S(1)} %get-tuple-element.27.in_pair_ref), channel_id=1, source_target_pairs={{14,15},{15,14},{30,31},{31,30},{46,47},{47,46},{62,63},{63,62},{7... | collective-permute-start | bytes 196616 | tf_op jit(solution)/shard_map/ppermute | solution.py:319
  24.0 32.1 %all-to-all-start = ((bf16[64,8,512]{2,1,0:T(8,128)(2,1)}), bf16[64,8,512]{2,1,0:T(8,128)(2,1)S(1)}, u32[]{:S(2)}, u32[]{:S(2)}) async-start(bf16[64,8,512]{2,1,0:T(8,128)(2,1)} %shard_map.67), calls=%async_computation | async-start | bytes 1048576 | tf_op jit(solution)/shard_map/all_to_all | solution.py:341
  37.7 0.7 copy-start.3
  37.7 0.7 copy-start.4
  37.7 0.7 copy-start.5

commit v6 on v4

--- a/solution.py
+++ b/solution.py
@@ -159,9 +159,13 @@
 
 
 def border_kernel(
-    owner_ref, velocity_ref, in_pair_ref, across_ref, got_across_ref, got_last_ref, first_ref, partial_ref, out_ref
+    slots_ref, velocity_ref, in_pair_ref, across_ref, got_across_ref, got_last_ref, first_ref, partial_ref, out_ref,
+    owner_ref, arrived,
 ):
+    slots = pltpu.make_async_copy(slots_ref, owner_ref, arrived)
+    slots.start()
     out_ref[...] = partial_ref[...]
+    slots.wait()
     border(is_even(), owner_ref, velocity_ref, across_ref, got_across_ref, first_ref, out_ref)
 
     @pl.when(in_last_pair())
@@ -228,33 +232,35 @@
     eye = jnp.where(
         lax.broadcasted_iota(jnp.int32, (obs, obs), 0) == lax.broadcasted_iota(jnp.int32, (obs, obs), 1), 1.0, 0.0
     )
-    y_a = ridge * over
-    y_c = eye
-    y_small = y_a * eye + dot(across, scaled) * over
-    z_a = 1.5 - 0.5 * y_a
-    z_c = -0.5 * y_c
-    z_small = 1.5 * eye - 0.5 * y_small
-    f_a, f_c, f_small = z_a, z_c, z_small
-    both = dot3(y_small, jnp.concatenate([f_small, f_c], axis=1))
-    y_c = both[:, obs:] + f_a * y_c
-    y_small = both[:, :obs]
-    y_a = y_a * f_a
-    for sweep in range(1, STEPS):
-        both = dot3(z_small, jnp.concatenate([y_small, y_c], axis=1))
-        f_small = 1.5 * eye - 0.5 * both[:, :obs]
-        f_c = -0.5 * (both[:, obs:] + y_a * z_c)
-        f_a = 1.5 - 0.5 * (z_a * y_a)
-        right = jnp.concatenate([f_small, f_c], axis=1)
-        if sweep + 1 < STEPS:
-            both = dot3(jnp.concatenate([z_small, y_small], axis=0), right)
-            y_c = both[obs:, obs:] + f_a * y_c
-            y_small = both[obs:, :obs]
-            y_a = y_a * f_a
+    w_a = ridge * over
+    w_c = eye
+    w_small = w_a * eye + dot(across, scaled) * over
+    z_a = 1.5 - 0.5 * w_a
+    z_c = -0.5 * w_c
+    z_small = 1.5 * eye - 0.5 * w_small
+    for sweep in range(STEPS - 1):
+        right = jnp.concatenate([w_small, w_c], axis=1)
+        if sweep == 0:
+            both = dot3(w_small, right)
         else:
-            both = dot3(z_small, right)
-        z_c = both[:obs, obs:] + f_a * z_c
-        z_small = both[:obs, :obs]
-        z_a = z_a * f_a
+            both = dot3(jnp.concatenate([w_small, z_small], axis=0), right)
+            z_c = 1.5 * z_c - 0.5 * (both[obs:, obs:] + w_a * z_c)
+            z_small = 1.5 * z_small - 0.5 * both[obs:, :obs]
+            z_a = z_a * (1.5 - 0.5 * w_a)
+        u_small = both[:obs, :obs]
+        u_c = both[:obs, obs:] + w_a * w_c
+        u_a = w_a * w_a
+        f_small = 2.25 * eye - 1.5 * w_small + 0.25 * u_small
+        f_c = 0.25 * u_c - 1.5 * w_c
+        f_a = 2.25 - 1.5 * w_a + 0.25 * u_a
+        both = dot3(w_small, jnp.concatenate([f_small, f_c], axis=1))
+        w_c = both[:, obs:] + f_a * w_c
+        w_small = both[:, :obs]
+        w_a = w_a * f_a
+    both = dot3(z_small, jnp.concatenate([w_small, w_c], axis=1))
+    z_c = 1.5 * z_c - 0.5 * (both[:, obs:] + w_a * z_c)
+    z_small = 1.5 * z_small - 0.5 * both[:, :obs]
+    z_a = z_a * (1.5 - 0.5 * w_a)
 
     scale = jnp.sqrt((members - 1) * over)
     line = jnp.broadcast_to(weights * innovation, (16, obs))
@@ -323,7 +329,14 @@
         tile_owner, prior_velocity, sample, obs_cells[0], obs_bins[0], obs_values[0],
         in_pair, got_pair, partial, kept,
     )
-    outgoing = call(border_kernel, pieces, [SMEM] + [VMEM] * 7, 10**6, 10**6)(
+    outgoing = call(
+        border_kernel,
+        pieces,
+        [VMEM] * 8,
+        10**6,
+        10**6,
+        scratch_shapes=[pltpu.SMEM(tile_owner.shape, jnp.int32), pltpu.SemaphoreType.DMA(())],
+    )(
         tile_owner, prior_velocity, in_pair, across, got_across, got_last, kept, partial
     )
     return outgoing, chosen, weights, observed

time: 86.2 us -> 86.1 us (level)
  no operation moved by 1% of the time
where the time goes in v6:
time: 86.1 us; the launch traced here: 85.7 us
  blocking collectives  56.8 us (66%)
  starting transfers between devices  18.6 us (22%)
  Pallas kernels  8.44 us (10%)
  local copies, waits for them, and re-layouts  1.71 us (2%)
    all_to_all x1, blocking collectives, body(): lax.all_to_all(outgoing, MEM, split_axis=0, concat_axis=0, tiled=True)  30.8 us
    all_to_all x1, blocking collectives, body(): lax.all_to_all(results, MEM, split_axis=0, concat_axis=0, tiled=True)  26 us
    ppermute x1, starting transfers between devices, advected(): lax.ppermute(ready, 'dom', [(i, (i + 1 if i % 2 else i - 1) % count) for...  14 us
    ppermute x1, starting transfers between devices, advected(): got_pair = lax.ppermute(in_pair, 'dom', swaps[:-2])  3.95 us
    pallas_call x1, Pallas kernels, analyse(): call(analysis_kernel, out, [VMEM] * 4, 10 ** 9, 2 * 10 ** 6)  3.59 us
  transfers between devices with their start and end apart: 3, of which 0 were waited for; matrix products, arithmetic and copies ran while one was open for 0% of the time, Pallas kernels for 3%

profile of v6, /device:TPU:1, one launch (start us, length us, event | category | flops | bytes accessed | tf_op | source)
XLA Modules:
  0.0 85.7 jit_solution(12730498888891261856)
XLA Ops:
  0.0 0.0 copy-start
  0.0 1.0 %copy-done = bf16[8,8,16,256]{3,2,1,0:T(8,128)(2,1)S(1)} copy-done((bf16[8,8,16,256]{3,2,1,0:T(8,128)(2,1)S(1)}, bf16[8,8,16,256]{3,2,1,0:T(8,128)(2,1)}, u32[]{:S(2)}) %copy-start) | copy-done | bytes 524312
  1.0 0.0 copy-start.1
  1.0 0.2 shard_map.64
  1.2 3.9 %collective-permute-start = (bf16[8,2,8,256]{3,2,1,0:T(8,128)(2,1)S(1)}, bf16[8,2,8,256]{3,2,1,0:T(8,128)(2,1)S(1)}, u32[]{:S(2)}, u32[]{:S(2)}) collective-permute-start(bf16[8,2,8,256]{3,2,1,0:T(8,128)(2,1)S(1)} %get-tuple-element.22.in_pair_ref), channel_id=1, source_target_pairs={{0,1},{1,0},{2,3},{3,2},{4,5},{5,4},{6,7},{7,6},{8,9},{9,8},{10,11... | collective-permute-start | bytes 196616 | tf_op jit(solution)/shard_map/ppermute | solution.py:314
  5.2 0.0 copy-done.1
  5.2 0.0 copy-start.5
  5.2 1.5 %shard_map.65 = (bf16[64,8,512]{2,1,0:T(8,128)(2,1)S(1)}, f32[8,4,8,256]{3,2,1,0:T(8,128)S(1)}) custom-call(f32[2,8,256]{2,1,0:T(8,128)S(1)} %copy-done.1, bf16[8,8,16,256]{3,2,1,0:T(8,128)(2,1)S(1)} %get-tuple-element.18.x_ref), custom_call_target="tpu_custom_call" | custom-call | flops 10000000 | bytes 2000000 | tf_op jit(solution)/shard_map/pallas_call | solution.py:318
  6.7 14.0 %collective-permute-start.1 = (bf16[8,2,8,256]{3,2,1,0:T(8,128)(2,1)S(1)}, bf16[8,2,8,256]{3,2,1,0:T(8,128)(2,1)S(1)}, u32[]{:S(2)}, u32[]{:S(2)}) collective-permute-start(bf16[8,2,8,256]{3,2,1,0:T(8,128)(2,1)S(1)} %get-tuple-element.28.across_ref), channel_id=1, source_target_pairs={{0,15},{1,2},{2,1},{3,4},{4,3},{5,6},{6,5},{7,8},{8,7},{9,10},{10,... | collective-permute-start | bytes 196616 | tf_op jit(solution)/shard_map/ppermute | solution.py:322
  20.7 0.7 collective-permute-start.2
  21.4 0.0 collective-permute-done.got_pair_ref
  21.4 0.0 copy-start.2
  21.4 0.0 copy-start.3
  21.4 0.0 copy-start.4
  21.4 0.0 copy-done.5
  21.4 0.6 copy-done.2
  22.1 0.0 copy-done.3
  22.1 0.0 copy-done.4
  22.1 0.9 %shard_map.66 = (bf16[64,8,512]{2,1,0:T(8,128)(2,1)S(1)}, f32[8,4,8,256]{3,2,1,0:T(8,128)S(1)}, bf16[512,128]{1,0:T(8,128)(2,1)S(1)}, f32[1,128]{1,0:T(1,128)S(1)}, f32[1,128]{1,0:T(1,128)S(1)}) custom-call(s32[1,64]{1,0:T(1,128)S(1)} %copy-done.2, f32[2,8,256]{2,1,0:T(8,128)S(1)} %copy-done.1, bf16[8,8,16,256]{3,2,1,0:T(8,128)(2,1)S(1)} %get-tuple-element.18.x_ref, ...), custom_call_target="tpu_custom_call" | custom-call | flops 10000000 | bytes 2000000 | tf_op jit(solution)/shard_map/pallas_call | solution.py:326
  23.0 0.0 collective-permute-done.1.got_across_ref
  23.0 0.0 collective-permute-done.2.got_last_ref
  23.0 0.8 shard_map.67
  23.8 30.8 %all_to_all.10 = bf16[64,8,512]{2,1,0:T(8,128)(2,1)S(1)} all-to-all(bf16[64,8,512]{2,1,0:T(8,128)(2,1)S(1)} %shard_map.67), channel_id=1, replica_groups=mesh['mem_0'=8,'mem_1'=4,'mem_2'=2,'dom'=16] {'mem_0','mem_1','mem_2'}, dimensions={0} | all-to-all | bytes 1048576 | tf_op jit(solution)/shard_map/all_to_all | solution.py:351
  54.7 3.6 %shard_map.68 = bf16[512,512]{1,0:T(8,128)(2,1)S(1)} custom-call(bf16[512,128]{1,0:T(8,128)(2,1)S(1)} %get-tuple-element.25.chosen_ref, f32[1,128]{1,0:T(1,128)S(1)} %get-tuple-element.26.weights_ref, f32[1,128]{1,0:T(1,128)S(1)} %get-tuple-element.27.values_ref, bf16[512,512]{1,0:T(8,128)(2,1)S(1)} %bitcast.5), custom_call_target="tpu_custom_call" | custom-call | flops 1000000000 | bytes 2000000 | tf_op jit(solution)/shard_map/pallas_call | solution.py:360
  58.3 26.0 %all_to_all.11.x_ref = bf16[64,8,512]{2,1,0:T(8,128)(2,1)S(1)} all-to-all(bf16[64,8,512]{2,1,0:T(8,128)(2,1)S(1)} %bitcast.6), channel_id=1, replica_groups=mesh['mem_0'=8,'mem_1'=4,'mem_2'=2,'dom'=16] {'mem_0','mem_1','mem_2'}, dimensions={0} | all-to-all | bytes 1048576 | tf_op jit(solution)/shard_map/all_to_all | solution.py:354
  84.3 1.5 %shard_map.69 = bf16[8,8,16,256]{3,2,1,0:T(8,128)(2,1)} custom-call(s32[1,64]{1,0:T(1,128)S(1)} %copy-done.2, bf16[64,8,512]{2,1,0:T(8,128)(2,1)S(1)} %all_to_all.11.x_ref), custom_call_target="tpu_custom_call" | custom-call | flops 1000000 | bytes 1000000 | tf_op jit(solution)/shard_map/pallas_call | solution.py:364
Async XLA Ops:
  0.0 1.0 %copy-start = (bf16[8,8,16,256]{3,2,1,0:T(8,128)(2,1)S(1)}, bf16[8,8,16,256]{3,2,1,0:T(8,128)(2,1)}, u32[]{:S(2)}) copy-start(bf16[8,8,16,256]{3,2,1,0:T(8,128)(2,1)} %x_ref.1) | copy-start | bytes 1572868
  1.0 4.1 %copy-start.1 = (f32[2,8,256]{2,1,0:T(8,128)S(1)}, f32[2,8,256]{2,1,0:T(8,128)}, u32[]{:S(2)}) copy-start(f32[2,8,256]{2,1,0:T(8,128)} %velocity_ref.5) | copy-start | bytes 49156
  1.2 20.2 %collective-permute-start = (bf16[8,2,8,256]{3,2,1,0:T(8,128)(2,1)S(1)}, bf16[8,2,8,256]{3,2,1,0:T(8,128)(2,1)S(1)}, u32[]{:S(2)}, u32[]{:S(2)}) collective-permute-start(bf16[8,2,8,256]{3,2,1,0:T(8,128)(2,1)S(1)} %get-tuple-element.22.in_pair_ref), channel_id=1, source_target_pairs={{0,1},{1,0},{2,3},{3,2},{4,5},{5,4},{6,7},{7,6},{8,9},{9,8},{10,11... | collective-permute-start | bytes 196616 | tf_op jit(solution)/shard_map/ppermute | solution.py:314
  5.2 16.3 %copy-start.5 = (f32[1,1,128]{2,1,0:T(1,128)S(1)}, f32[1,1,128]{2,1,0:T(1,128)}, u32[]{:S(2)}) copy-start(f32[1,1,128]{2,1,0:T(1,128)} %param.10) | copy-start | bytes 1540
  6.7 16.3 %collective-permute-start.1 = (bf16[8,2,8,256]{3,2,1,0:T(8,128)(2,1)S(1)}, bf16[8,2,8,256]{3,2,1,0:T(8,128)(2,1)S(1)}, u32[]{:S(2)}, u32[]{:S(2)}) collective-permute-start(bf16[8,2,8,256]{3,2,1,0:T(8,128)(2,1)S(1)} %get-tuple-element.28.across_ref), channel_id=1, source_target_pairs={{0,15},{1,2},{2,1},{3,4},{4,3},{5,6},{6,5},{7,8},{8,7},{9,10},{10,... | collective-permute-start | bytes 196616 | tf_op jit(solution)/shard_map/ppermute | solution.py:322
  20.7 2.3 %collective-permute-start.2 = (bf16[8,2,8,256]{3,2,1,0:T(8,128)(2,1)S(1)}, bf16[8,2,8,256]{3,2,1,0:T(8,128)(2,1)S(1)}, u32[]{:S(2)}, u32[]{:S(2)}) collective-permute-start(bf16[8,2,8,256]{3,2,1,0:T(8,128)(2,1)S(1)} %get-tuple-element.22.in_pair_ref), channel_id=1, source_target_pairs={{14,15},{15,14},{30,31},{31,30},{46,47},{47,46},{62,63},{63,62},{7... | collective-permute-start | bytes 196616 | tf_op jit(solution)/shard_map/ppermute | solution.py:325
  21.4 0.7 copy-start.2
  21.4 0.7 copy-start.3
  21.4 0.7 copy-start.4

commit v7 on v6

--- a/solution.py
+++ b/solution.py
@@ -109,12 +109,13 @@
         interior(lambda tile: tile, velocity_ref, x_ref, out_ref, first_ref)
 
 
-def border(at_top, owner_ref, velocity_ref, own_ref, got_ref, first_ref, out_ref):
+def border(at_top, owner_ref, velocity_ref, own_ref, got_ref, first_ref, out_ref, before_slots=None):
     levels, _, members, width = own_ref.shape
     pairs = owner_ref.shape[1] // levels
     top = jnp.broadcast_to(at_top.astype(jnp.int32), (members, width)) == 1
     kept = jnp.where(at_top, 0, 2)
     place = jnp.where(at_top, 0, pairs - 1)
+    done = []
     for level in range(levels):
         along_x = velocity_ref[0, level : level + 1, :]
         along_y = velocity_ref[1, level : level + 1, :]
@@ -124,7 +125,11 @@
         outer = step(rows, along_x, along_y)
         inner = [first_ref[level, kept + k] for k in range(2)]
         rows = [jnp.where(top, o, i) for o, i in zip(outer + inner, inner + outer)]
-        put(out_ref, owner_ref[0, level * pairs + place], step(rows, along_x, along_y), width)
+        done.append(step(rows, along_x, along_y))
+    if before_slots is not None:
+        before_slots()
+    for level in range(levels):
+        put(out_ref, owner_ref[0, level * pairs + place], done[level], width)
 
 
 def between_kernel(
@@ -164,9 +169,9 @@
 ):
     slots = pltpu.make_async_copy(slots_ref, owner_ref, arrived)
     slots.start()
-    out_ref[...] = partial_ref[...]
-    slots.wait()
-    border(is_even(), owner_ref, velocity_ref, across_ref, got_across_ref, first_ref, out_ref)
+    border(
+        is_even(), owner_ref, velocity_ref, across_ref, got_across_ref, first_ref, out_ref, before_slots=slots.wait
+    )
 
     @pl.when(in_last_pair())
     def _():
@@ -336,6 +341,7 @@
         10**6,
         10**6,
         scratch_shapes=[pltpu.SMEM(tile_owner.shape, jnp.int32), pltpu.SemaphoreType.DMA(())],
+        input_output_aliases={7: 0},
     )(
         tile_owner, prior_velocity, in_pair, across, got_across, got_last, kept, partial
     )

time: 86.1 us -> 85.9 us (level)
  no operation moved by 1% of the time
where the time goes in v7:
time: 85.9 us; the launch traced here: 85.6 us
  blocking collectives  56.9 us (66%)
  starting transfers between devices  18.6 us (22%)
  Pallas kernels  8.24 us (10%)
  local copies, waits for them, and re-layouts  1.71 us (2%)
    all_to_all x1, blocking collectives, body(): lax.all_to_all(outgoing, MEM, split_axis=0, concat_axis=0, tiled=True)  30.8 us
    all_to_all x1, blocking collectives, body(): lax.all_to_all(results, MEM, split_axis=0, concat_axis=0, tiled=True)  26 us
    ppermute x1, starting transfers between devices, advected(): lax.ppermute(ready, 'dom', [(i, (i + 1 if i % 2 else i - 1) % count) for...  14 us
    ppermute x1, starting transfers between devices, advected(): got_pair = lax.ppermute(in_pair, 'dom', swaps[:-2])  3.95 us
    pallas_call x1, Pallas kernels, analyse(): call(analysis_kernel, out, [VMEM] * 4, 10 ** 9, 2 * 10 ** 6)  3.57 us
  transfers between devices with their start and end apart: 3, of which 0 were waited for; matrix products, arithmetic and copies ran while one was open for 0% of the time, Pallas kernels for 3%

profile of v7, /device:TPU:1, one launch (start us, length us, event | category | flops | bytes accessed | tf_op | source)
XLA Modules:
  0.0 85.6 jit_solution(4396592241585718914)
XLA Ops:
  0.0 0.0 copy-start
  0.0 1.0 %copy-done = bf16[8,8,16,256]{3,2,1,0:T(8,128)(2,1)S(1)} copy-done((bf16[8,8,16,256]{3,2,1,0:T(8,128)(2,1)S(1)}, bf16[8,8,16,256]{3,2,1,0:T(8,128)(2,1)}, u32[]{:S(2)}) %copy-start) | copy-done | bytes 524312
  1.0 0.0 copy-start.1
  1.0 0.2 shard_map.64
  1.2 3.9 %collective-permute-start = (bf16[8,2,8,256]{3,2,1,0:T(8,128)(2,1)S(1)}, bf16[8,2,8,256]{3,2,1,0:T(8,128)(2,1)S(1)}, u32[]{:S(2)}, u32[]{:S(2)}) collective-permute-start(bf16[8,2,8,256]{3,2,1,0:T(8,128)(2,1)S(1)} %get-tuple-element.22.in_pair_ref), channel_id=1, source_target_pairs={{0,1},{1,0},{2,3},{3,2},{4,5},{5,4},{6,7},{7,6},{8,9},{9,8},{10,11... | collective-permute-start | bytes 196616 | tf_op jit(solution)/shard_map/ppermute | solution.py:319
  5.2 0.0 copy-done.1
  5.2 0.0 copy-start.5
  5.2 1.5 %shard_map.65 = (bf16[64,8,512]{2,1,0:T(8,128)(2,1)S(1)}, f32[8,4,8,256]{3,2,1,0:T(8,128)S(1)}) custom-call(f32[2,8,256]{2,1,0:T(8,128)S(1)} %copy-done.1, bf16[8,8,16,256]{3,2,1,0:T(8,128)(2,1)S(1)} %get-tuple-element.18.x_ref), custom_call_target="tpu_custom_call" | custom-call | flops 10000000 | bytes 2000000 | tf_op jit(solution)/shard_map/pallas_call | solution.py:323
  6.7 14.0 %collective-permute-start.1 = (bf16[8,2,8,256]{3,2,1,0:T(8,128)(2,1)S(1)}, bf16[8,2,8,256]{3,2,1,0:T(8,128)(2,1)S(1)}, u32[]{:S(2)}, u32[]{:S(2)}) collective-permute-start(bf16[8,2,8,256]{3,2,1,0:T(8,128)(2,1)S(1)} %get-tuple-element.28.across_ref), channel_id=1, source_target_pairs={{0,15},{1,2},{2,1},{3,4},{4,3},{5,6},{6,5},{7,8},{8,7},{9,10},{10,... | collective-permute-start | bytes 196616 | tf_op jit(solution)/shard_map/ppermute | solution.py:327
  20.7 0.7 collective-permute-start.2
  21.4 0.0 collective-permute-done.got_pair_ref
  21.4 0.0 copy-start.2
  21.4 0.0 copy-start.3
  21.4 0.0 copy-start.4
  21.4 0.0 copy-done.5
  21.4 0.6 copy-done.2
  22.1 0.0 copy-done.3
  22.1 0.0 copy-done.4
  22.1 0.9 %shard_map.66 = (bf16[64,8,512]{2,1,0:T(8,128)(2,1)S(1)}, f32[8,4,8,256]{3,2,1,0:T(8,128)S(1)}, bf16[512,128]{1,0:T(8,128)(2,1)S(1)}, f32[1,128]{1,0:T(1,128)S(1)}, f32[1,128]{1,0:T(1,128)S(1)}) custom-call(s32[1,64]{1,0:T(1,128)S(1)} %copy-done.2, f32[2,8,256]{2,1,0:T(8,128)S(1)} %copy-done.1, bf16[8,8,16,256]{3,2,1,0:T(8,128)(2,1)S(1)} %get-tuple-element.18.x_ref, ...), custom_call_target="tpu_custom_call" | custom-call | flops 10000000 | bytes 2000000 | tf_op jit(solution)/shard_map/pallas_call | solution.py:331
  23.0 0.0 collective-permute-done.1.got_across_ref
  23.0 0.0 collective-permute-done.2.got_last_ref
  23.0 0.6 shard_map.67
  23.6 30.8 %all_to_all.10 = bf16[64,8,512]{2,1,0:T(8,128)(2,1)S(1)} all-to-all(bf16[64,8,512]{2,1,0:T(8,128)(2,1)S(1)} %shard_map.67), channel_id=1, replica_groups=mesh['mem_0'=8,'mem_1'=4,'mem_2'=2,'dom'=16] {'mem_0','mem_1','mem_2'}, dimensions={0} | all-to-all | bytes 1048576 | tf_op jit(solution)/shard_map/all_to_all | solution.py:357
  54.5 3.6 %shard_map.68 = bf16[512,512]{1,0:T(8,128)(2,1)S(1)} custom-call(bf16[512,128]{1,0:T(8,128)(2,1)S(1)} %get-tuple-element.25.chosen_ref, f32[1,128]{1,0:T(1,128)S(1)} %get-tuple-element.26.weights_ref, f32[1,128]{1,0:T(1,128)S(1)} %get-tuple-element.27.values_ref, bf16[512,512]{1,0:T(8,128)(2,1)S(1)} %bitcast.5), custom_call_target="tpu_custom_call" | custom-call | flops 1000000000 | bytes 2000000 | tf_op jit(solution)/shard_map/pallas_call | solution.py:366
  58.0 26.0 %all_to_all.11.x_ref = bf16[64,8,512]{2,1,0:T(8,128)(2,1)S(1)} all-to-all(bf16[64,8,512]{2,1,0:T(8,128)(2,1)S(1)} %bitcast.6), channel_id=1, replica_groups=mesh['mem_0'=8,'mem_1'=4,'mem_2'=2,'dom'=16] {'mem_0','mem_1','mem_2'}, dimensions={0} | all-to-all | bytes 1048576 | tf_op jit(solution)/shard_map/all_to_all | solution.py:360
  84.1 1.5 %shard_map.69 = bf16[8,8,16,256]{3,2,1,0:T(8,128)(2,1)} custom-call(s32[1,64]{1,0:T(1,128)S(1)} %copy-done.2, bf16[64,8,512]{2,1,0:T(8,128)(2,1)S(1)} %all_to_all.11.x_ref), custom_call_target="tpu_custom_call" | custom-call | flops 1000000 | bytes 1000000 | tf_op jit(solution)/shard_map/pallas_call | solution.py:370
Async XLA Ops:
  0.0 1.0 %copy-start = (bf16[8,8,16,256]{3,2,1,0:T(8,128)(2,1)S(1)}, bf16[8,8,16,256]{3,2,1,0:T(8,128)(2,1)}, u32[]{:S(2)}) copy-start(bf16[8,8,16,256]{3,2,1,0:T(8,128)(2,1)} %x_ref.1) | copy-start | bytes 1572868
  1.0 4.1 %copy-start.1 = (f32[2,8,256]{2,1,0:T(8,128)S(1)}, f32[2,8,256]{2,1,0:T(8,128)}, u32[]{:S(2)}) copy-start(f32[2,8,256]{2,1,0:T(8,128)} %velocity_ref.5) | copy-start | bytes 49156
  1.2 20.2 %collective-permute-start = (bf16[8,2,8,256]{3,2,1,0:T(8,128)(2,1)S(1)}, bf16[8,2,8,256]{3,2,1,0:T(8,128)(2,1)S(1)}, u32[]{:S(2)}, u32[]{:S(2)}) collective-permute-start(bf16[8,2,8,256]{3,2,1,0:T(8,128)(2,1)S(1)} %get-tuple-element.22.in_pair_ref), channel_id=1, source_target_pairs={{0,1},{1,0},{2,3},{3,2},{4,5},{5,4},{6,7},{7,6},{8,9},{9,8},{10,11... | collective-permute-start | bytes 196616 | tf_op jit(solution)/shard_map/ppermute | solution.py:319
  5.2 16.3 %copy-start.5 = (f32[1,1,128]{2,1,0:T(1,128)S(1)}, f32[1,1,128]{2,1,0:T(1,128)}, u32[]{:S(2)}) copy-start(f32[1,1,128]{2,1,0:T(1,128)} %param.10) | copy-start | bytes 1540
  6.7 16.3 %collective-permute-start.1 = (bf16[8,2,8,256]{3,2,1,0:T(8,128)(2,1)S(1)}, bf16[8,2,8,256]{3,2,1,0:T(8,128)(2,1)S(1)}, u32[]{:S(2)}, u32[]{:S(2)}) collective-permute-start(bf16[8,2,8,256]{3,2,1,0:T(8,128)(2,1)S(1)} %get-tuple-element.28.across_ref), channel_id=1, source_target_pairs={{0,15},{1,2},{2,1},{3,4},{4,3},{5,6},{6,5},{7,8},{8,7},{9,10},{10,... | collective-permute-start | bytes 196616 | tf_op jit(solution)/shard_map/ppermute | solution.py:327
  20.7 2.3 %collective-permute-start.2 = (bf16[8,2,8,256]{3,2,1,0:T(8,128)(2,1)S(1)}, bf16[8,2,8,256]{3,2,1,0:T(8,128)(2,1)S(1)}, u32[]{:S(2)}, u32[]{:S(2)}) collective-permute-start(bf16[8,2,8,256]{3,2,1,0:T(8,128)(2,1)S(1)} %get-tuple-element.22.in_pair_ref), channel_id=1, source_target_pairs={{14,15},{15,14},{30,31},{31,30},{46,47},{47,46},{62,63},{63,62},{7... | collective-permute-start | bytes 196616 | tf_op jit(solution)/shard_map/ppermute | solution.py:330
  21.4 0.7 copy-start.2
  21.4 0.7 copy-start.3
  21.4 0.7 copy-start.4

commit v8 on v7

--- a/solution.py
+++ b/solution.py
@@ -228,7 +228,10 @@
     scaled = (exact * weights).astype(BF16)
     across = exact.T.astype(BF16)
     ridge = (members - 1) / inflation
-    sums = jnp.sum(jnp.abs(dot_t(scaled, picked)), axis=0, keepdims=True)
+    half = members // 2
+    sums = jnp.sum(jnp.abs(dot_t(scaled[:half], picked)), axis=0, keepdims=True) + jnp.sum(
+        jnp.abs(dot_t(scaled[half:], picked)), axis=0, keepdims=True
+    )
     norm_total = jnp.max(sums, axis=1, keepdims=True) + ridge
     over = 1.0 / norm_total
     gram = dot(across, spread)
@@ -268,12 +271,11 @@
     z_a = z_a * (1.5 - 0.5 * w_a)
 
     scale = jnp.sqrt((members - 1) * over)
-    line = jnp.broadcast_to(weights * innovation, (16, obs))
-    line = dot3(dot3(line, z_small), z_small) * over
-    mixed = dot3(jnp.concatenate([z_c * (scale * over), line], axis=0), gram)
+    line = dot3(jnp.broadcast_to(weights * innovation, (16, obs)), z_small) * over
+    mixed = dot3(jnp.concatenate([z_c * (scale * over), z_small], axis=0), gram)
     high, low = split(mixed[:obs])
+    base = average + dot3(line, mixed[obs:])[0:1]
     rest = dot(jnp.concatenate([scaled, scaled], axis=1), jnp.concatenate([low, high], axis=0))
-    base = average + mixed[obs : obs + 1]
     out_ref[...] = (base + ((scale * z_a) * spread.astype(F32) + rest)).astype(BF16)
 
 

time: 85.9 us -> 85.8 us (level)
  no operation moved by 1% of the time
where the time goes in v8:
time: 85.8 us; the launch traced here: 85.5 us
  blocking collectives  56.9 us (66%)
  starting transfers between devices  18.6 us (22%)
  Pallas kernels  8.18 us (10%)
  local copies, waits for them, and re-layouts  1.71 us (2%)
    all_to_all x1, blocking collectives, body(): lax.all_to_all(outgoing, MEM, split_axis=0, concat_axis=0, tiled=True)  30.8 us
    all_to_all x1, blocking collectives, body(): lax.all_to_all(results, MEM, split_axis=0, concat_axis=0, tiled=True)  26 us
    ppermute x1, starting transfers between devices, advected(): lax.ppermute(ready, 'dom', [(i, (i + 1 if i % 2 else i - 1) % count) for...  14 us
    ppermute x1, starting transfers between devices, advected(): got_pair = lax.ppermute(in_pair, 'dom', swaps[:-2])  3.95 us
    pallas_call x1, Pallas kernels, analyse(): call(analysis_kernel, out, [VMEM] * 4, 10 ** 9, 2 * 10 ** 6)  3.51 us
  transfers between devices with their start and end apart: 3, of which 0 were waited for; matrix products, arithmetic and copies ran while one was open for 0% of the time, Pallas kernels for 3%

profile of v8, /device:TPU:1, one launch (start us, length us, event | category | flops | bytes accessed | tf_op | source)
XLA Modules:
  0.0 85.5 jit_solution(9893386997241724780)
XLA Ops:
  0.0 0.0 copy-start
  0.0 1.0 %copy-done = bf16[8,8,16,256]{3,2,1,0:T(8,128)(2,1)S(1)} copy-done((bf16[8,8,16,256]{3,2,1,0:T(8,128)(2,1)S(1)}, bf16[8,8,16,256]{3,2,1,0:T(8,128)(2,1)}, u32[]{:S(2)}) %copy-start) | copy-done | bytes 524312
  1.0 0.0 copy-start.1
  1.0 0.2 shard_map.64
  1.2 3.9 %collective-permute-start = (bf16[8,2,8,256]{3,2,1,0:T(8,128)(2,1)S(1)}, bf16[8,2,8,256]{3,2,1,0:T(8,128)(2,1)S(1)}, u32[]{:S(2)}, u32[]{:S(2)}) collective-permute-start(bf16[8,2,8,256]{3,2,1,0:T(8,128)(2,1)S(1)} %get-tuple-element.22.in_pair_ref), channel_id=1, source_target_pairs={{0,1},{1,0},{2,3},{3,2},{4,5},{5,4},{6,7},{7,6},{8,9},{9,8},{10,11... | collective-permute-start | bytes 196616 | tf_op jit(solution)/shard_map/ppermute | solution.py:321
  5.2 0.0 copy-done.1
  5.2 0.0 copy-start.5
  5.2 1.5 %shard_map.65 = (bf16[64,8,512]{2,1,0:T(8,128)(2,1)S(1)}, f32[8,4,8,256]{3,2,1,0:T(8,128)S(1)}) custom-call(f32[2,8,256]{2,1,0:T(8,128)S(1)} %copy-done.1, bf16[8,8,16,256]{3,2,1,0:T(8,128)(2,1)S(1)} %get-tuple-element.18.x_ref), custom_call_target="tpu_custom_call" | custom-call | flops 10000000 | bytes 2000000 | tf_op jit(solution)/shard_map/pallas_call | solution.py:325
  6.7 14.0 %collective-permute-start.1 = (bf16[8,2,8,256]{3,2,1,0:T(8,128)(2,1)S(1)}, bf16[8,2,8,256]{3,2,1,0:T(8,128)(2,1)S(1)}, u32[]{:S(2)}, u32[]{:S(2)}) collective-permute-start(bf16[8,2,8,256]{3,2,1,0:T(8,128)(2,1)S(1)} %get-tuple-element.28.across_ref), channel_id=1, source_target_pairs={{0,15},{1,2},{2,1},{3,4},{4,3},{5,6},{6,5},{7,8},{8,7},{9,10},{10,... | collective-permute-start | bytes 196616 | tf_op jit(solution)/shard_map/ppermute | solution.py:329
  20.7 0.7 collective-permute-start.2
  21.4 0.0 collective-permute-done.got_pair_ref
  21.4 0.0 copy-start.2
  21.4 0.0 copy-start.3
  21.4 0.0 copy-start.4
  21.4 0.0 copy-done.5
  21.4 0.6 copy-done.2
  22.1 0.0 copy-done.3
  22.1 0.0 copy-done.4
  22.1 0.9 %shard_map.66 = (bf16[64,8,512]{2,1,0:T(8,128)(2,1)S(1)}, f32[8,4,8,256]{3,2,1,0:T(8,128)S(1)}, bf16[512,128]{1,0:T(8,128)(2,1)S(1)}, f32[1,128]{1,0:T(1,128)S(1)}, f32[1,128]{1,0:T(1,128)S(1)}) custom-call(s32[1,64]{1,0:T(1,128)S(1)} %copy-done.2, f32[2,8,256]{2,1,0:T(8,128)S(1)} %copy-done.1, bf16[8,8,16,256]{3,2,1,0:T(8,128)(2,1)S(1)} %get-tuple-element.18.x_ref, ...), custom_call_target="tpu_custom_call" | custom-call | flops 10000000 | bytes 2000000 | tf_op jit(solution)/shard_map/pallas_call | solution.py:333
  23.0 0.0 collective-permute-done.1.got_across_ref
  23.0 0.0 collective-permute-done.2.got_last_ref
  23.0 0.6 shard_map.67
  23.6 30.8 %all_to_all.10 = bf16[64,8,512]{2,1,0:T(8,128)(2,1)S(1)} all-to-all(bf16[64,8,512]{2,1,0:T(8,128)(2,1)S(1)} %shard_map.67), channel_id=1, replica_groups=mesh['mem_0'=8,'mem_1'=4,'mem_2'=2,'dom'=16] {'mem_0','mem_1','mem_2'}, dimensions={0} | all-to-all | bytes 1048576 | tf_op jit(solution)/shard_map/all_to_all | solution.py:359
  54.5 3.5 %shard_map.68 = bf16[512,512]{1,0:T(8,128)(2,1)S(1)} custom-call(bf16[512,128]{1,0:T(8,128)(2,1)S(1)} %get-tuple-element.25.chosen_ref, f32[1,128]{1,0:T(1,128)S(1)} %get-tuple-element.26.weights_ref, f32[1,128]{1,0:T(1,128)S(1)} %get-tuple-element.27.values_ref, bf16[512,512]{1,0:T(8,128)(2,1)S(1)} %bitcast.5), custom_call_target="tpu_custom_call" | custom-call | flops 1000000000 | bytes 2000000 | tf_op jit(solution)/shard_map/pallas_call | solution.py:368
  58.0 26.0 %all_to_all.11.x_ref = bf16[64,8,512]{2,1,0:T(8,128)(2,1)S(1)} all-to-all(bf16[64,8,512]{2,1,0:T(8,128)(2,1)S(1)} %bitcast.6), channel_id=1, replica_groups=mesh['mem_0'=8,'mem_1'=4,'mem_2'=2,'dom'=16] {'mem_0','mem_1','mem_2'}, dimensions={0} | all-to-all | bytes 1048576 | tf_op jit(solution)/shard_map/all_to_all | solution.py:362
  84.0 1.5 %shard_map.69 = bf16[8,8,16,256]{3,2,1,0:T(8,128)(2,1)} custom-call(s32[1,64]{1,0:T(1,128)S(1)} %copy-done.2, bf16[64,8,512]{2,1,0:T(8,128)(2,1)S(1)} %all_to_all.11.x_ref), custom_call_target="tpu_custom_call" | custom-call | flops 1000000 | bytes 1000000 | tf_op jit(solution)/shard_map/pallas_call | solution.py:372
Async XLA Ops:
  0.0 1.0 %copy-start = (bf16[8,8,16,256]{3,2,1,0:T(8,128)(2,1)S(1)}, bf16[8,8,16,256]{3,2,1,0:T(8,128)(2,1)}, u32[]{:S(2)}) copy-start(bf16[8,8,16,256]{3,2,1,0:T(8,128)(2,1)} %x_ref.1) | copy-start | bytes 1572868
  1.0 4.1 %copy-start.1 = (f32[2,8,256]{2,1,0:T(8,128)S(1)}, f32[2,8,256]{2,1,0:T(8,128)}, u32[]{:S(2)}) copy-start(f32[2,8,256]{2,1,0:T(8,128)} %velocity_ref.5) | copy-start | bytes 49156
  1.2 20.2 %collective-permute-start = (bf16[8,2,8,256]{3,2,1,0:T(8,128)(2,1)S(1)}, bf16[8,2,8,256]{3,2,1,0:T(8,128)(2,1)S(1)}, u32[]{:S(2)}, u32[]{:S(2)}) collective-permute-start(bf16[8,2,8,256]{3,2,1,0:T(8,128)(2,1)S(1)} %get-tuple-element.22.in_pair_ref), channel_id=1, source_target_pairs={{0,1},{1,0},{2,3},{3,2},{4,5},{5,4},{6,7},{7,6},{8,9},{9,8},{10,11... | collective-permute-start | bytes 196616 | tf_op jit(solution)/shard_map/ppermute | solution.py:321
  5.2 16.3 %copy-start.5 = (f32[1,1,128]{2,1,0:T(1,128)S(1)}, f32[1,1,128]{2,1,0:T(1,128)}, u32[]{:S(2)}) copy-start(f32[1,1,128]{2,1,0:T(1,128)} %param.10) | copy-start | bytes 1540
  6.7 16.3 %collective-permute-start.1 = (bf16[8,2,8,256]{3,2,1,0:T(8,128)(2,1)S(1)}, bf16[8,2,8,256]{3,2,1,0:T(8,128)(2,1)S(1)}, u32[]{:S(2)}, u32[]{:S(2)}) collective-permute-start(bf16[8,2,8,256]{3,2,1,0:T(8,128)(2,1)S(1)} %get-tuple-element.28.across_ref), channel_id=1, source_target_pairs={{0,15},{1,2},{2,1},{3,4},{4,3},{5,6},{6,5},{7,8},{8,7},{9,10},{10,... | collective-permute-start | bytes 196616 | tf_op jit(solution)/shard_map/ppermute | solution.py:329
  20.7 2.3 %collective-permute-start.2 = (bf16[8,2,8,256]{3,2,1,0:T(8,128)(2,1)S(1)}, bf16[8,2,8,256]{3,2,1,0:T(8,128)(2,1)S(1)}, u32[]{:S(2)}, u32[]{:S(2)}) collective-permute-start(bf16[8,2,8,256]{3,2,1,0:T(8,128)(2,1)S(1)} %get-tuple-element.22.in_pair_ref), channel_id=1, source_target_pairs={{14,15},{15,14},{30,31},{31,30},{46,47},{47,46},{62,63},{63,62},{7... | collective-permute-start | bytes 196616 | tf_op jit(solution)/shard_map/ppermute | solution.py:332
  21.4 0.7 copy-start.2
  21.4 0.7 copy-start.3
  21.4 0.7 copy-start.4

commit v9 on v8

--- a/solution.py
+++ b/solution.py
@@ -48,7 +48,6 @@
 
 
 def edges_kernel(x_ref, out_ref, in_pair_ref, across_ref):
-    out_ref[...] = x_ref[...]
     levels, rows = x_ref.shape[1], x_ref.shape[2]
     even = lax.rem(lax.axis_index("dom"), 2) == 0
 
@@ -314,7 +313,12 @@
     shape = jax.ShapeDtypeStruct
     edge = shape((levels, 2, members, width), BF16)
     sample, in_pair, across = call(
-        edges_kernel, (shape(prior_sample.shape, BF16), edge, edge), [VMEM], 10**5, 10**6
+        edges_kernel,
+        (shape(prior_sample.shape, BF16), edge, edge),
+        [VMEM],
+        10**5,
+        10**6,
+        input_output_aliases={0: 0},
     )(prior_sample)
     count = lax.axis_size("dom")
     swaps = [(i, i ^ 1) for i in range(count)]

time: 85.8 us -> 85.8 us (level)
  no operation moved by 1% of the time
where the time goes in v9:
time: 85.8 us; the launch traced here: 85.4 us
  blocking collectives  56.8 us (66%)
  starting transfers between devices  18.6 us (22%)
  Pallas kernels  8.14 us (9%)
  local copies, waits for them, and re-layouts  1.71 us (2%)
    all_to_all x1, blocking collectives, body(): lax.all_to_all(outgoing, MEM, split_axis=0, concat_axis=0, tiled=True)  30.8 us
    all_to_all x1, blocking collectives, body(): lax.all_to_all(results, MEM, split_axis=0, concat_axis=0, tiled=True)  26 us
    ppermute x1, starting transfers between devices, advected(): lax.ppermute(ready, 'dom', [(i, (i + 1 if i % 2 else i - 1) % count) for...  14 us
    ppermute x1, starting transfers between devices, advected(): got_pair = lax.ppermute(in_pair, 'dom', swaps[:-2])  3.94 us
    pallas_call x1, Pallas kernels, analyse(): call(analysis_kernel, out, [VMEM] * 4, 10 ** 9, 2 * 10 ** 6)  3.52 us
  transfers between devices with their start and end apart: 3, of which 0 were waited for; matrix products, arithmetic and copies ran while one was open for 0% of the time, Pallas kernels for 3%

profile of v9, /device:TPU:1, one launch (start us, length us, event | category | flops | bytes accessed | tf_op | source)
XLA Modules:
  0.0 85.4 jit_solution(1691658934839516067)
XLA Ops:
  0.0 1.0 %copy.12.x_ref = bf16[8,8,16,256]{3,2,1,0:T(8,128)(2,1)S(1)} copy(bf16[8,8,16,256]{3,2,1,0:T(8,128)(2,1)} %param.6) | data formatting | bytes 1048576
  1.0 0.0 copy-start
  1.0 0.1 shard_map.64
  1.2 3.9 %collective-permute-start = (bf16[8,2,8,256]{3,2,1,0:T(8,128)(2,1)S(1)}, bf16[8,2,8,256]{3,2,1,0:T(8,128)(2,1)S(1)}, u32[]{:S(2)}, u32[]{:S(2)}) collective-permute-start(bf16[8,2,8,256]{3,2,1,0:T(8,128)(2,1)S(1)} %get-tuple-element.22.in_pair_ref), channel_id=1, source_target_pairs={{0,1},{1,0},{2,3},{3,2},{4,5},{5,4},{6,7},{7,6},{8,9},{9,8},{10,11... | collective-permute-start | bytes 196616 | tf_op jit(solution)/shard_map/ppermute | solution.py:325
  5.1 0.0 copy-done
  5.1 0.0 copy-start.4
  5.1 1.5 %shard_map.65 = (bf16[64,8,512]{2,1,0:T(8,128)(2,1)S(1)}, f32[8,4,8,256]{3,2,1,0:T(8,128)S(1)}) custom-call(f32[2,8,256]{2,1,0:T(8,128)S(1)} %copy-done, bf16[8,8,16,256]{3,2,1,0:T(8,128)(2,1)S(1)} %get-tuple-element.18.x_ref), custom_call_target="tpu_custom_call" | custom-call | flops 10000000 | bytes 2000000 | tf_op jit(solution)/shard_map/pallas_call | solution.py:329
  6.7 14.0 %collective-permute-start.1 = (bf16[8,2,8,256]{3,2,1,0:T(8,128)(2,1)S(1)}, bf16[8,2,8,256]{3,2,1,0:T(8,128)(2,1)S(1)}, u32[]{:S(2)}, u32[]{:S(2)}) collective-permute-start(bf16[8,2,8,256]{3,2,1,0:T(8,128)(2,1)S(1)} %get-tuple-element.28.across_ref), channel_id=1, source_target_pairs={{0,15},{1,2},{2,1},{3,4},{4,3},{5,6},{6,5},{7,8},{8,7},{9,10},{10,... | collective-permute-start | bytes 196616 | tf_op jit(solution)/shard_map/ppermute | solution.py:333
  20.7 0.7 collective-permute-start.2
  21.4 0.0 collective-permute-done.got_pair_ref
  21.4 0.0 copy-start.1
  21.4 0.0 copy-start.2
  21.4 0.0 copy-start.3
  21.4 0.0 copy-done.4
  21.4 0.6 copy-done.1
  22.0 0.0 copy-done.2
  22.0 0.0 copy-done.3
  22.1 0.9 %shard_map.66 = (bf16[64,8,512]{2,1,0:T(8,128)(2,1)S(1)}, f32[8,4,8,256]{3,2,1,0:T(8,128)S(1)}, bf16[512,128]{1,0:T(8,128)(2,1)S(1)}, f32[1,128]{1,0:T(1,128)S(1)}, f32[1,128]{1,0:T(1,128)S(1)}) custom-call(s32[1,64]{1,0:T(1,128)S(1)} %copy-done.1, f32[2,8,256]{2,1,0:T(8,128)S(1)} %copy-done, bf16[8,8,16,256]{3,2,1,0:T(8,128)(2,1)S(1)} %get-tuple-element.18.x_ref, ...), custom_call_target="tpu_custom_call" | custom-call | flops 10000000 | bytes 2000000 | tf_op jit(solution)/shard_map/pallas_call | solution.py:337
  22.9 0.0 collective-permute-done.1.got_across_ref
  23.0 0.0 collective-permute-done.2.got_last_ref
  23.0 0.6 shard_map.67
  23.6 30.8 %all_to_all.10 = bf16[64,8,512]{2,1,0:T(8,128)(2,1)S(1)} all-to-all(bf16[64,8,512]{2,1,0:T(8,128)(2,1)S(1)} %shard_map.67), channel_id=1, replica_groups=mesh['mem_0'=8,'mem_1'=4,'mem_2'=2,'dom'=16] {'mem_0','mem_1','mem_2'}, dimensions={0} | all-to-all | bytes 1048576 | tf_op jit(solution)/shard_map/all_to_all | solution.py:363
  54.4 3.5 %shard_map.68 = bf16[512,512]{1,0:T(8,128)(2,1)S(1)} custom-call(bf16[512,128]{1,0:T(8,128)(2,1)S(1)} %get-tuple-element.25.chosen_ref, f32[1,128]{1,0:T(1,128)S(1)} %get-tuple-element.26.weights_ref, f32[1,128]{1,0:T(1,128)S(1)} %get-tuple-element.27.values_ref, bf16[512,512]{1,0:T(8,128)(2,1)S(1)} %bitcast.5), custom_call_target="tpu_custom_call" | custom-call | flops 1000000000 | bytes 2000000 | tf_op jit(solution)/shard_map/pallas_call | solution.py:372
  58.0 26.0 %all_to_all.11.x_ref = bf16[64,8,512]{2,1,0:T(8,128)(2,1)S(1)} all-to-all(bf16[64,8,512]{2,1,0:T(8,128)(2,1)S(1)} %bitcast.6), channel_id=1, replica_groups=mesh['mem_0'=8,'mem_1'=4,'mem_2'=2,'dom'=16] {'mem_0','mem_1','mem_2'}, dimensions={0} | all-to-all | bytes 1048576 | tf_op jit(solution)/shard_map/all_to_all | solution.py:366
  84.0 1.5 %shard_map.69 = bf16[8,8,16,256]{3,2,1,0:T(8,128)(2,1)} custom-call(s32[1,64]{1,0:T(1,128)S(1)} %copy-done.1, bf16[64,8,512]{2,1,0:T(8,128)(2,1)S(1)} %all_to_all.11.x_ref), custom_call_target="tpu_custom_call" | custom-call | flops 1000000 | bytes 1000000 | tf_op jit(solution)/shard_map/pallas_call | solution.py:376
Async XLA Ops:
  1.0 4.1 %copy-start = (f32[2,8,256]{2,1,0:T(8,128)S(1)}, f32[2,8,256]{2,1,0:T(8,128)}, u32[]{:S(2)}) copy-start(f32[2,8,256]{2,1,0:T(8,128)} %velocity_ref.5) | copy-start | bytes 49156
  1.2 20.2 %collective-permute-start = (bf16[8,2,8,256]{3,2,1,0:T(8,128)(2,1)S(1)}, bf16[8,2,8,256]{3,2,1,0:T(8,128)(2,1)S(1)}, u32[]{:S(2)}, u32[]{:S(2)}) collective-permute-start(bf16[8,2,8,256]{3,2,1,0:T(8,128)(2,1)S(1)} %get-tuple-element.22.in_pair_ref), channel_id=1, source_target_pairs={{0,1},{1,0},{2,3},{3,2},{4,5},{5,4},{6,7},{7,6},{8,9},{9,8},{10,11... | collective-permute-start | bytes 196616 | tf_op jit(solution)/shard_map/ppermute | solution.py:325
  5.1 16.3 %copy-start.4 = (f32[1,1,128]{2,1,0:T(1,128)S(1)}, f32[1,1,128]{2,1,0:T(1,128)}, u32[]{:S(2)}) copy-start(f32[1,1,128]{2,1,0:T(1,128)} %param.10) | copy-start | bytes 1540
  6.7 16.3 %collective-permute-start.1 = (bf16[8,2,8,256]{3,2,1,0:T(8,128)(2,1)S(1)}, bf16[8,2,8,256]{3,2,1,0:T(8,128)(2,1)S(1)}, u32[]{:S(2)}, u32[]{:S(2)}) collective-permute-start(bf16[8,2,8,256]{3,2,1,0:T(8,128)(2,1)S(1)} %get-tuple-element.28.across_ref), channel_id=1, source_target_pairs={{0,15},{1,2},{2,1},{3,4},{4,3},{5,6},{6,5},{7,8},{8,7},{9,10},{10,... | collective-permute-start | bytes 196616 | tf_op jit(solution)/shard_map/ppermute | solution.py:333
  20.7 2.3 %collective-permute-start.2 = (bf16[8,2,8,256]{3,2,1,0:T(8,128)(2,1)S(1)}, bf16[8,2,8,256]{3,2,1,0:T(8,128)(2,1)S(1)}, u32[]{:S(2)}, u32[]{:S(2)}) collective-permute-start(bf16[8,2,8,256]{3,2,1,0:T(8,128)(2,1)S(1)} %get-tuple-element.22.in_pair_ref), channel_id=1, source_target_pairs={{14,15},{15,14},{30,31},{31,30},{46,47},{47,46},{62,63},{63,62},{7... | collective-permute-start | bytes 196616 | tf_op jit(solution)/shard_map/ppermute | solution.py:336
  21.4 0.7 copy-start.1
  21.4 0.7 copy-start.2
  21.4 0.7 copy-start.3

commit v10 on v8

--- a/solution.py
+++ b/solution.py
@@ -8,6 +8,7 @@
 
 STEPS = 5
 MEM = ("mem_0", "mem_1", "mem_2")
+SENT = ("mem_1", "mem_2", "mem_0")
 
 advect_coef = 0.15
 diffuse_coef = 0.15
@@ -91,6 +92,12 @@
     lax.fori_loop(0, levels, one, 0, unroll=2)
 
 
+def place_of(owner_ref, tile):
+    slots, first = owner_ref.shape[1], lax.axis_size("mem_0")
+    slot = owner_ref[0, tile]
+    return lax.rem(slot, slots // first) * first + lax.div(slot, slots // first)
+
+
 def is_last():
     return lax.axis_index("dom") == lax.axis_size("dom") - 1
 
@@ -129,7 +136,7 @@
     if before_slots is not None:
         before_slots()
     for level in range(levels):
-        put(out_ref, owner_ref[0, level * pairs + place], done[level], width)
+        put(out_ref, place_of(owner_ref, level * pairs + place), done[level], width)
 
 
 def between_kernel(
@@ -142,13 +149,13 @@
 
     @pl.when(is_last())
     def _():
-        interior(lambda t: owner_ref[0, t], velocity_ref, x_ref, out_ref, first_ref)
+        interior(lambda t: place_of(owner_ref, t), velocity_ref, x_ref, out_ref, first_ref)
 
     @pl.when(jnp.logical_not(is_last()))
     def _():
         for level in range(levels):
             for p in range(1, pairs - 1):
-                out_ref[owner_ref[0, level * pairs + p]] = partial_ref[level * pairs + p]
+                out_ref[place_of(owner_ref, level * pairs + p)] = partial_ref[level * pairs + p]
         first_ref[...] = kept_ref[...]
 
     @pl.when(jnp.logical_not(in_last_pair()))
@@ -287,7 +294,7 @@
         return pltpu.make_async_copy(held_ref.at[:, level], out_ref.at[:, level], sent.at[level])
 
     for level in range(levels):
-        tiles = [x_ref[owner_ref[0, level * pairs + p]].astype(F32) for p in range(pairs)]
+        tiles = [x_ref[place_of(owner_ref, level * pairs + p)].astype(F32) for p in range(pairs)]
         field = jnp.stack([t[:, k * width : (k + 1) * width] for t in tiles for k in range(2)])
         held_ref[:, level] = jnp.swapaxes(field, 0, 1).astype(BF16)
         copy(level).start()
@@ -356,10 +363,10 @@
     )
     slots, members, tile = outgoing.shape
     total = slots * members
-    received = lax.all_to_all(outgoing, MEM, split_axis=0, concat_axis=0, tiled=True)
+    received = lax.all_to_all(outgoing, SENT, split_axis=0, concat_axis=0, tiled=True)
     updated = analyse(chosen, weights, values, received.reshape(total, tile))
     results = updated.reshape(slots, members, tile)
-    returned = lax.all_to_all(results, MEM, split_axis=0, concat_axis=0, tiled=True)
+    returned = lax.all_to_all(results, SENT, split_axis=0, concat_axis=0, tiled=True)
     return restored(tile_owner, returned, prior_sample.shape)
 
 

time: 85.8 us -> 84 us (0.979)
  blocking collectives: 56.9 us -> 54.8 us
    all_to_all x2, blocking collectives: 56.9 us -> 54.8 us  [the longest x1 29.5 us: body(): lax.all_to_all(outgoing, SENT, split_axis=0, concat_axis=0, tiled=True)]
where the time goes in v10:
time: 84 us; the launch traced here: 83.7 us
  blocking collectives  54.8 us (65%)
  starting transfers between devices  18.6 us (22%)
  Pallas kernels  8.35 us (10%)
  local copies, waits for them, and re-layouts  1.71 us (2%)
    all_to_all x1, blocking collectives, body(): lax.all_to_all(outgoing, SENT, split_axis=0, concat_axis=0, tiled=True)  29.5 us
    all_to_all x1, blocking collectives, body(): lax.all_to_all(results, SENT, split_axis=0, concat_axis=0, tiled=True)  25.4 us
    ppermute x1, starting transfers between devices, advected(): lax.ppermute(ready, 'dom', [(i, (i + 1 if i % 2 else i - 1) % count) for...  14 us
    ppermute x1, starting transfers between devices, advected(): got_pair = lax.ppermute(in_pair, 'dom', swaps[:-2])  3.95 us
    pallas_call x1, Pallas kernels, analyse(): call(analysis_kernel, out, [VMEM] * 4, 10 ** 9, 2 * 10 ** 6)  3.51 us
    unnamed x12, local copies, waits for them, and re-layouts  1.71 us
  transfers between devices with their start and end apart: 3, of which 0 were waited for; matrix products, arithmetic and copies ran while one was open for 0% of the time, Pallas kernels for 3%

profile of v10, /device:TPU:1, one launch (start us, length us, event | category | flops | bytes accessed | tf_op | source)
XLA Modules:
  0.0 83.7 jit_solution(2068920885097095979)
XLA Ops:
  0.0 0.0 copy-start
  0.0 1.0 %copy-done = bf16[8,8,16,256]{3,2,1,0:T(8,128)(2,1)S(1)} copy-done((bf16[8,8,16,256]{3,2,1,0:T(8,128)(2,1)S(1)}, bf16[8,8,16,256]{3,2,1,0:T(8,128)(2,1)}, u32[]{:S(2)}) %copy-start) | copy-done | bytes 524312
  1.0 0.0 copy-start.1
  1.0 0.2 shard_map.64
  1.2 3.9 %collective-permute-start = (bf16[8,2,8,256]{3,2,1,0:T(8,128)(2,1)S(1)}, bf16[8,2,8,256]{3,2,1,0:T(8,128)(2,1)S(1)}, u32[]{:S(2)}, u32[]{:S(2)}) collective-permute-start(bf16[8,2,8,256]{3,2,1,0:T(8,128)(2,1)S(1)} %get-tuple-element.22.in_pair_ref), channel_id=1, source_target_pairs={{0,1},{1,0},{2,3},{3,2},{4,5},{5,4},{6,7},{7,6},{8,9},{9,8},{10,11... | collective-permute-start | bytes 196616 | tf_op jit(solution)/shard_map/ppermute | solution.py:328
  5.2 0.0 copy-done.1
  5.2 0.0 copy-start.5
  5.2 1.5 %shard_map.65 = (bf16[64,8,512]{2,1,0:T(8,128)(2,1)S(1)}, f32[8,4,8,256]{3,2,1,0:T(8,128)S(1)}) custom-call(f32[2,8,256]{2,1,0:T(8,128)S(1)} %copy-done.1, bf16[8,8,16,256]{3,2,1,0:T(8,128)(2,1)S(1)} %get-tuple-element.18.x_ref), custom_call_target="tpu_custom_call" | custom-call | flops 10000000 | bytes 2000000 | tf_op jit(solution)/shard_map/pallas_call | solution.py:332
  6.7 14.0 %collective-permute-start.1 = (bf16[8,2,8,256]{3,2,1,0:T(8,128)(2,1)S(1)}, bf16[8,2,8,256]{3,2,1,0:T(8,128)(2,1)S(1)}, u32[]{:S(2)}, u32[]{:S(2)}) collective-permute-start(bf16[8,2,8,256]{3,2,1,0:T(8,128)(2,1)S(1)} %get-tuple-element.28.across_ref), channel_id=1, source_target_pairs={{0,15},{1,2},{2,1},{3,4},{4,3},{5,6},{6,5},{7,8},{8,7},{9,10},{10,... | collective-permute-start | bytes 196616 | tf_op jit(solution)/shard_map/ppermute | solution.py:336
  20.7 0.7 collective-permute-start.2
  21.4 0.0 collective-permute-done.got_pair_ref
  21.4 0.0 copy-start.2
  21.4 0.0 copy-start.3
  21.4 0.0 copy-start.4
  21.4 0.0 copy-done.5
  21.4 0.6 copy-done.2
  22.1 0.0 copy-done.3
  22.1 0.0 copy-done.4
  22.1 1.0 %shard_map.66 = (bf16[64,8,512]{2,1,0:T(8,128)(2,1)S(1)}, f32[8,4,8,256]{3,2,1,0:T(8,128)S(1)}, bf16[512,128]{1,0:T(8,128)(2,1)S(1)}, f32[1,128]{1,0:T(1,128)S(1)}, f32[1,128]{1,0:T(1,128)S(1)}) custom-call(s32[1,64]{1,0:T(1,128)S(1)} %copy-done.2, f32[2,8,256]{2,1,0:T(8,128)S(1)} %copy-done.1, bf16[8,8,16,256]{3,2,1,0:T(8,128)(2,1)S(1)} %get-tuple-element.18.x_ref, ...), custom_call_target="tpu_custom_call" | custom-call | flops 10000000 | bytes 2000000 | tf_op jit(solution)/shard_map/pallas_call | solution.py:340
  23.1 0.0 collective-permute-done.1.got_across_ref
  23.1 0.0 collective-permute-done.2.got_last_ref
  23.1 0.6 shard_map.67
  23.8 29.5 %all_to_all.10 = bf16[64,8,512]{2,1,0:T(8,128)(2,1)S(1)} all-to-all(bf16[64,8,512]{2,1,0:T(8,128)(2,1)S(1)} %shard_map.67), channel_id=1, replica_groups=mesh['mem_0'=8,'mem_1'=4,'mem_2'=2,'dom'=16] {'mem_1','mem_2','mem_0'}, dimensions={0} | all-to-all | bytes 1048576 | tf_op jit(solution)/shard_map/all_to_all | solution.py:366
  53.3 3.5 %shard_map.68 = bf16[512,512]{1,0:T(8,128)(2,1)S(1)} custom-call(bf16[512,128]{1,0:T(8,128)(2,1)S(1)} %get-tuple-element.25.chosen_ref, f32[1,128]{1,0:T(1,128)S(1)} %get-tuple-element.26.weights_ref, f32[1,128]{1,0:T(1,128)S(1)} %get-tuple-element.27.values_ref, bf16[512,512]{1,0:T(8,128)(2,1)S(1)} %bitcast.5), custom_call_target="tpu_custom_call" | custom-call | flops 1000000000 | bytes 2000000 | tf_op jit(solution)/shard_map/pallas_call | solution.py:375
  56.8 25.4 %all_to_all.11.x_ref = bf16[64,8,512]{2,1,0:T(8,128)(2,1)S(1)} all-to-all(bf16[64,8,512]{2,1,0:T(8,128)(2,1)S(1)} %bitcast.6), channel_id=1, replica_groups=mesh['mem_0'=8,'mem_1'=4,'mem_2'=2,'dom'=16] {'mem_1','mem_2','mem_0'}, dimensions={0} | all-to-all | bytes 1048576 | tf_op jit(solution)/shard_map/all_to_all | solution.py:369
  82.2 1.5 %shard_map.69 = bf16[8,8,16,256]{3,2,1,0:T(8,128)(2,1)} custom-call(s32[1,64]{1,0:T(1,128)S(1)} %copy-done.2, bf16[64,8,512]{2,1,0:T(8,128)(2,1)S(1)} %all_to_all.11.x_ref), custom_call_target="tpu_custom_call" | custom-call | flops 1000000 | bytes 1000000 | tf_op jit(solution)/shard_map/pallas_call | solution.py:379
Async XLA Ops:
  0.0 1.0 %copy-start = (bf16[8,8,16,256]{3,2,1,0:T(8,128)(2,1)S(1)}, bf16[8,8,16,256]{3,2,1,0:T(8,128)(2,1)}, u32[]{:S(2)}) copy-start(bf16[8,8,16,256]{3,2,1,0:T(8,128)(2,1)} %x_ref.1) | copy-start | bytes 1572868
  1.0 4.1 %copy-start.1 = (f32[2,8,256]{2,1,0:T(8,128)S(1)}, f32[2,8,256]{2,1,0:T(8,128)}, u32[]{:S(2)}) copy-start(f32[2,8,256]{2,1,0:T(8,128)} %velocity_ref.5) | copy-start | bytes 49156
  1.2 20.2 %collective-permute-start = (bf16[8,2,8,256]{3,2,1,0:T(8,128)(2,1)S(1)}, bf16[8,2,8,256]{3,2,1,0:T(8,128)(2,1)S(1)}, u32[]{:S(2)}, u32[]{:S(2)}) collective-permute-start(bf16[8,2,8,256]{3,2,1,0:T(8,128)(2,1)S(1)} %get-tuple-element.22.in_pair_ref), channel_id=1, source_target_pairs={{0,1},{1,0},{2,3},{3,2},{4,5},{5,4},{6,7},{7,6},{8,9},{9,8},{10,11... | collective-permute-start | bytes 196616 | tf_op jit(solution)/shard_map/ppermute | solution.py:328
  5.2 16.3 %copy-start.5 = (f32[1,1,128]{2,1,0:T(1,128)S(1)}, f32[1,1,128]{2,1,0:T(1,128)}, u32[]{:S(2)}) copy-start(f32[1,1,128]{2,1,0:T(1,128)} %param.10) | copy-start | bytes 1540
  6.7 16.4 %collective-permute-start.1 = (bf16[8,2,8,256]{3,2,1,0:T(8,128)(2,1)S(1)}, bf16[8,2,8,256]{3,2,1,0:T(8,128)(2,1)S(1)}, u32[]{:S(2)}, u32[]{:S(2)}) collective-permute-start(bf16[8,2,8,256]{3,2,1,0:T(8,128)(2,1)S(1)} %get-tuple-element.28.across_ref), channel_id=1, source_target_pairs={{0,15},{1,2},{2,1},{3,4},{4,3},{5,6},{6,5},{7,8},{8,7},{9,10},{10,... | collective-permute-start | bytes 196616 | tf_op jit(solution)/shard_map/ppermute | solution.py:336
  20.7 2.4 %collective-permute-start.2 = (bf16[8,2,8,256]{3,2,1,0:T(8,128)(2,1)S(1)}, bf16[8,2,8,256]{3,2,1,0:T(8,128)(2,1)S(1)}, u32[]{:S(2)}, u32[]{:S(2)}) collective-permute-start(bf16[8,2,8,256]{3,2,1,0:T(8,128)(2,1)S(1)} %get-tuple-element.22.in_pair_ref), channel_id=1, source_target_pairs={{14,15},{15,14},{30,31},{31,30},{46,47},{47,46},{62,63},{63,62},{7... | collective-permute-start | bytes 196616 | tf_op jit(solution)/shard_map/ppermute | solution.py:339
  21.4 0.7 copy-start.2
  21.4 0.7 copy-start.3
  21.4 0.7 copy-start.4
